TPU v7x, 32 devices: a whole 2x2x4 slice. The times are simulated.
32 devices in a mesh: dp: 8 (over z, core), seq: 4 (over y, x).
Axes of the slice: x: 2, y: 2, z: 4, core: 2. Of those that a mesh axis runs over, the one named last changes fastest.
Arguments:
- inputs: bfloat16 [8, 2048, 1024], P('dp', 'seq'), may hold values from -6 to 6
- segments: int32 [8, 2048], P('dp'), may hold values from 0 to 34, as said below
- cotangent: bfloat16 [8, 2048, 1024], P('dp', 'seq'), may hold values from -6 to 6
- norm_gain_mix: float32 [1024], replicated, may hold values from 0.5 to 1.5
- w_query: float32 [1024, 1024], P('dp'), may hold values from -0.1875 to 0.1875
- w_key: float32 [1024, 1024], P('dp'), may hold values from -0.1875 to 0.1875
- w_value: float32 [1024, 2048], P('dp'), may hold values from -0.1875 to 0.1875
- w_outgate: float32 [1024, 2048], P('dp'), may hold values from -0.1875 to 0.1875
- w_gates: float32 [1024, 16], P('dp'), may hold values from -0.1875 to 0.1875
- conv_weight: float32 [4, 4096], replicated, may hold values from -3 to 3
- decay_log: float32 [8], replicated, may hold values from 0 to 2.77
- dt_bias: float32 [8], replicated, may hold values from -6.9 to -2.25
- out_norm_gain: float32 [256], replicated, may hold values from 0.5 to 1.5
- w_out: float32 [2048, 1024], P(None, 'dp'), may hold values from -0.25 to 0.25
- norm_gain_ffn: float32 [1024], replicated, may hold values from 0.5 to 1.5
- w_ffn_gate: float32 [1024, 2816], P('dp'), may hold values from -0.1875 to 0.1875
- w_ffn_up: float32 [1024, 2816], P('dp'), may hold values from -0.1875 to 0.1875
- w_ffn_down: float32 [2816, 1024], P(None, 'dp'), may hold values from -0.21875 to 0.21875
Outputs:
- output: bfloat16 [8, 2048, 1024], P('dp', 'seq')
- grad_inputs: float32 [8, 2048, 1024], P('dp', 'seq')
- grad_norm_gain_mix: float32 [1024], replicated
- grad_w_query: float32 [1024, 1024], P('dp')
- grad_w_key: float32 [1024, 1024], P('dp')
- grad_w_value: float32 [1024, 2048], P('dp')
- grad_w_outgate: float32 [1024, 2048], P('dp')
- grad_w_gates: float32 [1024, 16], P('dp')
- grad_conv_weight: float32 [4, 4096], replicated
- grad_decay_log: float32 [8], replicated
- grad_dt_bias: float32 [8], replicated
- grad_out_norm_gain: float32 [256], replicated
- grad_w_out: float32 [2048, 1024], P(None, 'dp')
- grad_norm_gain_ffn: float32 [1024], replicated
- grad_w_ffn_gate: float32 [1024, 2816], P('dp')
- grad_w_ffn_up: float32 [1024, 2816], P('dp')
- grad_w_ffn_down: float32 [2816, 1024], P(None, 'dp')
Inputs may be any that keep to these rules, and one draw needn't show every extreme that they name: `segments`: per row, segment numbers start at 0, never fall, and rise by one at each document's first token; each row holds exactly 35 documents; one document of each row begins within the first 512 tokens and ends within the last 512.
All inputs are finite; a program needn't handle non-finite values.
Results may differ from a plain program's by a relative error of at most 0.019.
Values may be sent and summed in bfloat16 or wider, within the bound.
A program may use at most 448 MiB of HBM per device.

v0:
```python
import jax
import jax.numpy as jnp
from jax import lax
from jax.sharding import PartitionSpec as P

H = 8
DK = 128
DV = 256
CONV = 4
STRETCH = 64


precise = lax.Precision.HIGHEST


def shifted(block, axis, distance):
    devices = range(lax.axis_size(axis))
    route = [(i - distance, i) for i in devices if i - distance in devices]
    return lax.ppermute(block, axis, route)


def prefix_2(part, axis, combine, identity):
    place = lax.axis_index(axis)
    gathered = jax.tree.map(lambda a: lax.all_gather(a, axis), part)
    state = jax.tree.map(lambda a, e: jnp.zeros_like(a) + jnp.asarray(e, a.dtype), part, identity)

    def prefix_one(lap, state):
        return combine(
            state, jax.tree.map(lambda a: lax.dynamic_index_in_dim(a, lap, 0, False), gathered)
        )

    return lax.fori_loop(0, place, prefix_one, state)


def entering(value, axis, join, neutral):
    count = lax.axis_size(axis)
    place = lax.axis_index(axis)
    ahead = count - 1 - place
    gathered = jax.tree.map(
        lambda a, kind: lax.all_gather(a.astype(kind), axis),
        value,
        jax.tree.map(lambda a: jnp.bfloat16 if a.dtype == jnp.float32 else a.dtype, value),
    )
    state = jax.tree.map(lambda a, e: jnp.zeros_like(a) + jnp.asarray(e, a.dtype), value, neutral)

    def entering_one(lap, state):
        source = count - 1 - lap
        return join(
            state,
            jax.tree.map(
                lambda a, own: lax.dynamic_index_in_dim(a, source, 0, False).astype(own.dtype),
                gathered,
                value,
            ),
        )

    return lax.fori_loop(0, ahead, entering_one, state)


def dense(left, right):
    return jnp.dot(left, right, preferred_element_type=jnp.float32)


def rms_scale(values, weights, epsilon):
    return values * lax.rsqrt(jnp.mean(values * values, axis=-1, keepdims=True) + epsilon) * weights


def unit_rows(values):
    return values * lax.rsqrt(jnp.sum(values * values, axis=-1, keepdims=True) + 1e-06)


def conv_mix(padded, seg_ext, conv_weight):
    length = padded.shape[0] - (CONV - 1)
    current = seg_ext[CONV - 1 :]
    total = jnp.zeros((length, padded.shape[1]), jnp.float32)
    for offset in range(CONV):
        begin = CONV - 1 - offset
        same_doc = (seg_ext[begin : begin + length] == current).astype(jnp.float32)
        total = total + padded[begin : begin + length] * conv_weight[offset] * same_doc[:, None]
    return jax.nn.silu(total)


def prepare(padded, gate_logits, conv_weight, decay_log, dt_bias, seg_ext):
    mixed = conv_mix(padded, seg_ext, conv_weight)
    length = mixed.shape[0]
    query_rows = unit_rows(mixed[:, : H * DK].reshape(length, H, DK)) * DK ** (-0.5)
    key_rows = unit_rows(mixed[:, H * DK : 2 * H * DK].reshape(length, H, DK))
    value_rows = mixed[:, 2 * H * DK :].reshape(length, H, DV)
    strength = jax.nn.sigmoid(gate_logits[:, H:])
    decay = -jnp.exp(decay_log) * jax.nn.softplus(gate_logits[:, :H] + dt_bias)
    return (query_rows, key_rows, value_rows, strength, decay)


def delta_stretch(state, block):
    query_rows, key_rows, value_rows, strength, decay, seg_block, seg_before = block
    length = query_rows.shape[0]
    cumulative = jnp.cumsum(decay, axis=0).T
    row_ids = jnp.arange(length)
    same_doc = seg_block[:, None] == seg_block[None, :]
    causal = (row_ids[:, None] >= row_ids[None, :]) & same_doc
    strict = causal & (row_ids[:, None] > row_ids[None, :])
    spread = jnp.where(causal[None], cumulative[:, :, None] - cumulative[:, None, :], 0.0)
    gamma = jnp.exp(spread) * causal[None]
    carry_scale = jnp.exp(cumulative) * (seg_block == seg_before)[None, :]
    queries = jnp.transpose(query_rows, (1, 0, 2))
    keys_t = jnp.transpose(key_rows, (1, 0, 2))
    values_t = jnp.transpose(value_rows, (1, 0, 2))
    beta_t = strength.T
    key_dots = jnp.einsum("hid,hjd->hij", keys_t, keys_t, precision=precise)
    system = (
        jnp.eye(length, dtype=jnp.float32)[None]
        + beta_t[:, :, None] * gamma * key_dots * strict[None]
    )
    target = beta_t[:, :, None] * (
        values_t
        - carry_scale[:, :, None] * jnp.einsum("hcd,hdw->hcw", keys_t, state, precision=precise)
    )
    updates = jax.scipy.linalg.solve_triangular(system, target, lower=True, unit_diagonal=True)
    scores = jnp.einsum("hid,hjd->hij", queries, keys_t, precision=precise) * gamma
    readout = carry_scale[:, :, None] * jnp.einsum(
        "hcd,hdw->hcw", queries, state, precision=precise
    )
    readout = readout + jnp.einsum("hij,hjw->hiw", scores, updates, precision=precise)
    new_state = carry_scale[:, -1][:, None, None] * state + jnp.einsum(
        "hc,hcd,hcw->hdw", gamma[:, -1, :], keys_t, updates, precision=precise
    )
    return (new_state, jnp.transpose(readout, (1, 0, 2)))


def local_states(query_rows, key_rows, value_rows, strength, decay, seg_dev, seg_prev):
    length = query_rows.shape[0]
    heads_local = query_rows.shape[1]
    count = length // STRETCH

    def blocked(values):
        return values.reshape((count, STRETCH) + values.shape[1:])

    value_aug = jnp.concatenate(
        [value_rows, jnp.zeros((length, heads_local, DK), jnp.float32)], axis=-1
    )
    identity_part = jnp.broadcast_to(jnp.eye(DK, dtype=jnp.float32), (heads_local, DK, DK))
    start_state = jnp.concatenate(
        [jnp.zeros((heads_local, DK, DV), jnp.float32), identity_part], axis=-1
    )
    starts = jnp.concatenate([seg_prev[None], seg_dev[STRETCH - 1 : length - 1 : STRETCH]])
    final, readout = lax.scan(
        delta_stretch,
        start_state,
        (
            blocked(query_rows),
            blocked(key_rows),
            blocked(value_aug),
            blocked(strength),
            blocked(decay),
            blocked(seg_dev),
            starts,
        ),
    )
    readout = readout.reshape((length,) + readout.shape[2:])
    return (readout[..., :DV], readout[..., DV:], final[..., DV:], final[..., :DV])


def gated_norm(attn, gate_pre, out_norm_gain):
    length = attn.shape[0]
    normed = rms_scale(attn, out_norm_gain, 1e-05)
    return (normed * jax.nn.silu(gate_pre.reshape(length, H, DV))).reshape(length, H * DV)


def compose_forward(earlier, later):
    first_map, first_sum = earlier
    second_map, second_sum = later
    return (
        jnp.einsum("hij,hjk->hik", second_map, first_map, precision=precise),
        jnp.einsum("hij,hjw->hiw", second_map, first_sum, precision=precise) + second_sum,
    )


def compose_backward(earlier, later):
    upper_map, upper_sum = earlier
    lower_map, lower_sum = later
    return (
        jnp.einsum("hij,hjk->hik", lower_map, upper_map, precision=precise),
        lower_sum + jnp.einsum("hij,hjw->hiw", lower_map, upper_sum, precision=precise),
    )


def span_segments(seg_pad, start, length):
    seg_ext = lax.dynamic_slice_in_dim(seg_pad, start, length + CONV - 1)
    return (seg_ext[CONV - 1 :], seg_ext[CONV - 2])


def local(
    inputs,
    segments,
    cotangent,
    norm_gain_mix,
    w_query,
    w_key,
    w_value,
    w_outgate,
    w_gates,
    conv_weight,
    decay_log,
    dt_bias,
    out_norm_gain,
    w_out,
    norm_gain_ffn,
    w_ffn_gate,
    w_ffn_up,
    w_ffn_down,
):
    row_in = inputs[0].astype(jnp.float32)
    grad_out = cotangent[0].astype(jnp.float32)
    tokens = row_in.shape[0]
    halo_width = CONV - 1
    my_index = lax.axis_index("seq")
    seg_pad = jnp.concatenate([jnp.full((halo_width,), -1, jnp.int32), segments[0]])
    seg_ext = lax.dynamic_slice_in_dim(seg_pad, my_index * tokens, tokens + halo_width)
    gathered = (
        lax.all_gather(w_query.astype(jnp.bfloat16), "dp", axis=0, tiled=True),
        lax.all_gather(w_key.astype(jnp.bfloat16), "dp", axis=0, tiled=True),
        lax.all_gather(w_value.astype(jnp.bfloat16), "dp", axis=0, tiled=True),
        lax.all_gather(w_outgate.astype(jnp.bfloat16), "dp", axis=0, tiled=True),
        lax.all_gather(w_gates.astype(jnp.bfloat16), "dp", axis=0, tiled=True),
        lax.all_gather(w_out.astype(jnp.bfloat16), "dp", axis=1, tiled=True),
        lax.all_gather(w_ffn_gate.astype(jnp.bfloat16), "dp", axis=0, tiled=True),
        lax.all_gather(w_ffn_up.astype(jnp.bfloat16), "dp", axis=0, tiled=True),
        lax.all_gather(w_ffn_down.astype(jnp.bfloat16), "dp", axis=1, tiled=True),
    )
    query_w, key_w, value_w, outgate_w, gates_w, out_w, ffn_gate_w, ffn_up_w, ffn_down_w = gathered
    normed_in, norm_in_back = jax.vjp(
        lambda values, weights: rms_scale(values, weights, 1e-06), row_in, norm_gain_mix
    )
    hidden_in = normed_in.astype(jnp.bfloat16)
    projected = jnp.concatenate(
        [dense(hidden_in, query_w), dense(hidden_in, key_w), dense(hidden_in, value_w)], axis=1
    ).astype(jnp.bfloat16)
    gate_pre = dense(hidden_in, outgate_w)
    gate_logits = dense(hidden_in, gates_w)
    halo_rows = shifted(projected[tokens - halo_width :], "seq", 1)
    padded = jnp.concatenate([halo_rows, projected], axis=0).astype(jnp.float32)

    def prepare_local(pad_in, logit_in, conv_in, log_in, bias_in):
        return prepare(pad_in, logit_in, conv_in, log_in, bias_in, seg_ext)

    mixer_in, prepare_back = jax.vjp(
        prepare_local, padded, gate_logits, conv_weight, decay_log, dt_bias
    )
    span_start = my_index * tokens
    span_dev, span_prev = span_segments(seg_pad, span_start, tokens)

    def states_local(*parts):
        return local_states(*parts, span_dev, span_prev)

    local_out, local_back = jax.vjp(states_local, *mixer_in)
    partial_out, response, transfer, offset_state = local_out
    heads_local = transfer.shape[0]
    keep_mask = (my_index > 0).astype(jnp.float32)
    eye_maps = jnp.broadcast_to(jnp.eye(DK, dtype=jnp.float32), (heads_local, DK, DK))
    empty_states = jnp.zeros((heads_local, DK, DV), jnp.float32)
    prefix = prefix_2(
        (transfer * keep_mask, offset_state), "seq", compose_forward, (eye_maps, empty_states)
    )
    state_in = prefix[1] * keep_mask
    attn_local = partial_out + jnp.einsum("thj,hjw->thw", response, state_in, precision=precise)
    gated, gated_back = jax.vjp(gated_norm, attn_local, gate_pre, out_norm_gain)
    gated_low = gated.astype(jnp.bfloat16)
    resid = row_in + dense(gated_low, out_w)
    normed_mid, norm_mid_back = jax.vjp(
        lambda values, weights: rms_scale(values, weights, 1e-06), resid, norm_gain_ffn
    )
    hidden_mid = normed_mid.astype(jnp.bfloat16)
    gate_val = dense(hidden_mid, ffn_gate_w)
    up_val = dense(hidden_mid, ffn_up_w)
    sigmoid_gate = jax.nn.sigmoid(gate_val)
    swish = gate_val * sigmoid_gate
    activ = (swish * up_val).astype(jnp.bfloat16)
    result = resid + dense(activ, ffn_down_w)
    d_branch = grad_out.astype(jnp.bfloat16)
    d_activ = dense(d_branch, ffn_down_w.T)
    d_gate = (d_activ * up_val * sigmoid_gate * (1.0 + gate_val * (1.0 - sigmoid_gate))).astype(
        jnp.bfloat16
    )
    d_up = (d_activ * swish).astype(jnp.bfloat16)
    g_ffn_down = dense(activ.T, d_branch)
    g_ffn_gate = dense(hidden_mid.T, d_gate)
    g_ffn_up = dense(hidden_mid.T, d_up)
    d_hidden_mid = dense(d_gate, ffn_gate_w.T) + dense(d_up, ffn_up_w.T)
    d_resid_norm, d_gain_mid = norm_mid_back(d_hidden_mid)
    d_resid = grad_out + d_resid_norm
    d_mixer_out = d_resid.astype(jnp.bfloat16)
    g_out = dense(gated_low.T, d_mixer_out)
    d_gated = dense(d_mixer_out, out_w.T)
    d_attn, d_gate_pre, d_gain_out = gated_back(d_gated)
    local_grad = jnp.einsum("thj,thw->hjw", response, d_attn, precision=precise)
    d_response = jnp.einsum("thw,hjw->thj", d_attn, state_in, precision=precise)
    suffix = entering(
        (jnp.transpose(transfer, (0, 2, 1)) * keep_mask, local_grad * keep_mask),
        "seq",
        compose_backward,
        (eye_maps, empty_states),
    )
    later_grad = suffix[1]
    d_transfer = jnp.einsum("hiw,hjw->hij", later_grad, state_in, precision=precise)
    d_local = local_back((d_attn, d_response, d_transfer, later_grad))
    d_padded, d_logits, d_conv, d_decay_log, d_dt_bias = prepare_back(d_local)
    sent_back = shifted(d_padded[:halo_width].astype(jnp.bfloat16), "seq", -1).astype(jnp.float32)
    d_proj = d_padded[halo_width:] + jnp.pad(sent_back, ((tokens - halo_width, 0), (0, 0)))
    d_proj_low = d_proj.astype(jnp.bfloat16)
    d_gate_low = d_gate_pre.astype(jnp.bfloat16)
    d_logit_low = d_logits.astype(jnp.bfloat16)
    query_part = d_proj_low[:, : H * DK]
    key_part = d_proj_low[:, H * DK : 2 * H * DK]
    value_part = d_proj_low[:, 2 * H * DK :]
    g_query = dense(hidden_in.T, query_part)
    g_key = dense(hidden_in.T, key_part)
    g_value = dense(hidden_in.T, value_part)
    g_outgate = dense(hidden_in.T, d_gate_low)
    g_gates = dense(hidden_in.T, d_logit_low)
    d_hidden_in = (
        dense(query_part, query_w.T) + dense(key_part, key_w.T) + dense(value_part, value_w.T)
    )
    d_hidden_in = d_hidden_in + dense(d_gate_low, outgate_w.T) + dense(d_logit_low, gates_w.T)
    d_in_norm, d_gain_in = norm_in_back(d_hidden_in)
    d_inputs = d_resid + d_in_norm
    full_grads = (
        g_query,
        g_key,
        g_value,
        g_outgate,
        g_gates,
        g_out,
        g_ffn_gate,
        g_ffn_up,
        g_ffn_down,
    )
    partial_shards = (
        lax.psum_scatter(
            full_grads[0].astype(jnp.bfloat16), "dp", scatter_dimension=0, tiled=True
        ).astype(jnp.float32),
        lax.psum_scatter(
            full_grads[1].astype(jnp.bfloat16), "dp", scatter_dimension=0, tiled=True
        ).astype(jnp.float32),
        lax.psum_scatter(
            full_grads[2].astype(jnp.bfloat16), "dp", scatter_dimension=0, tiled=True
        ).astype(jnp.float32),
        lax.psum_scatter(
            full_grads[3].astype(jnp.bfloat16), "dp", scatter_dimension=0, tiled=True
        ).astype(jnp.float32),
        lax.psum_scatter(
            full_grads[4].astype(jnp.bfloat16), "dp", scatter_dimension=0, tiled=True
        ).astype(jnp.float32),
        lax.psum_scatter(
            full_grads[5].astype(jnp.bfloat16), "dp", scatter_dimension=1, tiled=True
        ).astype(jnp.float32),
        lax.psum_scatter(
            full_grads[6].astype(jnp.bfloat16), "dp", scatter_dimension=0, tiled=True
        ).astype(jnp.float32),
        lax.psum_scatter(
            full_grads[7].astype(jnp.bfloat16), "dp", scatter_dimension=0, tiled=True
        ).astype(jnp.float32),
        lax.psum_scatter(
            full_grads[8].astype(jnp.bfloat16), "dp", scatter_dimension=1, tiled=True
        ).astype(jnp.float32),
    )
    shards = (
        lax.psum(partial_shards[0].astype(jnp.bfloat16), "seq").astype(jnp.float32),
        lax.psum(partial_shards[1].astype(jnp.bfloat16), "seq").astype(jnp.float32),
        lax.psum(partial_shards[2].astype(jnp.bfloat16), "seq").astype(jnp.float32),
        lax.psum(partial_shards[3].astype(jnp.bfloat16), "seq").astype(jnp.float32),
        lax.psum(partial_shards[4].astype(jnp.bfloat16), "seq").astype(jnp.float32),
        lax.psum(partial_shards[5].astype(jnp.bfloat16), "seq").astype(jnp.float32),
        lax.psum(partial_shards[6].astype(jnp.bfloat16), "seq").astype(jnp.float32),
        lax.psum(partial_shards[7].astype(jnp.bfloat16), "seq").astype(jnp.float32),
        lax.psum(partial_shards[8].astype(jnp.bfloat16), "seq").astype(jnp.float32),
    )
    small = lax.psum(
        (d_gain_in, d_conv, d_decay_log, d_dt_bias, d_gain_out, d_gain_mid), ("dp", "seq")
    )
    return (
        result.astype(jnp.bfloat16)[None],
        d_inputs[None],
        small[0],
        shards[0],
        shards[1],
        shards[2],
        shards[3],
        shards[4],
        small[1],
        small[2],
        small[3],
        small[4],
        shards[5],
        small[5],
        shards[6],
        shards[7],
        shards[8],
    )


def solution(mesh):
    in_specs = (
        P("dp", "seq", None),
        P("dp", None),
        P("dp", "seq", None),
        P(),
        P("dp", None),
        P("dp", None),
        P("dp", None),
        P("dp", None),
        P("dp", None),
        P(),
        P(),
        P(),
        P(),
        P(None, "dp"),
        P(),
        P("dp", None),
        P("dp", None),
        P(None, "dp"),
    )
    out_specs = (
        P("dp", "seq", None),
        P("dp", "seq", None),
        P(),
        P("dp", None),
        P("dp", None),
        P("dp", None),
        P("dp", None),
        P("dp", None),
        P(),
        P(),
        P(),
        P(),
        P(None, "dp"),
        P(),
        P("dp", None),
        P("dp", None),
        P(None, "dp"),
    )
    return jax.shard_map(local, mesh=mesh, in_specs=in_specs, out_specs=out_specs, check_vma=False)
```

profile of v0, /device:TPU:8, one launch (start us, length us, event | category | flops | bytes accessed | tf_op | source)
XLA Modules:
  0.0 2582.9 jit_solution(16211878357115041261)
XLA Ops:
  14.4 13.0 all_gather.51
  28.0 12.6 all-gather.17.cloned.1.call-done
  43.5 27.9 %all-gather.19.cloned.1.call-done = bf16[1024,1024]{1,0:T(8,128)(2,1)} async-done(((bf16[128,1024]{1,0:T(8,128)(2,1)}), bf16[1024,1024]{1,0:T(8,128)(2,1)}) %all-gather.19.cloned.1.call-update) | async-done | bytes 2097168 | tf_op jit(solution)/shard_map/all_gather | solution.py:221
  74.7 44.1 %all-gather.21.cloned.1.call-done = bf16[1024,2048]{1,0:T(8,128)(2,1)} async-done(((bf16[128,2048]{1,0:T(8,128)(2,1)}), bf16[1024,2048]{1,0:T(8,128)(2,1)}) %all-gather.21.cloned.1.call-update) | async-done | bytes 4194320 | tf_op jit(solution)/shard_map/all_gather | solution.py:222
  138.8 21.0 fusion.173
  185.7 593.2 %while.121 = (s32[]{:T(128)}, f32[8,128,384]{2,1,0:T(8,128)S(1)}, f32[8,64,8,384]{3,1,0,2:T(8,128)}, pred[8,8,64,64]{3,2,1,0:T(32,128)(4,1)}, f32[8,8,64,64]{3,2...) while((s32[]{:T(128)}, f32[8,128,384]{2,1,0:T(8,128)S(1)}, ...), condition=%wide.region_5.6_spmd.clone.clone, body=%wide.region_3.5_spmd.clone.clone.sunk | while | flops 1311847296 | bytes 29483256 | solution.py:146
  197.8 39.9 %custom-call.52 = f32[8,1,64,64]{2,3,1,0:T(8,128)} custom-call(f32[8,1,64,64]{3,2,1,0:T(8,128)S(1)} %get-tuple-element.2681), custom_call_target="InvertDiagBlocksLowerTriangular" | custom-call | tf_op jit(solution)/shard_map/jvp()/while/body/eval_jaxpr/jit(_solve_triangular)/vmap()/triangular_solve | solution.py:118
  271.9 39.9 %custom-call.52 = f32[8,1,64,64]{2,3,1,0:T(8,128)} custom-call(f32[8,1,64,64]{3,2,1,0:T(8,128)S(1)} %get-tuple-element.2681), custom_call_target="InvertDiagBlocksLowerTriangular" | custom-call | tf_op jit(solution)/shard_map/jvp()/while/body/eval_jaxpr/jit(_solve_triangular)/vmap()/triangular_solve | solution.py:118
  346.0 39.9 %custom-call.52 = f32[8,1,64,64]{2,3,1,0:T(8,128)} custom-call(f32[8,1,64,64]{3,2,1,0:T(8,128)S(1)} %get-tuple-element.2681), custom_call_target="InvertDiagBlocksLowerTriangular" | custom-call | tf_op jit(solution)/shard_map/jvp()/while/body/eval_jaxpr/jit(_solve_triangular)/vmap()/triangular_solve | solution.py:118
  420.1 39.9 %custom-call.52 = f32[8,1,64,64]{2,3,1,0:T(8,128)} custom-call(f32[8,1,64,64]{3,2,1,0:T(8,128)S(1)} %get-tuple-element.2681), custom_call_target="InvertDiagBlocksLowerTriangular" | custom-call | tf_op jit(solution)/shard_map/jvp()/while/body/eval_jaxpr/jit(_solve_triangular)/vmap()/triangular_solve | solution.py:118
  494.3 39.9 %custom-call.52 = f32[8,1,64,64]{2,3,1,0:T(8,128)} custom-call(f32[8,1,64,64]{3,2,1,0:T(8,128)S(1)} %get-tuple-element.2681), custom_call_target="InvertDiagBlocksLowerTriangular" | custom-call | tf_op jit(solution)/shard_map/jvp()/while/body/eval_jaxpr/jit(_solve_triangular)/vmap()/triangular_solve | solution.py:118
  568.5 39.9 %custom-call.52 = f32[8,1,64,64]{2,3,1,0:T(8,128)} custom-call(f32[8,1,64,64]{3,2,1,0:T(8,128)S(1)} %get-tuple-element.2681), custom_call_target="InvertDiagBlocksLowerTriangular" | custom-call | tf_op jit(solution)/shard_map/jvp()/while/body/eval_jaxpr/jit(_solve_triangular)/vmap()/triangular_solve | solution.py:118
  642.7 39.9 %custom-call.52 = f32[8,1,64,64]{2,3,1,0:T(8,128)} custom-call(f32[8,1,64,64]{3,2,1,0:T(8,128)S(1)} %get-tuple-element.2681), custom_call_target="InvertDiagBlocksLowerTriangular" | custom-call | tf_op jit(solution)/shard_map/jvp()/while/body/eval_jaxpr/jit(_solve_triangular)/vmap()/triangular_solve | solution.py:118
  716.7 39.9 %custom-call.52 = f32[8,1,64,64]{2,3,1,0:T(8,128)} custom-call(f32[8,1,64,64]{3,2,1,0:T(8,128)S(1)} %get-tuple-element.2681), custom_call_target="InvertDiagBlocksLowerTriangular" | custom-call | tf_op jit(solution)/shard_map/jvp()/while/body/eval_jaxpr/jit(_solve_triangular)/vmap()/triangular_solve | solution.py:118
  785.9 6.5 copy.260
  793.3 21.3 all-gather.33.cloned.1.call-done
  814.6 55.0 %all-gather.35.cloned.1.call-done = f32[32,128,256]{2,1,0:T(8,128)} async-done(((f32[8,128,256]{2,1,0:T(8,128)}), f32[32,128,256]{2,1,0:T(8,128)}) %all-gather.35.cloned.1.call-update) | async-done | bytes 4194320 | tf_op jit(solution)/shard_map/all_gather | solution.py:24
  870.0 7.1 multiply_reduce_fusion.6
  884.5 33.9 %all-gather.25.cloned.1.call-done = bf16[2048,1024]{1,0:T(8,128)(2,1)} async-done(((bf16[2048,128]{1,0:T(8,128)(2,1)}), bf16[2048,1024]{1,0:T(8,128)(2,1)}) %all-gather.25.cloned.1.call-update) | async-done | bytes 4194320 | tf_op jit(solution)/shard_map/all_gather | solution.py:225
  918.4 5.5 multiply_reduce_fusion.11
  925.3 53.2 %all-gather.27.cloned.1.call-done = bf16[1024,2816]{1,0:T(8,128)(2,1)} async-done(((bf16[128,2816]{1,0:T(8,128)(2,1)}), bf16[1024,2816]{1,0:T(8,128)(2,1)}) %all-gather.27.cloned.1.call-update) | async-done | bytes 5767184 | tf_op jit(solution)/shard_map/all_gather | solution.py:226
  978.5 8.6 fusion.267
  987.2 52.7 %all-gather.29.cloned.1.call-done = bf16[1024,2816]{1,0:T(8,128)(2,1)} async-done(((bf16[128,2816]{1,0:T(8,128)(2,1)}), bf16[1024,2816]{1,0:T(8,128)(2,1)}) %all-gather.29.cloned.1.call-update) | async-done | bytes 5767184 | tf_op jit(solution)/shard_map/all_gather | solution.py:227
  1039.9 8.6 fusion.268
  1048.5 52.0 %all-gather.31.cloned.1.call-done = bf16[2816,1024]{1,0:T(8,128)(2,1)} async-done(((bf16[2816,128]{1,0:T(8,128)(2,1)}), bf16[2816,1024]{1,0:T(8,128)(2,1)}) %all-gather.31.cloned.1.call-update) | async-done | bytes 5767184 | tf_op jit(solution)/shard_map/all_gather | solution.py:228
  1100.5 11.2 multiply_convert_fusion
  1111.7 8.0 fusion.269
  1130.5 5.4 copy.265
  1135.9 7.9 multiply_reduce_fusion.4
  1148.9 6.1 fusion.206
  1155.1 6.0 convolution_convert_fusion.3
  1161.1 6.5 copy.311
  1169.2 6.9 convolution_convert_fusion
  1176.1 8.4 copy.313
  1184.5 5.7 convolution_bitcast_fusion.4
  1193.5 5.8 while.119
  1207.4 709.4 %while.120 = (s32[]{:T(128)}, f32[8,128,384]{2,1,0:T(8,128)S(1)}, f32[8,64,8,128]{3,2,1,0:T(8,128)}, f32[8,64,8,128]{3,2,1,0:T(8,128)}, f32[8,64,8,384]{3,2,1,0:...) while((s32[]{:T(128)}, f32[8,128,384]{2,1,0:T(8,128)S(1)}, ...), condition=%wide.region_23.24_spmd.clone, body=%wide.region_14.23_spmd.clone.sunk | while | flops 2649174016 | bytes 44770684 | solution.py:146
  1215.3 39.3 %custom-call.51 = f32[8,1,64,64]{2,3,1,0:T(8,128)S(1)} custom-call(f32[8,1,64,64]{3,2,1,0:T(8,128)S(1)} %add_bitcast_fusion.3), custom_call_target="InvertDiagBlocksLowerTriangular" | custom-call | tf_op jit(solution)/shard_map/transpose(jvp())/while/body/eval_jaxpr/jit(_solve_triangular)/vmap()/triangular_solve | solution.py:118
  1304.1 39.3 %custom-call.51 = f32[8,1,64,64]{2,3,1,0:T(8,128)S(1)} custom-call(f32[8,1,64,64]{3,2,1,0:T(8,128)S(1)} %add_bitcast_fusion.3), custom_call_target="InvertDiagBlocksLowerTriangular" | custom-call | tf_op jit(solution)/shard_map/transpose(jvp())/while/body/eval_jaxpr/jit(_solve_triangular)/vmap()/triangular_solve | solution.py:118
  1392.7 39.3 %custom-call.51 = f32[8,1,64,64]{2,3,1,0:T(8,128)S(1)} custom-call(f32[8,1,64,64]{3,2,1,0:T(8,128)S(1)} %add_bitcast_fusion.3), custom_call_target="InvertDiagBlocksLowerTriangular" | custom-call | tf_op jit(solution)/shard_map/transpose(jvp())/while/body/eval_jaxpr/jit(_solve_triangular)/vmap()/triangular_solve | solution.py:118
  1481.3 39.3 %custom-call.51 = f32[8,1,64,64]{2,3,1,0:T(8,128)S(1)} custom-call(f32[8,1,64,64]{3,2,1,0:T(8,128)S(1)} %add_bitcast_fusion.3), custom_call_target="InvertDiagBlocksLowerTriangular" | custom-call | tf_op jit(solution)/shard_map/transpose(jvp())/while/body/eval_jaxpr/jit(_solve_triangular)/vmap()/triangular_solve | solution.py:118
  1569.9 39.3 %custom-call.51 = f32[8,1,64,64]{2,3,1,0:T(8,128)S(1)} custom-call(f32[8,1,64,64]{3,2,1,0:T(8,128)S(1)} %add_bitcast_fusion.3), custom_call_target="InvertDiagBlocksLowerTriangular" | custom-call | tf_op jit(solution)/shard_map/transpose(jvp())/while/body/eval_jaxpr/jit(_solve_triangular)/vmap()/triangular_solve | solution.py:118
  1658.4 39.3 %custom-call.51 = f32[8,1,64,64]{2,3,1,0:T(8,128)S(1)} custom-call(f32[8,1,64,64]{3,2,1,0:T(8,128)S(1)} %add_bitcast_fusion.3), custom_call_target="InvertDiagBlocksLowerTriangular" | custom-call | tf_op jit(solution)/shard_map/transpose(jvp())/while/body/eval_jaxpr/jit(_solve_triangular)/vmap()/triangular_solve | solution.py:118
  1747.0 39.3 %custom-call.51 = f32[8,1,64,64]{2,3,1,0:T(8,128)S(1)} custom-call(f32[8,1,64,64]{3,2,1,0:T(8,128)S(1)} %add_bitcast_fusion.3), custom_call_target="InvertDiagBlocksLowerTriangular" | custom-call | tf_op jit(solution)/shard_map/transpose(jvp())/while/body/eval_jaxpr/jit(_solve_triangular)/vmap()/triangular_solve | solution.py:118
  1835.6 39.3 %custom-call.51 = f32[8,1,64,64]{2,3,1,0:T(8,128)S(1)} custom-call(f32[8,1,64,64]{3,2,1,0:T(8,128)S(1)} %add_bitcast_fusion.3), custom_call_target="InvertDiagBlocksLowerTriangular" | custom-call | tf_op jit(solution)/shard_map/transpose(jvp())/while/body/eval_jaxpr/jit(_solve_triangular)/vmap()/triangular_solve | solution.py:118
  1937.4 10.7 add_add_fusion.4
  1948.2 12.4 multiply_reduce_fusion.3
  1960.7 15.2 multiply_multiply_fusion.2
  1975.9 12.7 pad_add_fusion
  2008.4 6.3 convolution_convert_fusion.4
  2015.9 6.8 convolution_convert_fusion.1
  2022.8 6.9 convolution_convert_fusion.2
  2029.8 6.1 convolution_convert_fusion.5
  2042.9 25.9 %reduce-scatter.18.cloned.1.call-done = bf16[128,1024]{1,0:T(8,128)(2,1)} async-done(((bf16[1024,1024]{1,0:T(8,128)(2,1)}), bf16[128,1024]{1,0:T(8,128)(2,1)}) %reduce-scatter.18.cloned.1.call-update) | async-done | bytes 262160 | tf_op jit(solution)/shard_map/reduce_scatter | solution.py:341
  2068.8 50.8 %reduce-scatter.22.cloned.1.call-done = bf16[128,2048]{1,0:T(8,128)(2,1)} async-done(((bf16[1024,2048]{1,0:T(8,128)(2,1)}), bf16[128,2048]{1,0:T(8,128)(2,1)}) %reduce-scatter.22.cloned.1.call-update) | async-done | bytes 524304 | tf_op jit(solution)/shard_map/reduce_scatter | solution.py:347
  2119.6 66.2 %reduce-scatter.26.cloned.1.call-done = bf16[128,2816]{1,0:T(8,128)(2,1)} async-done(((bf16[1024,2816]{1,0:T(8,128)(2,1)}), bf16[128,2816]{1,0:T(8,128)(2,1)}) %reduce-scatter.26.cloned.1.call-update) | async-done | bytes 720912 | tf_op jit(solution)/shard_map/reduce_scatter | solution.py:359
  2185.8 65.5 %reduce-scatter.24.cloned.1.call-done = bf16[128,2816]{1,0:T(8,128)(2,1)} async-done(((bf16[1024,2816]{1,0:T(8,128)(2,1)}), bf16[128,2816]{1,0:T(8,128)(2,1)}) %reduce-scatter.24.cloned.1.call-update) | async-done | bytes 720912 | tf_op jit(solution)/shard_map/reduce_scatter | solution.py:356
  2251.3 49.6 %reduce-scatter.20.cloned.1.call-done = bf16[128,2048]{1,0:T(8,128)(2,1)} async-done(((bf16[1024,2048]{1,0:T(8,128)(2,1)}), bf16[128,2048]{1,0:T(8,128)(2,1)}) %reduce-scatter.20.cloned.1.call-update) | async-done | bytes 524304 | tf_op jit(solution)/shard_map/reduce_scatter | solution.py:344
  2301.2 6.7 fusion.270
  2307.9 6.8 fusion.205
  2327.8 43.4 %all-reduce.23 = (f32[1024]{0:T(1024)}, f32[8]{0:T(128)}, f32[8]{0:T(128)}, f32[256]{0:T(256)}, f32[1024]{0:T(1024)}) all-reduce(f32[1024]{0:T(1024)S(1)} %get-tuple-element.1896, f32[8]{0:T(128)S(1)} %negate_multiply_fusion, f32[8]{0:T(128)S(1)} %get-tuple-element.2066, ...), channel_id=1, replica_groups=mesh['dp'=8,'seq'=4] {'dp','seq'}, use_global_device_ids=true, to_apply=%region_28.29 | all-reduce | flops 2320 | bytes 18560 | tf_op jit(solution)/shard_map/psum | solution.py:377
  2371.9 10.4 psum.110
  2382.9 66.0 %all-reduce.30.cloned.1.call-done = (bf16[128,1024]{1,0:T(8,128)(2,1)}, bf16[128,1024]{1,0:T(8,128)(2,1)}, bf16[128,2048]{1,0:T(8,128)(2,1)}, bf16[128,2048]{1,0...) async-done(((bf16[128,1024]{1,0:T(8,128)(2,1)}, bf16[128,1024]{1,0:T(8,128)(2,1)}, ...) | async-done | bytes 4259856 | tf_op jit(solution)/shard_map/psum | solution.py:367
  2458.6 116.2 %all-reduce.28.cloned.1.call-done = f32[4,4096]{1,0:T(4,128)} async-done(((f32[4,4096]{1,0:T(4,128)}), f32[4,4096]{1,0:T(4,128)}) %all-reduce.28.cloned.1.call-update) | async-done | bytes 65552 | tf_op jit(solution)/shard_map/psum | solution.py:377
  (1197 shorter events, 850.3 us)
Async XLA Ops:
  7.2 33.4 %all-gather.17.cloned.1.call-start = ((), (), s32[]{:S(2)}) async-start(), calls=%async_computation.9 | async-start | bytes 2359296 | tf_op jit(solution)/shard_map/all_gather | solution.py:220
  9.2 62.3 %all-gather.19.cloned.1.call-start = ((), (), s32[]{:S(2)}) async-start(), calls=%async_computation.10 | async-start | bytes 2359296 | tf_op jit(solution)/shard_map/all_gather | solution.py:221
  11.1 107.7 %all-gather.21.cloned.1.call-start = ((), (), s32[]{:S(2)}) async-start(), calls=%async_computation.11 | async-start | bytes 4718592 | tf_op jit(solution)/shard_map/all_gather | solution.py:222
  12.0 15.4 copy-start.105
  12.0 15.5 copy-start.91
  12.0 773.8 %all-gather.23.cloned.1.call-start = ((), (), s32[]{:S(2)}) async-start(), calls=%async_computation.12 | async-start | bytes 4718592 | tf_op jit(solution)/shard_map/all_gather | solution.py:223
  13.0 15.0 copy-start.97
  13.0 801.6 %all-gather.33.cloned.1.call-start = ((), (), s32[]{:S(2)}) async-start(), calls=%async_computation.24 | async-start | bytes 2621440 | tf_op jit(solution)/shard_map/all_gather | solution.py:24
  13.2 125.6 %copy-start.75 = (f32[512]{0:T(512)}, f32[512]{0:T(512)S(1)}, u32[]{:S(2)}) copy-start(f32[512]{0:T(512)S(1)} %get-tuple-element.2138) | copy-start | bytes 6148
  13.2 125.6 %copy-start.77 = (f32[512]{0:T(512)}, f32[512]{0:T(512)S(1)}, u32[]{:S(2)}) copy-start(f32[512]{0:T(512)S(1)} %get-tuple-element.2139) | copy-start | bytes 6148
  13.2 125.6 %copy-start.79 = (f32[512]{0:T(512)}, f32[512]{0:T(512)S(1)}, u32[]{:S(2)}) copy-start(f32[512]{0:T(512)S(1)} %get-tuple-element.2140) | copy-start | bytes 6148
  14.2 13.3 copy-start.83
  14.2 104.6 %copy-start.86 = (f32[512]{0:T(512)}, f32[512]{0:T(512)S(1)}, u32[]{:S(2)}) copy-start(f32[512]{0:T(512)S(1)} %fusion.249) | copy-start | bytes 6148
  14.3 124.5 %copy-start.54 = (f32[1,4096]{1,0:T(1,128)}, f32[1,4096]{1,0:T(1,128)S(1)}, u32[]{:S(2)}) copy-start(f32[1,4096]{1,0:T(1,128)S(1)} %get-tuple-element.2128) | copy-start | bytes 49156
  14.3 124.5 %copy-start.56 = (f32[1,4096]{1,0:T(1,128)}, f32[1,4096]{1,0:T(1,128)S(1)}, u32[]{:S(2)}) copy-start(f32[1,4096]{1,0:T(1,128)S(1)} %get-tuple-element.2129) | copy-start | bytes 49156
  14.3 124.5 %copy-start.58 = (f32[1,4096]{1,0:T(1,128)}, f32[1,4096]{1,0:T(1,128)S(1)}, u32[]{:S(2)}) copy-start(f32[1,4096]{1,0:T(1,128)S(1)} %get-tuple-element.2130) | copy-start | bytes 49156
  14.3 124.5 %copy-start.60 = (f32[1,4096]{1,0:T(1,128)}, f32[1,4096]{1,0:T(1,128)S(1)}, u32[]{:S(2)}) copy-start(f32[1,4096]{1,0:T(1,128)S(1)} %get-tuple-element.2131) | copy-start | bytes 49156
  27.4 16.1 copy-start.68
  27.5 16.1 copy-start.99
  27.9 15.6 copy-start.70
  74.7 49.0 %copy-start.28 = (bf16[512,1024]{1,0:T(8,128)(2,1)}, bf16[512,1024]{1,0:T(8,128)(2,1)S(1)}, u32[]{:S(2)}) copy-start(bf16[512,1024]{1,0:T(8,128)(2,1)S(1)} %convolution_convert_fusion.9) | copy-start | bytes 3145732
  125.1 7.0 collective-permute-start
  196.8 41.0 %copy-start.23 = (f32[64,64]{1,0:T(8,128)}, f32[64,64]{1,0:T(8,128)S(1)}, u32[]{:S(2)}) copy-start(f32[64,64]{1,0:T(8,128)S(1)} %convert_bitcast_fusion.4) | copy-start | bytes 49156 | tf_op jit(solution)/shard_map/jvp()/while
  270.9 41.0 %copy-start.23 = (f32[64,64]{1,0:T(8,128)}, f32[64,64]{1,0:T(8,128)S(1)}, u32[]{:S(2)}) copy-start(f32[64,64]{1,0:T(8,128)S(1)} %convert_bitcast_fusion.4) | copy-start | bytes 49156 | tf_op jit(solution)/shard_map/jvp()/while
  345.0 41.0 %copy-start.23 = (f32[64,64]{1,0:T(8,128)}, f32[64,64]{1,0:T(8,128)S(1)}, u32[]{:S(2)}) copy-start(f32[64,64]{1,0:T(8,128)S(1)} %convert_bitcast_fusion.4) | copy-start | bytes 49156 | tf_op jit(solution)/shard_map/jvp()/while
  419.1 41.0 %copy-start.23 = (f32[64,64]{1,0:T(8,128)}, f32[64,64]{1,0:T(8,128)S(1)}, u32[]{:S(2)}) copy-start(f32[64,64]{1,0:T(8,128)S(1)} %convert_bitcast_fusion.4) | copy-start | bytes 49156 | tf_op jit(solution)/shard_map/jvp()/while
  493.3 41.0 %copy-start.23 = (f32[64,64]{1,0:T(8,128)}, f32[64,64]{1,0:T(8,128)S(1)}, u32[]{:S(2)}) copy-start(f32[64,64]{1,0:T(8,128)S(1)} %convert_bitcast_fusion.4) | copy-start | bytes 49156 | tf_op jit(solution)/shard_map/jvp()/while
  567.5 41.0 %copy-start.23 = (f32[64,64]{1,0:T(8,128)}, f32[64,64]{1,0:T(8,128)S(1)}, u32[]{:S(2)}) copy-start(f32[64,64]{1,0:T(8,128)S(1)} %convert_bitcast_fusion.4) | copy-start | bytes 49156 | tf_op jit(solution)/shard_map/jvp()/while
  641.7 41.0 %copy-start.23 = (f32[64,64]{1,0:T(8,128)}, f32[64,64]{1,0:T(8,128)S(1)}, u32[]{:S(2)}) copy-start(f32[64,64]{1,0:T(8,128)S(1)} %convert_bitcast_fusion.4) | copy-start | bytes 49156 | tf_op jit(solution)/shard_map/jvp()/while
  715.7 41.0 %copy-start.23 = (f32[64,64]{1,0:T(8,128)}, f32[64,64]{1,0:T(8,128)S(1)}, u32[]{:S(2)}) copy-start(f32[64,64]{1,0:T(8,128)S(1)} %convert_bitcast_fusion.4) | copy-start | bytes 49156 | tf_op jit(solution)/shard_map/jvp()/while
  779.8 89.8 %all-gather.35.cloned.1.call-start = ((), (), s32[]{:S(2)}) async-start(), calls=%async_computation.25 | async-start | bytes 5242880 | tf_op jit(solution)/shard_map/all_gather | solution.py:24
  780.9 137.4 %all-gather.25.cloned.1.call-start = ((), (), s32[]{:S(2)}) async-start(), calls=%async_computation.13 | async-start | bytes 4718592 | tf_op jit(solution)/shard_map/all_gather | solution.py:225
  782.2 196.3 %all-gather.27.cloned.1.call-start = ((), (), s32[]{:S(2)}) async-start(), calls=%async_computation.14 | async-start | bytes 6488064 | tf_op jit(solution)/shard_map/all_gather | solution.py:226
  783.3 256.6 %all-gather.29.cloned.1.call-start = ((), (), s32[]{:S(2)}) async-start(), calls=%async_computation.15 | async-start | bytes 6488064 | tf_op jit(solution)/shard_map/all_gather | solution.py:227
  784.8 315.7 %all-gather.31.cloned.1.call-start = ((), (), s32[]{:S(2)}) async-start(), calls=%async_computation.16 | async-start | bytes 6488064 | tf_op jit(solution)/shard_map/all_gather | solution.py:228
  785.8 407.6 %all-gather.39.cloned.1.call-start = ((), (), s32[]{:S(2)}) async-start(), calls=%async_computation.27 | async-start | bytes 1310720 | tf_op jit(solution)/shard_map/all_gather | solution.py:40
  793.2 400.2 %all-gather.37.cloned.1.call-start = ((), (), s32[]{:S(2)}) async-start(), calls=%async_computation.26 | async-start | bytes 2621440 | tf_op jit(solution)/shard_map/all_gather | solution.py:40
  923.9 199.9 %copy-start.17 = (f32[512,1024]{1,0:T(8,128)}, f32[512,1024]{1,0:T(8,128)S(1)}, u32[]{:S(2)}) copy-start(f32[512,1024]{1,0:T(8,128)S(1)} %get-tuple-element.2146) | copy-start | bytes 6291460
  1135.9 9.1 copy-start.14
  1155.0 883.6 %reduce-scatter.30.cloned.1.call-start = ((), (), s32[]{:S(2)}) async-start(), calls=%async_computation.29 | async-start | bytes 4718592
  1167.7 873.0 %reduce-scatter.32.cloned.1.call-start = ((), (), s32[]{:S(2)}) async-start(), calls=%async_computation.30 | async-start | bytes 6488064
  1193.3 849.6 %reduce-scatter.16.cloned.1.call-start = ((), (), s32[]{:S(2)}) async-start(), calls=%async_computation.17 | async-start | bytes 2359296 | tf_op jit(solution)/shard_map/reduce_scatter | solution.py:338
  1937.4 10.7 slice-start
  1937.4 10.7 slice-start.1
  1937.4 10.7 slice-start.2
  1937.4 10.7 copy-start.76
  1937.4 10.7 copy-start.78
  1937.4 10.7 copy-start.80
  1948.1 12.5 copy-start.55
  1948.2 12.5 copy-start.57
  1948.2 12.5 copy-start.59
  1948.2 12.5 copy-start.61
  1988.6 9.0 copy-start.31
  1988.7 9.0 copy-start.88
  1988.7 9.0 copy-start.93
  1988.7 5.9 collective-permute-start.1
  2000.4 68.4 %reduce-scatter.18.cloned.1.call-start = ((), (), s32[]{:S(2)}) async-start(), calls=%async_computation.18 | async-start | bytes 2359296 | tf_op jit(solution)/shard_map/reduce_scatter | solution.py:341
  2004.5 115.2 %reduce-scatter.22.cloned.1.call-start = ((), (), s32[]{:S(2)}) async-start(), calls=%async_computation.20 | async-start | bytes 4718592 | tf_op jit(solution)/shard_map/reduce_scatter | solution.py:347
  2014.7 171.1 %reduce-scatter.26.cloned.1.call-start = ((), (), s32[]{:S(2)}) async-start(), calls=%async_computation.23 | async-start | bytes 6488064 | tf_op jit(solution)/shard_map/reduce_scatter | solution.py:359
  2022.8 228.6 %reduce-scatter.24.cloned.1.call-start = ((), (), s32[]{:S(2)}) async-start(), calls=%async_computation.22 | async-start | bytes 6488064 | tf_op jit(solution)/shard_map/reduce_scatter | solution.py:356
  2029.7 271.2 %reduce-scatter.20.cloned.1.call-start = ((), (), s32[]{:S(2)}) async-start(), calls=%async_computation.19 | async-start | bytes 4718592 | tf_op jit(solution)/shard_map/reduce_scatter | solution.py:344
  2035.9 335.2 %reduce-scatter.28.cloned.1.call-start = ((), (), s32[]{:S(2)}) async-start(), calls=%async_computation.28 | async-start | bytes 294912
  2038.6 410.3 %all-reduce.30.cloned.1.call-start = ((), (), s32[]{:S(2)}) async-start(), calls=%async_computation.31 | async-start | bytes 8519680 | tf_op jit(solution)/shard_map/psum | solution.py:367
  2300.9 273.8 %all-reduce.28.cloned.1.call-start = ((), (), s32[]{:S(2)}) async-start(), calls=%async_computation.21 | async-start | bytes 131072 | tf_op jit(solution)/shard_map/psum | solution.py:377
  (145 other events, 618.5 us)
Sparse Core Ops, SparseCore 0:
  10.2 30.3 all-gather.16
  42.8 28.6 all-gather.18
  73.6 45.1 all-gather.20
  120.8 45.8 all-gather.22
  779.9 34.6 all-gather.32
  816.9 52.6 all-gather.34
  871.8 46.5 all-gather.24
  920.6 57.9 all-gather.26
  980.7 59.0 all-gather.28
  1041.9 58.5 all-gather.30
  1102.9 27.7 all-gather.38
  1155.2 36.4 all-gather.36
  1193.9 46.1 reduce-scatter.29
  1242.3 64.1 reduce-scatter.31
  2000.5 31.8 reduce-scatter.15
  2034.6 34.1 reduce-scatter.17
  2070.9 48.6 reduce-scatter.21
  2121.8 63.9 reduce-scatter.25
  2188.1 63.1 reduce-scatter.23
  2253.5 47.3 reduce-scatter.19
  2303.7 28.7 reduce-scatter.27
  2338.9 109.9 all-reduce.29
  2455.9 118.7 all-reduce.27
where the time goes:
time: 2600 us; the launch traced here: 2580 us
  other arithmetic  858 us (33%)
  waiting for transfers between devices  798 us (31%)
  matrix products  586 us (23%)
  local copies, waits for them, and re-layouts  249 us (10%)
  blocking collectives  66.7 us (3%)
    another operation x72, other arithmetic, delta_stretch(): jax.scipy.linalg.solve_triangular(system, target, lower=True, unit_diagon...  643 us
    dot_general x27, matrix products, dense(): return jnp.dot(left, right, preferred_element_type=jnp.float32)  135 us
    psum x1, waiting for transfers between devices, local(): lax.psum((d_gain_in, d_conv, d_decay_log, d_dt_bias, d_gain_out, d_gain_m...  116 us
    dot_general x24, matrix products, delta_stretch(): jnp.einsum('hcd,hdw->hcw', keys_t, state, precision=precise)  84.4 us
    all_gather x2, waiting for transfers between devices, prefix_2(): gathered = jax.tree.map(lambda a: lax.all_gather(a, axis), part)  76.3 us
    dot_general x24, matrix products, delta_stretch(): jnp.einsum('hcd,hdw->hcw', queries, state, precision=precise)  70.2 us
    dot_general x24, matrix products, delta_stretch(): jnp.einsum('hc,hcd,hcw->hdw', gamma[:, -1, :], keys_t, updates, precision...  69 us
    reduce_scatter x1, waiting for transfers between devices, local(): lax.psum_scatter(full_grads[7].astype(jnp.bfloat16), 'dp', scatter_dimens...  66.2 us
  transfers between devices with their start and end apart: 25, of which 17 were waited for; matrix products, arithmetic and copies ran while one was open for 65% of the time, Pallas kernels for 0%

commit v1 on v0

v1 whole, which is shorter than its diff:
```python
import functools

import jax
import jax.numpy as jnp
from jax import lax
from jax.experimental import pallas as pl
from jax.experimental.pallas import tpu as pltpu
from jax.sharding import PartitionSpec as P

H = 8
DK = 128
DV = 256
CONV = 4
HALO = 16
CHUNK = 128
HC = 2 * DK + DV
LANES = 128
VMEM_LIMIT = 56 * 2**20

F32 = jnp.float32
BF16 = jnp.bfloat16
NN = ((1,), (0,))
NT = ((1,), (1,))
TN = ((0,), (0,))


def mm(left, right, dims=NN):
    return lax.dot_general(
        left.astype(BF16), right.astype(BF16), (dims, ((), ())), preferred_element_type=F32
    )


def mm_exact(left, right, dims=NN):
    return lax.dot_general(
        left, right, (dims, ((), ())), precision=lax.Precision.HIGHEST, preferred_element_type=F32
    )


def halves(value):
    high = value.astype(BF16)
    return high, (value - high.astype(F32)).astype(BF16)


def mm_three(left, right):
    left_high, left_low = halves(left)
    right_high, right_low = halves(right)
    return mm(left_high, right_high) + (mm(left_high, right_low) + mm(left_low, right_high))


def params(**more):
    return pltpu.CompilerParams(vmem_limit_bytes=VMEM_LIMIT, **more)


def cost(flops, nbytes):
    return pl.CostEstimate(flops=int(flops), bytes_accessed=int(nbytes), transcendentals=0)


def iota2(shape, axis):
    return lax.broadcasted_iota(jnp.int32, shape, axis)


def lane(value, index):
    picked = jnp.where(iota2(value.shape, 1) == index, value, 0.0)
    return jnp.sum(picked, axis=1, keepdims=True)


def to_row(column):
    size = column.shape[0]
    same = iota2((size, size), 0) == iota2((size, size), 1)
    return jnp.sum(jnp.where(same, column, 0.0), axis=0, keepdims=True)


def to_column(row):
    size = row.shape[1]
    same = iota2((size, size), 0) == iota2((size, size), 1)
    return jnp.sum(jnp.where(same, row, 0.0), axis=1, keepdims=True)


def project_kernel(x_ref, gain_ref, w_ref, wg_ref, p_ref, logit_ref, h_ref):
    @pl.when(pl.program_id(0) == 0)
    def _():
        value = x_ref[...].astype(F32)
        scale = lax.rsqrt(jnp.mean(value * value, axis=-1, keepdims=True) + 1e-06)
        h_ref[...] = (value * scale * gain_ref[...]).astype(BF16)
        logit_ref[...] = mm(h_ref[...], wg_ref[...])

    p_ref[...] = mm(h_ref[...], w_ref[...]).astype(BF16)


def project(x_ext, gain, w_qkv, w_gates):
    rows, width = x_ext.shape
    block = 512
    cols = w_qkv.shape[1]
    return pl.pallas_call(
        project_kernel,
        grid=(cols // block,),
        in_specs=[
            pl.BlockSpec((rows, width), lambda j: (0, 0)),
            pl.BlockSpec((1, width), lambda j: (0, 0)),
            pl.BlockSpec((width, block), lambda j: (0, j)),
            pl.BlockSpec((width, LANES), lambda j: (0, 0)),
        ],
        out_specs=[
            pl.BlockSpec((rows, block), lambda j: (0, j)),
            pl.BlockSpec((rows, LANES), lambda j: (0, 0)),
            pl.BlockSpec((rows, width), lambda j: (0, 0)),
        ],
        out_shape=[
            jax.ShapeDtypeStruct((rows, cols), BF16),
            jax.ShapeDtypeStruct((rows, LANES), F32),
            jax.ShapeDtypeStruct((rows, width), BF16),
        ],
        compiler_params=params(),
        cost_estimate=cost(2 * rows * width * cols, 2 * width * cols + 2 * rows * cols),
        name="project",
    )(x_ext, gain, w_qkv, w_gates)


def outgate_kernel(h_ref, w_ref, g_ref):
    g_ref[...] = mm(h_ref[HALO:, :], w_ref[...])


def outgate(hidden, w_og):
    rows, width = hidden.shape
    cols = w_og.shape[1]
    block = 512
    return pl.pallas_call(
        outgate_kernel,
        grid=(cols // block,),
        in_specs=[
            pl.BlockSpec((rows, width), lambda j: (0, 0)),
            pl.BlockSpec((width, block), lambda j: (0, j)),
        ],
        out_specs=pl.BlockSpec((rows - HALO, block), lambda j: (0, j)),
        out_shape=jax.ShapeDtypeStruct((rows - HALO, cols), F32),
        compiler_params=params(),
        cost_estimate=cost(2 * rows * width * cols, 2 * width * cols + 4 * rows * cols),
        name="outgate",
    )(hidden, w_og)


def outer_kernel(left_ref, right_ref, out_ref, *, skip_left, skip_right):
    out_ref[...] = mm(left_ref[skip_left:, :], right_ref[skip_right:, :], TN).astype(BF16)


def outer(left, right, block=512, skip_left=0, skip_right=0):
    rows, width = left.shape
    cols = right.shape[1]
    block = min(block, cols)
    return pl.pallas_call(
        functools.partial(outer_kernel, skip_left=skip_left, skip_right=skip_right),
        grid=(cols // block,),
        in_specs=[
            pl.BlockSpec((rows, width), lambda j: (0, 0)),
            pl.BlockSpec((right.shape[0], block), lambda j: (0, j)),
        ],
        out_specs=pl.BlockSpec((width, block), lambda j: (0, j)),
        out_shape=jax.ShapeDtypeStruct((width, cols), BF16),
        compiler_params=params(),
        cost_estimate=cost(2 * rows * width * cols, 2 * width * cols + 2 * rows * cols),
        name="outer",
    )(left, right)


def gate_tables(logit_ref, par_ref, beta_ref, decay_ref, cum_ref):
    logits = logit_ref[HALO:, :]
    beta_ref[...] = jax.nn.sigmoid(logits)
    shifted = logits + par_ref[1:2, :]
    soft = jnp.maximum(shifted, 0.0) + jnp.log1p(jnp.exp(-jnp.abs(shifted)))
    decay_ref[...] = -jnp.exp(par_ref[0:1, :]) * soft
    lower = (iota2((CHUNK, CHUNK), 0) >= iota2((CHUNK, CHUNK), 1)).astype(F32)
    for c in range(logits.shape[0] // CHUNK):
        part = decay_ref[c * CHUNK : (c + 1) * CHUNK, :]
        cum_ref[c * CHUNK : (c + 1) * CHUNK, :] = mm_exact(lower, part)


def mix_taps(p_ref, taps_ref, cols, pf_ref):
    tokens = cols.shape[0]
    pf_ref[...] = p_ref[...].astype(F32)
    total = pf_ref[HALO:, :] * taps_ref[0:1, :]
    for j in range(1, CONV):
        total += pf_ref[HALO - j : HALO - j + tokens, :] * taps_ref[j : j + 1, :] * cols[:, j : j + 1]
    return total


def chunk_tables(c, head, cols, segr_ref, cum_ref):
    rows = slice(c * CHUNK, (c + 1) * CHUNK)
    cum = lane(cum_ref[rows, :], head)
    cum_row = to_row(cum)
    same = cols[rows, 0:1] == segr_ref[0:1, rows]
    row_ids, col_ids = iota2((CHUNK, CHUNK), 0), iota2((CHUNK, CHUNK), 1)
    gamma = jnp.where((row_ids >= col_ids) & same, jnp.exp(jnp.minimum(cum - cum_row, 0.0)), 0.0)
    strict = jnp.where(row_ids > col_ids, gamma, 0.0)
    carry = jnp.exp(cum) * cols[rows, 4:5]
    last = jnp.exp(cum[CHUNK - 1 :, :] - cum) * cols[rows, 5:6]
    return gamma, strict, carry, last


def unit_lower_inverses(systems):
    size = systems[0].shape[0]
    row_ids, col_ids = iota2((size, size), 0), iota2((size, size), 1)
    eye = (row_ids == col_ids).astype(F32)
    found = [eye - jnp.where(row_ids // 2 == col_ids // 2, low, 0.0) for low in systems]
    width = 2
    while width < size:
        joined = (row_ids // (2 * width) == col_ids // (2 * width)) & (
            row_ids // width != col_ids // width
        )
        first = [mm_three(jnp.where(joined, low, 0.0), inv) for low, inv in zip(systems, found)]
        found = [inv - mm_three(inv, part) for inv, part in zip(found, first)]
        width *= 2
    return found


def forward_kernel(
    p_ref, taps_ref, logit_ref, par_ref, cols_ref, segr_ref,
    part_ref, resp_ref, map_ref, sum_ref, inv_ref, upd_ref, st_ref, stm_ref, amap_ref, rmap_ref,
    beta_ref, decay_ref, cum_ref, pf_ref, mix_ref,
):
    head = pl.program_id(0)

    @pl.when(head == 0)
    def _():
        gate_tables(logit_ref, par_ref, beta_ref, decay_ref, cum_ref)

    cols = cols_ref[...]
    tokens = cols.shape[0]
    total = mix_taps(p_ref, taps_ref, cols, pf_ref)
    mix_ref[...] = total * jax.nn.sigmoid(total)
    beta = lane(beta_ref[...], head + H)
    chunks = range(tokens // CHUNK)
    tables, lows, keys, queries = [], [], [], []
    for c in chunks:
        rows = slice(c * CHUNK, (c + 1) * CHUNK)
        query = mix_ref[rows, :DK]
        query = query * (lax.rsqrt(jnp.sum(query * query, axis=1, keepdims=True) + 1e-06) * DK**-0.5)
        key = mix_ref[rows, DK : 2 * DK]
        key = key * lax.rsqrt(jnp.sum(key * key, axis=1, keepdims=True) + 1e-06)
        gamma, strict, carry, last = chunk_tables(c, head, cols, segr_ref, cum_ref)
        dots = mm(jnp.concatenate([key, query], axis=0), key, NT)
        lows.append(beta[rows] * strict * dots[:CHUNK])
        tables.append((gamma * dots[CHUNK:], carry, last))
        keys.append(key)
        queries.append(query)
    inverses = unit_lower_inverses(lows)
    state = None
    for c in chunks:
        rows = slice(c * CHUNK, (c + 1) * CHUNK)
        scores, carry, last = tables[c]
        key, query = keys[c], queries[c]
        target = jnp.concatenate([mix_ref[rows, 2 * DK :], carry * key], axis=1) * beta[rows]
        updates = mm(inverses[c], target)
        inv_ref[0, c] = inverses[c].astype(BF16)
        upd_ref[0, rows, :] = updates
        weighted_t = jnp.transpose(last * key)
        both = mm(jnp.concatenate([weighted_t, scores], axis=0), updates)
        eye = (iota2((DK, DK), 0) == iota2((DK, DK), 1)).astype(F32)
        step_map = carry[CHUNK - 1 :, :] * eye - both[:DK, DV:]
        read_map = carry * query - both[DK:, DV:]
        amap_ref[0, c] = step_map.astype(BF16)
        rmap_ref[0, c] = read_map.astype(BF16)
        if c == 0:
            st_ref[0, c] = jnp.zeros((DK, DV), F32)
            stm_ref[0, c] = eye.astype(BF16)
            part_ref[rows, :] = both[DK:, :DV]
            resp_ref[rows, :] = read_map.astype(BF16)
            state = jnp.concatenate([both[:DK, :DV], step_map], axis=1)
        else:
            st_ref[0, c] = state[:, :DV]
            stm_ref[0, c] = state[:, DV:].astype(BF16)
            moved = mm(jnp.concatenate([step_map, read_map], axis=0), state)
            part_ref[rows, :] = both[DK:, :DV] + moved[DK:, :DV]
            resp_ref[rows, :] = moved[DK:, DV:].astype(BF16)
            state = moved[:DK] + jnp.concatenate(
                [both[:DK, :DV], jnp.zeros((DK, DK), F32)], axis=1
            )
    map_ref[0] = state[:, DV:].astype(BF16)
    sum_ref[0] = state[:, :DV].astype(BF16)


def delta_forward(proj, taps, logits, par, cols, segr):
    rows = proj.shape[0]
    tokens = rows - HALO
    chunks = tokens // CHUNK
    whole = lambda shape: pl.BlockSpec(shape, lambda h: (0,) * len(shape))
    by_head = lambda shape: pl.BlockSpec(shape, lambda h: (h,) + (0,) * (len(shape) - 1))
    return pl.pallas_call(
        forward_kernel,
        grid=(H,),
        in_specs=[
            pl.BlockSpec((rows, HC), lambda h: (0, h)),
            pl.BlockSpec((8, HC), lambda h: (0, h)),
            whole((rows, LANES)),
            whole((8, LANES)),
            whole((tokens, LANES)),
            whole((8, tokens)),
        ],
        out_specs=[
            pl.BlockSpec((tokens, DV), lambda h: (0, h)),
            pl.BlockSpec((tokens, DK), lambda h: (0, h)),
            by_head((1, DK, DK)),
            by_head((1, DK, DV)),
            by_head((1, chunks, CHUNK, CHUNK)),
            by_head((1, tokens, DV + DK)),
            by_head((1, chunks, DK, DV)),
            by_head((1, chunks, DK, DK)),
            by_head((1, chunks, DK, DK)),
            by_head((1, chunks, CHUNK, DK)),
        ],
        out_shape=[
            jax.ShapeDtypeStruct((tokens, H * DV), F32),
            jax.ShapeDtypeStruct((tokens, H * DK), BF16),
            jax.ShapeDtypeStruct((H, DK, DK), BF16),
            jax.ShapeDtypeStruct((H, DK, DV), BF16),
            jax.ShapeDtypeStruct((H, chunks, CHUNK, CHUNK), BF16),
            jax.ShapeDtypeStruct((H, tokens, DV + DK), F32),
            jax.ShapeDtypeStruct((H, chunks, DK, DV), F32),
            jax.ShapeDtypeStruct((H, chunks, DK, DK), BF16),
            jax.ShapeDtypeStruct((H, chunks, DK, DK), BF16),
            jax.ShapeDtypeStruct((H, chunks, CHUNK, DK), BF16),
        ],
        scratch_shapes=[
            pltpu.VMEM((tokens, LANES), F32),
            pltpu.VMEM((tokens, LANES), F32),
            pltpu.VMEM((tokens, LANES), F32),
            pltpu.VMEM((rows, HC), F32),
            pltpu.VMEM((tokens, HC), F32),
        ],
        compiler_params=params(),
        cost_estimate=cost(3e10, 3e7),
        name="delta_forward",
    )(proj, taps, logits, par, cols, segr)


def backward_kernel(
    place_ref, p_ref, taps_ref, logit_ref, par_ref, cols_ref, back_ref, segr_ref,
    dattn_ref, sin_ref, maps_ref, grads_ref,
    inv_ref, upd_ref, st_ref, stm_ref, amap_ref, rmap_ref,
    dp_ref, dlogit_ref, dtaps_ref, dpar_ref,
    beta_ref, decay_ref, cum_ref, pf_ref, pre_ref, dmix_ref,
):
    head = pl.program_id(0)
    place = place_ref[0]
    places = maps_ref.shape[0]

    @pl.when(head == 0)
    def _():
        gate_tables(logit_ref, par_ref, beta_ref, decay_ref, cum_ref)
        dlogit_ref[...] = jnp.zeros_like(dlogit_ref)
        dpar_ref[...] = jnp.zeros_like(dpar_ref)

    cols = cols_ref[...]
    tokens = cols.shape[0]
    chunks = range(tokens // CHUNK)
    pre = mix_taps(p_ref, taps_ref, cols, pf_ref)
    pre_ref[...] = pre
    beta = lane(beta_ref[...], head + H)

    def behind(lap, grad):
        source = places - 1 - lap
        return jnp.where(
            source > place,
            grads_ref[source, 0].astype(F32) + mm(maps_ref[source, 0], grad, TN),
            grad,
        )

    d_state = lax.fori_loop(0, places - 1, behind, jnp.zeros((DK, DV), F32))
    state_in = sin_ref[0]
    d_states = [None] * len(chunks)
    for c in reversed(chunks):
        rows = slice(c * CHUNK, (c + 1) * CHUNK)
        d_states[c] = d_state
        if c > 0:
            d_state = mm(amap_ref[0, c], d_state, TN) + mm(rmap_ref[0, c], dattn_ref[rows, :], TN)

    row_ids, col_ids = iota2((CHUNK, CHUNK), 0), iota2((CHUNK, CHUNK), 1)
    d_beta_all, d_decay_all = [], []
    for c in chunks:
        rows = slice(c * CHUNK, (c + 1) * CHUNK)
        mixed = pre_ref[rows, :]
        gate = jax.nn.sigmoid(mixed)
        slope = gate * (1.0 + mixed * (1.0 - gate))
        mixed = mixed * gate
        query_raw, key_raw, value = mixed[:, :DK], mixed[:, DK : 2 * DK], mixed[:, 2 * DK :]
        query_size = lax.rsqrt(jnp.sum(query_raw * query_raw, axis=1, keepdims=True) + 1e-06)
        key_size = lax.rsqrt(jnp.sum(key_raw * key_raw, axis=1, keepdims=True) + 1e-06)
        query_unit, key = query_raw * query_size, key_raw * key_size
        query = query_unit * DK**-0.5
        gamma, strict, carry, last = chunk_tables(c, head, cols, segr_ref, cum_ref)
        strength = beta[rows]
        dots = mm(jnp.concatenate([key, query], axis=0), key, NT)
        weights = strict * dots[:CHUNK]
        low = strength * weights
        scores = gamma * dots[CHUNK:]
        if c == 0:
            state = state_in
        else:
            state = st_ref[0, c] + mm(stm_ref[0, c], state_in)
        updates = upd_ref[0, rows, :DV] - mm(upd_ref[0, rows, DV:], state)
        d_attn = dattn_ref[rows, :]
        d_state = d_states[c]
        d_updates = mm(scores, d_attn, TN) + mm(last * key, d_state)
        solved = mm(inv_ref[0, c], d_updates, TN)
        both = jnp.concatenate([d_attn, solved.astype(BF16)], axis=0)
        by_updates = mm(both, updates, NT)
        by_state = mm(both, state, NT)
        d_scores = by_updates[:CHUNK]
        d_low = -by_updates[CHUNK:]
        d_query = carry * by_state[:CHUNK]
        key_state = jnp.sum(key * by_state[CHUNK:], axis=1, keepdims=True)
        d_carry = jnp.sum(query * by_state[:CHUNK], axis=1, keepdims=True) - strength * key_state
        d_beta = (
            jnp.sum(solved * value, axis=1, keepdims=True)
            - carry * key_state
            + jnp.sum(d_low * weights, axis=1, keepdims=True)
        )
        d_dots_q = d_scores * gamma
        d_dots_k = d_low * strength * strict
        by_key = mm(jnp.concatenate([d_dots_q, d_dots_k], axis=0), key)
        d_query += by_key[:CHUNK]
        from_state = mm(updates, d_state, NT)
        d_key = (
            by_key[CHUNK:]
            + mm(
                jnp.concatenate([d_dots_q, d_dots_k], axis=0),
                jnp.concatenate([query, key], axis=0),
                TN,
            )
            - strength * carry * by_state[CHUNK:]
            + last * from_state
        )
        d_last = jnp.sum(key * from_state, axis=1, keepdims=True) * last
        d_spread = d_scores * scores + d_low * low
        final = (iota2((CHUNK, 1), 0) == CHUNK - 1).astype(F32)
        d_carry += final * jnp.sum(d_state * state)
        d_cum = (
            jnp.sum(d_spread, axis=1, keepdims=True)
            - to_column(jnp.sum(d_spread, axis=0, keepdims=True))
            + final * jnp.sum(d_last)
            - d_last
            + d_carry * carry
        )
        d_decay = jnp.sum(
            jnp.where(row_ids <= col_ids, to_row(d_cum), 0.0), axis=1, keepdims=True
        )
        d_beta_all.append(d_beta)
        d_decay_all.append(d_decay)
        d_query = d_query * DK**-0.5
        d_query = query_size * (
            d_query - query_unit * jnp.sum(d_query * query_unit, axis=1, keepdims=True)
        )
        d_key = key_size * (d_key - key * jnp.sum(d_key * key, axis=1, keepdims=True))
        d_value = strength * solved
        dmix_ref[HALO + c * CHUNK : HALO + (c + 1) * CHUNK, :] = slope * jnp.concatenate(
            [d_query, d_key, d_value], axis=1
        )

    d_beta = jnp.concatenate(d_beta_all, axis=0)
    d_decay = jnp.concatenate(d_decay_all, axis=0)
    lanes = iota2((tokens, LANES), 1)
    slope = jax.nn.sigmoid(logit_ref[HALO:, :] + par_ref[1:2, :]) * -jnp.exp(par_ref[0:1, :])
    here = jnp.where(lanes == head, d_decay, 0.0)
    d_first = here * slope
    strengths = beta_ref[...]
    d_second = jnp.where(lanes == head + H, d_beta, 0.0) * strengths * (1.0 - strengths)
    dlogit_ref[...] += d_first + d_second
    dpar_ref[0:1, :] += jnp.sum(here * decay_ref[...], axis=0, keepdims=True)
    dpar_ref[1:2, :] += jnp.sum(d_first, axis=0, keepdims=True)

    dmix_ref[:HALO, :] = jnp.zeros((HALO, HC), F32)
    dmix_ref[HALO + tokens :, :] = jnp.zeros((8, HC), F32)
    d_mix = dmix_ref[HALO : HALO + tokens, :]
    dtaps_ref[...] = jnp.zeros_like(dtaps_ref)
    dtaps_ref[0:1, :] = jnp.sum(d_mix * pf_ref[HALO:, :], axis=0, keepdims=True)
    total = dmix_ref[: HALO + tokens, :] * taps_ref[0:1, :]
    for j in range(1, CONV):
        total += dmix_ref[j : j + HALO + tokens, :] * taps_ref[j : j + 1, :] * back_ref[:, j : j + 1]
        dtaps_ref[j : j + 1, :] = jnp.sum(
            d_mix * cols[:, j : j + 1] * pf_ref[HALO - j : HALO - j + tokens, :],
            axis=0,
            keepdims=True,
        )
    dp_ref[...] = total.astype(BF16)


def delta_backward(place, proj, taps, logits, par, cols, back, segr, d_attn, state_in, maps, grads, saved):
    rows = proj.shape[0]
    tokens = rows - HALO
    chunks = tokens // CHUNK
    places = maps.shape[0]
    whole = lambda shape: pl.BlockSpec(shape, lambda h: (0,) * len(shape))
    by_head = lambda shape: pl.BlockSpec(shape, lambda h: (h,) + (0,) * (len(shape) - 1))
    return pl.pallas_call(
        backward_kernel,
        grid=(H,),
        in_specs=[
            pl.BlockSpec(memory_space=pltpu.SMEM),
            pl.BlockSpec((rows, HC), lambda h: (0, h)),
            pl.BlockSpec((8, HC), lambda h: (0, h)),
            whole((rows, LANES)),
            whole((8, LANES)),
            whole((tokens, LANES)),
            whole((rows, LANES)),
            whole((8, tokens)),
            pl.BlockSpec((tokens, DV), lambda h: (0, h)),
            by_head((1, DK, DV)),
            pl.BlockSpec((places, 1, DK, DK), lambda h: (0, h, 0, 0)),
            pl.BlockSpec((places, 1, DK, DV), lambda h: (0, h, 0, 0)),
            by_head((1, chunks, CHUNK, CHUNK)),
            by_head((1, tokens, DV + DK)),
            by_head((1, chunks, DK, DV)),
            by_head((1, chunks, DK, DK)),
            by_head((1, chunks, DK, DK)),
            by_head((1, chunks, CHUNK, DK)),
        ],
        out_specs=[
            pl.BlockSpec((rows, HC), lambda h: (0, h)),
            whole((tokens, LANES)),
            pl.BlockSpec((8, HC), lambda h: (0, h)),
            whole((8, LANES)),
        ],
        out_shape=[
            jax.ShapeDtypeStruct((rows, H * HC), BF16),
            jax.ShapeDtypeStruct((tokens, LANES), F32),
            jax.ShapeDtypeStruct((8, H * HC), F32),
            jax.ShapeDtypeStruct((8, LANES), F32),
        ],
        scratch_shapes=[
            pltpu.VMEM((tokens, LANES), F32),
            pltpu.VMEM((tokens, LANES), F32),
            pltpu.VMEM((tokens, LANES), F32),
            pltpu.VMEM((rows, HC), F32),
            pltpu.VMEM((tokens, HC), F32),
            pltpu.VMEM((rows + 8, HC), F32),
        ],
        compiler_params=params(),
        cost_estimate=cost(4e10, 4e7),
        name="delta_backward",
    )(place, proj, taps, logits, par, cols, back, segr, d_attn, state_in, maps, grads, *saved)


def mixer_kernel(
    place_ref, part_ref, resp_ref, maps_ref, sums_ref, gpre_ref, gain_ref, w_ref, x_ref, gain2_ref,
    sin_ref, attn_ref, gated_ref, y_ref, h_ref,
):
    head = pl.program_id(0)
    place = place_ref[0]
    places = maps_ref.shape[0]

    def ahead(source, state):
        return jnp.where(
            source < place,
            sums_ref[source, 0].astype(F32) + mm(maps_ref[source, 0], state),
            state,
        )

    state = lax.fori_loop(0, places - 1, ahead, jnp.zeros((DK, DV), F32))
    sin_ref[0] = state
    attn = part_ref[...] + mm(resp_ref[...], state)
    attn_ref[...] = attn
    scale = lax.rsqrt(jnp.mean(attn * attn, axis=-1, keepdims=True) + 1e-05)
    gate = gpre_ref[...]
    gated = (attn * scale * gain_ref[...] * (gate * jax.nn.sigmoid(gate))).astype(BF16)
    gated_ref[...] = gated

    @pl.when(head == 0)
    def _():
        y_ref[...] = x_ref[...].astype(F32)

    y_ref[...] += mm(gated, w_ref[...])

    @pl.when(head == pl.num_programs(0) - 1)
    def _():
        value = y_ref[...]
        size = lax.rsqrt(jnp.mean(value * value, axis=-1, keepdims=True) + 1e-06)
        h_ref[...] = (value * size * gain2_ref[...]).astype(BF16)


def mixer_out(place, part, resp, maps, sums, gpre, gain, w_out, x, gain2):
    tokens, width = x.shape
    places = maps.shape[0]
    whole = lambda shape: pl.BlockSpec(shape, lambda h: (0,) * len(shape))
    return pl.pallas_call(
        mixer_kernel,
        grid=(H,),
        in_specs=[
            pl.BlockSpec(memory_space=pltpu.SMEM),
            pl.BlockSpec((tokens, DV), lambda h: (0, h)),
            pl.BlockSpec((tokens, DK), lambda h: (0, h)),
            pl.BlockSpec((places, 1, DK, DK), lambda h: (0, h, 0, 0)),
            pl.BlockSpec((places, 1, DK, DV), lambda h: (0, h, 0, 0)),
            pl.BlockSpec((tokens, DV), lambda h: (0, h)),
            whole((1, DV)),
            pl.BlockSpec((DV, width), lambda h: (h, 0)),
            whole((tokens, width)),
            whole((1, width)),
        ],
        out_specs=[
            pl.BlockSpec((1, DK, DV), lambda h: (h, 0, 0)),
            pl.BlockSpec((tokens, DV), lambda h: (0, h)),
            pl.BlockSpec((tokens, DV), lambda h: (0, h)),
            whole((tokens, width)),
            whole((tokens, width)),
        ],
        out_shape=[
            jax.ShapeDtypeStruct((H, DK, DV), F32),
            jax.ShapeDtypeStruct((tokens, H * DV), F32),
            jax.ShapeDtypeStruct((tokens, H * DV), BF16),
            jax.ShapeDtypeStruct((tokens, width), F32),
            jax.ShapeDtypeStruct((tokens, width), BF16),
        ],
        compiler_params=params(),
        cost_estimate=cost(2 * tokens * width * H * DV, 2e7),
        name="mixer_out",
    )(place, part, resp, maps, sums, gpre, gain, w_out, x, gain2)


def mixer_back_kernel(
    dmix_ref, w_ref, attn_ref, gpre_ref, gain_ref, resp_ref,
    dattn_ref, dgpre_ref, grad_ref, dgain_ref,
):
    @pl.when(pl.program_id(0) == 0)
    def _():
        dgain_ref[...] = jnp.zeros_like(dgain_ref)

    d_gated = mm(dmix_ref[...], w_ref[...], NT)
    attn = attn_ref[...]
    size = lax.rsqrt(jnp.mean(attn * attn, axis=-1, keepdims=True) + 1e-05)
    unit = attn * size
    gate = gpre_ref[...]
    slope = jax.nn.sigmoid(gate)
    swish = gate * slope
    gain = gain_ref[...]
    dgpre_ref[...] = (d_gated * (unit * gain) * (slope * (1.0 + gate * (1.0 - slope)))).astype(BF16)
    d_normed = d_gated * swish
    dgain_ref[0:1, :] += jnp.sum(d_normed * unit, axis=0, keepdims=True)
    d_unit = d_normed * gain
    d_attn = size * (d_unit - unit * jnp.mean(d_unit * unit, axis=-1, keepdims=True))
    d_attn = d_attn.astype(BF16)
    dattn_ref[...] = d_attn
    grad_ref[0] = mm(resp_ref[...], d_attn, TN).astype(BF16)


def mixer_back(d_mixer, w_out, attn, gpre, gain, resp):
    tokens, width = d_mixer.shape
    whole = lambda shape: pl.BlockSpec(shape, lambda h: (0,) * len(shape))
    return pl.pallas_call(
        mixer_back_kernel,
        grid=(H,),
        in_specs=[
            whole((tokens, width)),
            pl.BlockSpec((DV, width), lambda h: (h, 0)),
            pl.BlockSpec((tokens, DV), lambda h: (0, h)),
            pl.BlockSpec((tokens, DV), lambda h: (0, h)),
            whole((1, DV)),
            pl.BlockSpec((tokens, DK), lambda h: (0, h)),
        ],
        out_specs=[
            pl.BlockSpec((tokens, DV), lambda h: (0, h)),
            pl.BlockSpec((tokens, DV), lambda h: (0, h)),
            pl.BlockSpec((1, DK, DV), lambda h: (h, 0, 0)),
            whole((8, DV)),
        ],
        out_shape=[
            jax.ShapeDtypeStruct((tokens, H * DV), BF16),
            jax.ShapeDtypeStruct((tokens, H * DV), BF16),
            jax.ShapeDtypeStruct((H, DK, DV), BF16),
            jax.ShapeDtypeStruct((8, DV), F32),
        ],
        compiler_params=params(),
        cost_estimate=cost(2 * tokens * width * H * DV, 2e7),
        name="mixer_back",
    )(d_mixer, w_out, attn, gpre, gain, resp)


def ffn_kernel(
    h_ref, dout_ref, y_ref, gain_ref, wg_ref, wu_ref, wd_ref,
    out_ref, act_ref, dg_ref, du_ref, dy_ref, dmix_ref, dgain_ref, res_ref, dh_ref,
):
    step = pl.program_id(0)

    @pl.when(step == 0)
    def _():
        res_ref[...] = y_ref[...]
        dh_ref[...] = jnp.zeros_like(dh_ref)

    hidden = h_ref[...]
    gate = mm(hidden, wg_ref[...])
    up = mm(hidden, wu_ref[...])
    d_act = mm(dout_ref[...], wd_ref[...], NT)
    slope = jax.nn.sigmoid(gate)
    swish = gate * slope
    act = (swish * up).astype(BF16)
    act_ref[...] = act
    d_gate = (d_act * up * slope * (1.0 + gate * (1.0 - slope))).astype(BF16)
    d_up = (d_act * swish).astype(BF16)
    dg_ref[...] = d_gate
    du_ref[...] = d_up
    res_ref[...] += mm(act, wd_ref[...])
    dh_ref[...] += mm(d_gate, wg_ref[...], NT) + mm(d_up, wu_ref[...], NT)

    @pl.when(step == pl.num_programs(0) - 1)
    def _():
        out_ref[...] = res_ref[...].astype(BF16)
        value = y_ref[...]
        size = lax.rsqrt(jnp.mean(value * value, axis=-1, keepdims=True) + 1e-06)
        unit = value * size
        d_hidden = dh_ref[...]
        dgain_ref[...] = jnp.zeros_like(dgain_ref)
        dgain_ref[0:1, :] = jnp.sum(d_hidden * unit, axis=0, keepdims=True)
        d_unit = d_hidden * gain_ref[...]
        d_y = dout_ref[...].astype(F32) + size * (
            d_unit - unit * jnp.mean(d_unit * unit, axis=-1, keepdims=True)
        )
        dy_ref[...] = d_y
        dmix_ref[...] = d_y.astype(BF16)


def feed_forward(hidden, d_out, y1, gain, w_gate, w_up, w_down):
    tokens, width = hidden.shape
    inner = w_down.shape[0]
    block = 256
    whole = lambda shape: pl.BlockSpec(shape, lambda j: (0,) * len(shape))
    across = pl.BlockSpec((tokens, block), lambda j: (0, j))
    return pl.pallas_call(
        ffn_kernel,
        grid=(inner // block,),
        in_specs=[
            whole((tokens, width)),
            whole((tokens, width)),
            whole((tokens, width)),
            whole((1, width)),
            pl.BlockSpec((width, block), lambda j: (0, j)),
            pl.BlockSpec((width, block), lambda j: (0, j)),
            pl.BlockSpec((block, width), lambda j: (j, 0)),
        ],
        out_specs=[
            whole((tokens, width)), across, across, across,
            whole((tokens, width)), whole((tokens, width)), whole((8, width)),
        ],
        out_shape=[
            jax.ShapeDtypeStruct((tokens, width), BF16),
            jax.ShapeDtypeStruct((tokens, inner), BF16),
            jax.ShapeDtypeStruct((tokens, inner), BF16),
            jax.ShapeDtypeStruct((tokens, inner), BF16),
            jax.ShapeDtypeStruct((tokens, width), F32),
            jax.ShapeDtypeStruct((tokens, width), BF16),
            jax.ShapeDtypeStruct((8, width), F32),
        ],
        scratch_shapes=[pltpu.VMEM((tokens, width), F32), pltpu.VMEM((tokens, width), F32)],
        compiler_params=params(),
        cost_estimate=cost(12 * tokens * width * inner, 3e7),
        name="feed_forward",
    )(hidden, d_out, y1, gain, w_gate, w_up, w_down)


def input_grad_kernel(
    dp_ref, dg_ref, dl_ref, wq_ref, wo_ref, wl_ref, x_ref, gain_ref, dy_ref,
    out_ref, dgain_ref, acc_ref, *, first,
):
    step = pl.program_id(0)

    @pl.when(step == 0)
    def _():
        acc_ref[...] = mm(dl_ref[...], wl_ref[...], NT)

    @pl.when(step < first)
    def _():
        acc_ref[...] += mm(dp_ref[HALO:, :], wq_ref[...], NT)

    @pl.when(step >= first)
    def _():
        acc_ref[...] += mm(dg_ref[...], wo_ref[...], NT)

    @pl.when(step == pl.num_programs(0) - 1)
    def _():
        value = x_ref[...].astype(F32)
        size = lax.rsqrt(jnp.mean(value * value, axis=-1, keepdims=True) + 1e-06)
        unit = value * size
        d_hidden = acc_ref[...]
        dgain_ref[...] = jnp.zeros_like(dgain_ref)
        dgain_ref[0:1, :] = jnp.sum(d_hidden * unit, axis=0, keepdims=True)
        d_unit = d_hidden * gain_ref[...]
        out_ref[...] = dy_ref[...] + size * (
            d_unit - unit * jnp.mean(d_unit * unit, axis=-1, keepdims=True)
        )


def input_grad(d_proj, d_gpre, d_logit, w_qkv, w_og, w_gates, x, gain, d_y):
    tokens, width = x.shape
    rows = d_proj.shape[0]
    block = 512
    first, second = w_qkv.shape[1] // block, w_og.shape[1] // block
    whole = lambda shape: pl.BlockSpec(shape, lambda j: (0,) * len(shape))
    early = lambda j: (0, jnp.minimum(j, first - 1))
    late = lambda j: (0, jnp.maximum(j - first, 0))
    return pl.pallas_call(
        functools.partial(input_grad_kernel, first=first),
        grid=(first + second,),
        in_specs=[
            pl.BlockSpec((rows, block), early),
            pl.BlockSpec((tokens, block), late),
            whole((tokens, LANES)),
            pl.BlockSpec((width, block), early),
            pl.BlockSpec((width, block), late),
            whole((width, LANES)),
            whole((tokens, width)),
            whole((1, width)),
            whole((tokens, width)),
        ],
        out_specs=[whole((tokens, width)), whole((8, width))],
        out_shape=[
            jax.ShapeDtypeStruct((tokens, width), F32),
            jax.ShapeDtypeStruct((8, width), F32),
        ],
        scratch_shapes=[pltpu.VMEM((tokens, width), F32)],
        compiler_params=params(),
        cost_estimate=cost(2 * tokens * width * (first + second) * block, 3e7),
        name="input_grad",
    )(d_proj, d_gpre, d_logit, w_qkv, w_og, w_gates, x, gain, d_y)


def shifted(block, axis, distance):
    devices = range(lax.axis_size(axis))
    route = [(i - distance, i) for i in devices if i - distance in devices]
    return lax.ppermute(block, axis, route)


def by_heads(query, key, value):
    lead = query.shape[:-1]
    parts = [query.reshape(lead + (H, DK)), key.reshape(lead + (H, DK)), value.reshape(lead + (H, DV))]
    return jnp.concatenate(parts, axis=-1).reshape(lead + (H * HC,))


def from_heads(value):
    lead = value.shape[:-1]
    parts = value.reshape(lead + (H, HC))
    return (
        parts[..., :DK].reshape(lead + (H * DK,)),
        parts[..., DK : 2 * DK].reshape(lead + (H * DK,)),
        parts[..., 2 * DK :].reshape(lead + (H * DV,)),
    )


def token_tables(segments, place, tokens):
    seg_pad = jnp.concatenate([jnp.full((HALO,), -1, jnp.int32), segments, jnp.full((8,), -2, jnp.int32)])
    ext = lax.dynamic_slice_in_dim(seg_pad, place * tokens, tokens + HALO + 8)
    seg = ext[HALO : HALO + tokens]
    columns = [seg.astype(F32)]
    for j in range(1, CONV):
        columns.append((ext[HALO - j : HALO - j + tokens] == seg).astype(F32))
    blocks = seg.reshape(-1, CHUNK)
    before = ext[HALO - 1 : HALO - 1 + tokens : CHUNK]
    columns.append((blocks == before[:, None]).astype(F32).reshape(-1))
    columns.append((blocks == blocks[:, -1:]).astype(F32).reshape(-1))
    columns += [jnp.zeros_like(columns[0])] * (LANES - len(columns))
    cols = jnp.stack(columns, axis=1)
    rows = tokens + HALO
    back = [jnp.zeros((rows,), F32)]
    for j in range(1, CONV):
        back.append((ext[j : j + rows] == ext[:rows]).astype(F32))
    back += [jnp.zeros((rows,), F32)] * (LANES - len(back))
    segr = jnp.broadcast_to(seg.astype(F32)[None], (8, tokens))
    return cols, jnp.stack(back, axis=1), segr


def wide(value):
    return jnp.pad(value, ((0, 0), (0, LANES - value.shape[1])))


def local(
    inputs, segments, cotangent, norm_gain_mix, w_query, w_key, w_value, w_outgate, w_gates,
    conv_weight, decay_log, dt_bias, out_norm_gain, w_out, norm_gain_ffn, w_ffn_gate, w_ffn_up, w_ffn_down,
):
    x, d_out = inputs[0], cotangent[0]
    tokens = x.shape[0]
    place = lax.axis_index("seq")
    place_arr = place.reshape((1,)).astype(jnp.int32)
    low = lambda a: a.astype(BF16)
    gather = lambda a, axis: lax.all_gather(a, "dp", axis=axis, tiled=True)

    qkv_w = gather(
        jnp.concatenate([by_heads(low(w_query), low(w_key), low(w_value)), wide(low(w_gates))], axis=1), 0
    )
    gates_w = qkv_w[:, H * HC :]
    qkv_w = qkv_w[:, : H * HC]
    og_w = gather(low(w_outgate), 0)
    out_w = gather(low(w_out), 1)
    gate_w = gather(low(w_ffn_gate), 0)
    up_w = gather(low(w_ffn_up), 0)
    down_w = gather(low(w_ffn_down), 1)

    gain_mix, gain_ffn, gain_out = norm_gain_mix[None], norm_gain_ffn[None], out_norm_gain[None]
    taps_parts = by_heads(conv_weight[:, : H * DK], conv_weight[:, H * DK : 2 * H * DK], conv_weight[:, 2 * H * DK :])
    taps = jnp.pad(taps_parts, ((0, 8 - CONV), (0, 0)))
    par = jnp.pad(jnp.stack([decay_log, dt_bias]), ((0, 6), (0, LANES - H)))
    cols, back, segr = token_tables(segments[0], place, tokens)

    x_ext = jnp.concatenate([shifted(x[tokens - HALO :], "seq", 1), x], axis=0)
    proj, logits, hidden = project(x_ext, gain_mix, qkv_w, gates_w)
    gpre = outgate(hidden, og_w)
    part, resp, step_map, step_sum, *saved = delta_forward(proj, taps, logits, par, cols, segr)
    maps = lax.all_gather(step_map, "seq")
    sums = lax.all_gather(step_sum, "seq")
    state_in, attn, gated, y1, hidden_mid = mixer_out(
        place_arr, part, resp, maps, sums, gpre, gain_out, out_w, x, gain_ffn
    )
    result, act, d_gate, d_up, d_y, d_mixer, d_gain_ffn = feed_forward(
        hidden_mid, d_out, y1, gain_ffn, gate_w, up_w, down_w
    )
    d_attn, d_gpre, local_grad, d_gain_out = mixer_back(d_mixer, out_w, attn, gpre, gain_out, resp)
    grads = lax.all_gather(local_grad, "seq")

    def scattered(grad, axis):
        part_sum = lax.psum_scatter(grad, "dp", scatter_dimension=axis, tiled=True)
        return lax.psum(part_sum, "seq").astype(F32)

    g_down = scattered(outer(act, d_out), 1)
    g_gate = scattered(outer(hidden_mid, d_gate, 256), 0)
    g_up = scattered(outer(hidden_mid, d_up, 256), 0)
    g_out = scattered(outer(gated, d_mixer), 1)
    g_og = scattered(outer(hidden, d_gpre, 512, HALO, 0), 0)
    d_proj, d_logits, d_taps, d_par = delta_backward(
        place_arr, proj, taps, logits, par, cols, back, segr, d_attn, state_in, maps, grads, saved
    )
    sent_back = shifted(d_proj[:HALO], "seq", -1)
    d_proj = d_proj.at[tokens:].add(sent_back)
    d_logit = low(d_logits)
    g_qkv = scattered(outer(hidden, d_proj, 512, HALO, HALO), 0)
    g_gates = scattered(outer(hidden, d_logit, 128, HALO, 0), 0)
    d_inputs, d_gain_mix = input_grad(d_proj, d_gpre, d_logit, qkv_w, og_w, gates_w, x, gain_mix, d_y)

    g_query, g_key, g_value = from_heads(g_qkv)
    small = lax.psum(
        (
            d_gain_mix[0],
            jnp.concatenate(from_heads(d_taps[:CONV]), axis=1),
            d_par[0, :H],
            d_par[1, :H],
            d_gain_out[0],
            d_gain_ffn[0],
        ),
        ("dp", "seq"),
    )
    return (
        result[None], d_inputs[None], small[0], g_query, g_key, g_value, g_og, g_gates[:, : 2 * H],
        small[1], small[2], small[3], small[4], g_out, small[5], g_gate, g_up, g_down,
    )


def solution(mesh):
    rows, cols, copied = P("dp", None), P(None, "dp"), P()
    tokens = P("dp", "seq", None)
    in_specs = (
        tokens, rows, tokens, copied, rows, rows, rows, rows, rows,
        copied, copied, copied, copied, cols, copied, rows, rows, cols,
    )
    out_specs = (
        tokens, tokens, copied, rows, rows, rows, rows, rows,
        copied, copied, copied, copied, cols, copied, rows, rows, cols,
    )
    return jax.shard_map(local, mesh=mesh, in_specs=in_specs, out_specs=out_specs, check_vma=False)
```

time: 2600 us -> 1190 us (0.46)
  other arithmetic: 858 us -> 17.6 us
  matrix products: 586 us -> 0 us
  Pallas kernels: 0 us -> 244 us
  local copies, waits for them, and re-layouts: 249 us -> 53.2 us
    another operation x117 -> x2, other arithmetic: 653 us -> 0.68 us  [the longest x1 0.6 us: local(): par = jnp.pad(jnp.stack([decay_log, dt_bias]), ((0, 6), (0, LANES - H)))]
    dot_general x186 -> x0, matrix products: 537 us -> none  [the longest x27 135 us: dense(): return jnp.dot(left, right, preferred_element_type=jnp.float32)]
    pallas_call x0 -> x15, Pallas kernels: none -> 244 us  [the longest x7 54.5 us: outer(): pl.pallas_call(functools.partial(outer_kernel, skip_left=skip_left, skip_...]
    dynamic_update_slice x88 -> x0, local copies, waits for them, and re-layouts: 55.2 us -> none  [local_states(): lax.scan(delta_stretch, start_state, (blocked(query_rows), blocked(key_ro...]
    mul x32 -> x0, other arithmetic: 54.9 us -> none  [the longest x1 21 us: conv_mix(): return jax.nn.silu(total)]
    reduce_sum x32 -> x0, other arithmetic: 51.6 us -> none  [the longest x8 13.4 us: delta_stretch(): carry_scale[:, -1][:, None, None] * state]
    another operation x24 -> x0, matrix products: 49 us -> none  [delta_stretch(): jax.scipy.linalg.solve_triangular(system, target, lower=True, unit_diagon...]
    mul x77 -> x0, local copies, waits for them, and re-layouts: 39.1 us -> none  [the longest x24 6.25 us: delta_stretch(): carry_scale = jnp.exp(cumulative) * (seg_block == seg_before)[None, :]]
  transfers between devices with their start and end apart: 25 -> 20, of which waited for: 17 -> 16; matrix products, arithmetic and copies ran while one was open for 65% -> 5% of each run, Pallas kernels for 0% -> 17%
where the time goes in v1:
time: 1190 us; the launch traced here: 1180 us
  waiting for transfers between devices  786 us (66%)
  Pallas kernels  244 us (21%)
  blocking collectives  59.8 us (5%)
  local copies, waits for them, and re-layouts  53.2 us (4%)
  other arithmetic  17.6 us (1%)
  between operations  14.9 us (1%)
    reduce_scatter x5, waiting for transfers between devices, scattered(): part_sum = lax.psum_scatter(grad, 'dp', scatter_dimension=axis, tiled=True)  267 us
    all_gather x6, waiting for transfers between devices, local(): gather = lambda a, axis: lax.all_gather(a, 'dp', axis=axis, tiled=True)  257 us
    psum x1, waiting for transfers between devices, local(): lax.psum((d_gain_mix[0], jnp.concatenate(from_heads(d_taps[:CONV]), axis=...  115 us
    psum x1, waiting for transfers between devices, scattered(): return lax.psum(part_sum, 'seq').astype(F32)  63.1 us
    pallas_call x7, Pallas kernels, outer(): pl.pallas_call(functools.partial(outer_kernel, skip_left=skip_left, skip_...  54.5 us
    pallas_call x1, Pallas kernels, delta_backward(): pl.pallas_call(backward_kernel, grid=(H,), in_specs=[pl.BlockSpec(memory_...  54.2 us
    psum x1, blocking collectives, local(): lax.psum((d_gain_mix[0], jnp.concatenate(from_heads(d_taps[:CONV]), axis=...  42.4 us
    pallas_call x1, Pallas kernels, delta_forward(): pl.pallas_call(forward_kernel, grid=(H,), in_specs=[pl.BlockSpec((rows, H...  42.3 us
  transfers between devices with their start and end apart: 20, of which 16 were waited for; matrix products, arithmetic and copies ran while one was open for 5% of the time, Pallas kernels for 17%

profile of v1, /device:TPU:8, one launch (start us, length us, event | category | flops | bytes accessed | tf_op | source)
XLA Modules:
  0.0 1181.8 jit_solution(2169899648808691973)
XLA Ops:
  7.3 1.4 convert_element_type.79
  9.8 1.1 fusion.1
  11.1 0.9 convert_element_type.86
  13.0 3.4 collective-permute-start
  20.8 2.6 stack.99.cols_ref
  23.4 1.1 pad_maximum_fusion.x_ref
  24.5 69.2 %all-gather.13.cloned.1.call-done = bf16[1024,4224]{1,0:T(8,128)(2,1)} async-done(((bf16[128,4224]{1,0:T(8,128)(2,1)}), bf16[1024,4224]{1,0:T(8,128)(2,1)}) %all-gather.13.cloned.1.call-update) | async-done | bytes 8650768 | tf_op jit(solution)/shard_map/all_gather | solution.py:880
  93.7 7.8 slice.150.w_ref.wq_ref
  101.5 1.7 slice.151.wg_ref.wl_ref
  103.2 11.5 project.1
  115.3 42.3 %delta_forward.1 = (f32[512,2048]{1,0:T(8,128)}, bf16[512,1024]{1,0:T(8,128)(2,1)}, bf16[8,128,128]{2,1,0:T(8,128)(2,1)}, bf16[8,128,256]{2,1,0:T(8,128)(2,1)}, ...) custom-call(bf16[528,4096]{1,0:T(8,128)(2,1)} %get-tuple-element.64., ...), custom_call_target="tpu_custom_call" | custom-call | flops 30000001024 | bytes 30000000 | tf_op jit(solution)/shard_map/delta_forward/pallas_call | solution.py:287
  158.3 0.9 convert_element_type.88
  159.3 0.9 convert_element_type.89
  160.8 0.9 convert_element_type.90
  162.1 6.4 outgate.1.gpre_ref
  168.5 23.2 %all-gather.17.cloned.1.call-done.w_ref = bf16[2048,1024]{1,0:T(8,128)(2,1)} async-done(((bf16[2048,128]{1,0:T(8,128)(2,1)}), bf16[2048,1024]{1,0:T(8,128)(2,1)}) %all-gather.17.cloned.1.call-update) | async-done | bytes 4194320 | tf_op jit(solution)/shard_map/all_gather | solution.py:880
  191.7 27.9 %all-gather.25.cloned.1.call-done = bf16[32,128,128]{2,1,0:T(8,128)(2,1)} async-done(((bf16[8,128,128]{2,1,0:T(8,128)(2,1)}), bf16[32,128,128]{2,1,0:T(8,128)(2,1)}) %all-gather.25.cloned.1.call-update) | async-done | bytes 1048592 | tf_op jit(solution)/shard_map/all_gather | solution.py:903
  219.6 37.6 %all-gather.27.cloned.1.call-done = bf16[32,128,256]{2,1,0:T(8,128)(2,1)} async-done(((bf16[8,128,256]{2,1,0:T(8,128)(2,1)}), bf16[32,128,256]{2,1,0:T(8,128)(2,1)}) %all-gather.27.cloned.1.call-update) | async-done | bytes 2097168 | tf_op jit(solution)/shard_map/all_gather | solution.py:904
  257.2 16.8 %mixer_out.1 = (f32[8,128,256]{2,1,0:T(8,128)}, f32[512,2048]{1,0:T(8,128)}, bf16[512,2048]{1,0:T(8,128)(2,1)}, f32[512,1024]{1,0:T(8,128)}, bf16[512,1024]{1,0:T(8,128)(2,1)}) custom-call(s32[1]{0:T(128)} %bitcast.4.place_ref, f32[512,2048]{1,0:T(8,128)} %get-tuple-element.66.part_ref, bf16[512,1024]{1,0:T(8,128)(2,1)} %get-tuple-element.67.resp_ref, ...), custom_call_target="tpu_custom_call" | custom-call | flops 2147483648 | bytes 20000000 | tf_op jit(solution)/shard_map/mixer_out/pallas_call | solution.py:583
  274.0 43.8 %all-gather.19.cloned.1.call-done.wg_ref = bf16[1024,2816]{1,0:T(8,128)(2,1)} async-done(((bf16[128,2816]{1,0:T(8,128)(2,1)}), bf16[1024,2816]{1,0:T(8,128)(2,1)}) %all-gather.19.cloned.1.call-update) | async-done | bytes 5767184 | tf_op jit(solution)/shard_map/all_gather | solution.py:880
  317.8 60.7 %all-gather.21.cloned.1.call-done.wu_ref = bf16[1024,2816]{1,0:T(8,128)(2,1)} async-done(((bf16[128,2816]{1,0:T(8,128)(2,1)}), bf16[1024,2816]{1,0:T(8,128)(2,1)}) %all-gather.21.cloned.1.call-update) | async-done | bytes 5767184 | tf_op jit(solution)/shard_map/all_gather | solution.py:880
  378.5 60.2 %all-gather.23.cloned.1.call-done.wd_ref = bf16[2816,1024]{1,0:T(8,128)(2,1)} async-done(((bf16[2816,128]{1,0:T(8,128)(2,1)}), bf16[2816,1024]{1,0:T(8,128)(2,1)}) %all-gather.23.cloned.1.call-update) | async-done | bytes 5767184 | tf_op jit(solution)/shard_map/all_gather | solution.py:880
  438.7 27.8 %feed_forward.1 = (bf16[512,1024]{1,0:T(8,128)(2,1)}, bf16[512,2816]{1,0:T(8,128)(2,1)}, bf16[512,2816]{1,0:T(8,128)(2,1)}, bf16[512,2816]{1,0:T(8,128)(2,1)}, f...) custom-call(bf16[512,1024]{1,0:T(8,128)(2,1)} %get-tuple-element.71.h_ref.left_ref, ...), custom_call_target="tpu_custom_call" | custom-call | flops 17716740096 | bytes 30000000 | tf_op jit(solution)/shard_map/feed_forward/pallas_call | solution.py:725
  466.5 12.1 %mixer_back.1 = (bf16[512,2048]{1,0:T(8,128)(2,1)}, bf16[512,2048]{1,0:T(8,128)(2,1)}, bf16[8,128,256]{2,1,0:T(8,128)(2,1)}, f32[8,256]{1,0:T(8,128)}) custom-call(bf16[512,1024]{1,0:T(8,128)(2,1)} %get-tuple-element.74.dmix_ref.right_ref, bf16[2048,1024]{1,0:T(8,128)(2,1)} %all-gather.17.cloned.1.call-done.w_ref, f32[512,2048]{1,0:T(8,128)} %get-tuple-element.75.attn_ref, ...), custom_call_target="tpu_custom_call" | custom-call | flops 2147483648 | bytes 20000000 | tf_op jit(solution)/shard_map/mixer_back/pallas_call | solution.py:647
  478.7 5.8 outer.10
  484.4 6.5 copy.81
  491.0 7.0 outer.13
  498.0 8.5 copy.83
  507.4 1.5 stack.111.back_ref
  509.0 6.3 all-gather.29.cloned.1.call-done
  515.2 54.2 %delta_backward.1 = (bf16[528,4096]{1,0:T(8,128)(2,1)}, f32[512,128]{1,0:T(8,128)}, f32[8,4096]{1,0:T(8,128)}, f32[8,128]{1,0:T(8,128)}) custom-call(s32[1]{0:T(128)} %bitcast.4.place_ref, bf16[528,4096]{1,0:T(8,128)(2,1)} %get-tuple-element.64.p_ref, f32[8,4096]{1,0:T(8,128)} %pad.15.taps_ref, f32[528,128]{1,0:T(8,128)} %get-tuple-element.65.logit_ref, ...), custom_call_target="tpu_custom_call" | custom-call | flops 40000000000 | bytes 40000000 | tf_op jit(solution)/shard_map/delta_backward/pallas_call | solution.py:493
  569.4 0.9 slice.135
  570.3 1.3 collective-permute-start.1
  571.6 5.8 collective-permute-done.1
  577.5 1.6 add_dynamic-update-slice_fusion.dp_ref.right_ref
  579.1 10.7 outer.7
  589.8 6.3 outer.8
  596.2 11.2 outer.12
  607.4 11.1 outer.11
  618.6 0.9 copy-done.14
  620.2 2.5 outer.9
  622.8 2.0 copy.82
  624.8 5.1 reduce-scatter.24.cloned.1.call-done
  629.9 2.2 copy.84
  632.1 87.9 %reduce-scatter.12.cloned.1.call-done = bf16[128,4096]{1,0:T(8,128)(2,1)} async-done(((bf16[1024,4096]{1,0:T(8,128)(2,1)}), bf16[128,4096]{1,0:T(8,128)(2,1)}) %reduce-scatter.12.cloned.1.call-update) | async-done | bytes 1048592 | tf_op jit(solution)/shard_map/reduce_scatter | solution.py:915
  720.0 2.6 copy.93
  722.6 47.1 %reduce-scatter.14.cloned.1.call-done = bf16[128,2048]{1,0:T(8,128)(2,1)} async-done(((bf16[1024,2048]{1,0:T(8,128)(2,1)}), bf16[128,2048]{1,0:T(8,128)(2,1)}) %reduce-scatter.14.cloned.1.call-update) | async-done | bytes 524304 | tf_op jit(solution)/shard_map/reduce_scatter | solution.py:915
  769.8 66.1 %reduce-scatter.20.cloned.1.call-done = bf16[128,2816]{1,0:T(8,128)(2,1)} async-done(((bf16[1024,2816]{1,0:T(8,128)(2,1)}), bf16[128,2816]{1,0:T(8,128)(2,1)}) %reduce-scatter.20.cloned.1.call-update) | async-done | bytes 720912 | tf_op jit(solution)/shard_map/reduce_scatter | solution.py:915
  835.9 65.4 %reduce-scatter.18.cloned.1.call-done = bf16[128,2816]{1,0:T(8,128)(2,1)} async-done(((bf16[1024,2816]{1,0:T(8,128)(2,1)}), bf16[128,2816]{1,0:T(8,128)(2,1)}) %reduce-scatter.18.cloned.1.call-update) | async-done | bytes 720912 | tf_op jit(solution)/shard_map/reduce_scatter | solution.py:915
  904.7 18.7 %input_grad.1 = (f32[512,1024]{1,0:T(8,128)}, f32[8,1024]{1,0:T(8,128)}) custom-call(bf16[528,4096]{1,0:T(8,128)(2,1)} %add_dynamic-update-slice_fusion.dp_ref.right_ref, bf16[512,2048]{1,0:T(8,128)(2,1)} %get-tuple-element.86.dg_ref.right_ref, bf16[512,128]{1,0:T(8,128)(2,1)} %convert_element_type.91.dl_ref.right_ref, ...), custom_call_target="tpu_custom_call" | custom-call | flops 6442450944 | bytes 30000000 | tf_op jit(solution)/shard_map/input_grad/pallas_call | solution.py:797
  924.1 42.4 %all-reduce.3 = (f32[1024]{0:T(1024)}, f32[8]{0:T(128)}, f32[8]{0:T(128)}, f32[256]{0:T(256)}, f32[1024]{0:T(1024)}) all-reduce(f32[1024]{0:T(1024)S(1)} %bitcast.132, f32[8]{0:T(128)S(1)} %get-tuple-element.202, f32[8]{0:T(128)S(1)} %get-tuple-element.201, f32[256]{0:T(256)S(1)} %bitcast.141, ...), channel_id=1, replica_groups=mesh['dp'=8,'seq'=4] {'dp','seq'}, use_global_device_ids=true, to_apply=%region_0.1 | all-reduce | flops 2320 | bytes 18560 | tf_op jit(solution)/shard_map/psum | solution.py:934
  966.5 17.4 %psum.94 = bf16[128,128]{1,0:T(8,128)(2,1)S(1)} all-reduce(bf16[128,128]{1,0:T(8,128)(2,1)} %reduce-scatter.16.cloned.1.call-done), channel_id=1, replica_groups=mesh['dp'=8,'seq'=4] {'seq'}, use_global_device_ids=true, to_apply=%region_6.7 | all-reduce | flops 16384 | bytes 65536 | tf_op jit(solution)/shard_map/psum | solution.py:916
  984.6 63.1 %all-reduce.10.cloned.1.call-done = (bf16[128,8,512]{2,1,0:T(8,128)(2,1)}, bf16[128,2048]{1,0:T(8,128)(2,1)}, bf16[2048,128]{1,0:T(8,128)(2,1)}, bf16[128,2816]{...) async-done(((bf16[128,8,512]{2,1,0:T(8,128)(2,1)}, bf16[128,2048]{1,0:T(8,128)(2,1)}, bf16[2048,128]{1,0:T(8,128)(2,1)}, ...) | async-done | bytes 4259856 | tf_op jit(solution)/shard_map/psum | solution.py:916
  1047.7 1.2 fusion.10
  1049.2 1.3 copy.96
  1050.5 0.9 copy.109
  1051.4 0.9 copy.110
  1052.3 1.2 convert_element_type.94
  1053.5 1.2 convert_element_type.95
  1054.7 1.2 convert_element_type.96
  1055.9 1.1 convert_element_type.92
  1057.0 1.0 convert_element_type.93
  1058.0 115.5 %all-reduce.8.cloned.1.call-done = f32[4,4096]{1,0:T(4,128)} async-done(((f32[4,4096]{1,0:T(4,128)}), f32[4,4096]{1,0:T(4,128)}) %all-reduce.8.cloned.1.call-update) | async-done | bytes 65552 | tf_op jit(solution)/shard_map/psum | solution.py:934
  1173.5 1.5 copy.123
  (147 shorter events, 15.7 us)
Async XLA Ops:
  7.2 1.6 copy-start.12
  7.2 1.7 copy-start.13
  7.2 86.5 %all-gather.13.cloned.1.call-start = ((), (), s32[]{:S(2)}) async-start(), calls=%async_computation.7 | async-start | bytes 9732096 | tf_op jit(solution)/shard_map/all_gather | solution.py:880
  9.0 0.7 copy-start.17
  9.7 1.4 copy-start.5
  9.8 2.2 copy-start.6
  10.9 2.1 copy-start
  10.9 5.5 copy-start.18
  10.9 5.7 slice-start
  10.9 6.0 copy-start.15
  10.9 6.1 copy-start.19
  10.9 6.1 copy-start.20
  11.0 151.1 %all-gather.15.cloned.1.call-start = ((), (), s32[]{:S(2)}) async-start(), calls=%async_computation.8 | async-start | bytes 4718592 | tf_op jit(solution)/shard_map/all_gather | solution.py:880
  12.0 179.8 %all-gather.17.cloned.1.call-start = ((), (), s32[]{:S(2)}) async-start(), calls=%async_computation.9 | async-start | bytes 4718592 | tf_op jit(solution)/shard_map/all_gather | solution.py:880
  12.9 206.7 %all-gather.25.cloned.1.call-start = ((), (), s32[]{:S(2)}) async-start(), calls=%async_computation.19 | async-start | bytes 1310720 | tf_op jit(solution)/shard_map/all_gather | solution.py:903
  13.0 10.5 collective-permute-start
  115.3 43.0 %copy-start.2 = (f32[128,2816]{1,0:T(8,128)S(1)}, f32[128,2816]{1,0:T(8,128)}, u32[]{:S(2)}) copy-start(f32[128,2816]{1,0:T(8,128)} %param.35) | copy-start | bytes 4325380
  157.6 1.7 copy-start.3
  157.6 99.6 %all-gather.27.cloned.1.call-start = ((), (), s32[]{:S(2)}) async-start(), calls=%async_computation.20 | async-start | bytes 2621440 | tf_op jit(solution)/shard_map/all_gather | solution.py:904
  158.2 159.6 %all-gather.19.cloned.1.call-start = ((), (), s32[]{:S(2)}) async-start(), calls=%async_computation.10 | async-start | bytes 6488064 | tf_op jit(solution)/shard_map/all_gather | solution.py:880
  159.2 1.6 copy-start.4
  159.2 219.3 %all-gather.21.cloned.1.call-start = ((), (), s32[]{:S(2)}) async-start(), calls=%async_computation.11 | async-start | bytes 6488064 | tf_op jit(solution)/shard_map/all_gather | solution.py:880
  160.3 278.4 %all-gather.23.cloned.1.call-start = ((), (), s32[]{:S(2)}) async-start(), calls=%async_computation.12 | async-start | bytes 6488064 | tf_op jit(solution)/shard_map/all_gather | solution.py:880
  161.8 353.4 %all-gather.29.cloned.1.call-start = ((), (), s32[]{:S(2)}) async-start(), calls=%async_computation.21 | async-start | bytes 2621440 | tf_op jit(solution)/shard_map/all_gather | solution.py:912
  478.6 144.1 %reduce-scatter.22.cloned.1.call-start = ((), (), s32[]{:S(2)}) async-start(), calls=%async_computation.22 | async-start | bytes 4718592
  490.9 138.9 %reduce-scatter.24.cloned.1.call-start = ((), (), s32[]{:S(2)}) async-start(), calls=%async_computation.23 | async-start | bytes 6488064
  506.5 213.5 %reduce-scatter.12.cloned.1.call-start = ((), (), s32[]{:S(2)}) async-start(), calls=%async_computation.13 | async-start | bytes 9437184 | tf_op jit(solution)/shard_map/reduce_scatter | solution.py:915
  570.3 7.1 collective-permute-start.1
  589.8 180.0 %reduce-scatter.14.cloned.1.call-start = ((), (), s32[]{:S(2)}) async-start(), calls=%async_computation.14 | async-start | bytes 4718592 | tf_op jit(solution)/shard_map/reduce_scatter | solution.py:915
  596.1 239.8 %reduce-scatter.20.cloned.1.call-start = ((), (), s32[]{:S(2)}) async-start(), calls=%async_computation.18 | async-start | bytes 6488064 | tf_op jit(solution)/shard_map/reduce_scatter | solution.py:915
  607.4 294.0 %reduce-scatter.18.cloned.1.call-start = ((), (), s32[]{:S(2)}) async-start(), calls=%async_computation.17 | async-start | bytes 6488064 | tf_op jit(solution)/shard_map/reduce_scatter | solution.py:915
  618.6 0.9 copy-start.14
  618.6 347.9 %reduce-scatter.16.cloned.1.call-start = ((), (), s32[]{:S(2)}) async-start(), calls=%async_computation.15 | async-start | bytes 294912 | tf_op jit(solution)/shard_map/reduce_scatter | solution.py:915
  622.7 425.1 %all-reduce.10.cloned.1.call-start = ((), (), s32[]{:S(2)}) async-start(), calls=%async_computation.24 | async-start | bytes 8519680 | tf_op jit(solution)/shard_map/psum | solution.py:916
  722.6 180.5 %copy-start.16 = (f32[8,4096]{1,0:T(8,128)S(1)}, f32[8,4096]{1,0:T(8,128)}, u32[]{:S(2)}) copy-start(f32[8,4096]{1,0:T(8,128)} %get-tuple-element.91) | copy-start | bytes 393220
  901.3 272.1 %all-reduce.8.cloned.1.call-start = ((), (), s32[]{:S(2)}) async-start(), calls=%async_computation.16 | async-start | bytes 131072 | tf_op jit(solution)/shard_map/psum | solution.py:934
  1047.7 1.4 copy-start.1
  1049.2 3.1 copy-start.9
  1050.5 3.0 copy-start.8
  1052.3 2.4 copy-start.7
  1053.5 2.4 copy-start.11
  1054.7 2.3 copy-start.10
Sparse Core Ops, SparseCore 0:
  11.0 82.6 all-gather.12
  95.9 46.8 all-gather.14
  144.9 46.7 all-gather.16
  193.4 26.1 all-gather.24
  221.9 35.2 all-gather.26
  259.3 58.4 all-gather.18
  319.4 59.0 all-gather.20
  380.1 58.5 all-gather.22
  478.7 36.4 all-gather.28
  517.4 46.1 reduce-scatter.21
  565.9 63.9 reduce-scatter.23
  632.0 87.9 reduce-scatter.11
  722.3 47.3 reduce-scatter.13
  771.9 63.9 reduce-scatter.19
  838.1 63.2 reduce-scatter.17
  904.0 28.0 reduce-scatter.15
  938.0 109.6 all-reduce.9
  1054.7 118.7 all-reduce.7

commit v2 on v1

--- a/solution.py
+++ b/solution.py
@@ -15,6 +15,12 @@
 CHUNK = 128
 HC = 2 * DK + DV
 LANES = 128
+PLANES, CORES, SPOTS = 4, 2, 4
+
+AT_LOGIT = H * HC
+AT_GATE = AT_LOGIT + 512
+AT_OUT = AT_GATE + H * DV
+AT_FFN = AT_OUT + H * DV
 VMEM_LIMIT = 56 * 2**20
 
 F32 = jnp.float32
@@ -76,90 +82,72 @@
     return jnp.sum(jnp.where(same, row, 0.0), axis=1, keepdims=True)
 
 
-def project_kernel(x_ref, gain_ref, w_ref, wg_ref, p_ref, logit_ref, h_ref):
-    @pl.when(pl.program_id(0) == 0)
-    def _():
-        value = x_ref[...].astype(F32)
-        scale = lax.rsqrt(jnp.mean(value * value, axis=-1, keepdims=True) + 1e-06)
-        h_ref[...] = (value * scale * gain_ref[...]).astype(BF16)
-        logit_ref[...] = mm(h_ref[...], wg_ref[...])
-
-    p_ref[...] = mm(h_ref[...], w_ref[...]).astype(BF16)
-
-
-def project(x_ext, gain, w_qkv, w_gates):
-    rows, width = x_ext.shape
-    block = 512
-    cols = w_qkv.shape[1]
-    return pl.pallas_call(
-        project_kernel,
-        grid=(cols // block,),
-        in_specs=[
-            pl.BlockSpec((rows, width), lambda j: (0, 0)),
-            pl.BlockSpec((1, width), lambda j: (0, 0)),
-            pl.BlockSpec((width, block), lambda j: (0, j)),
-            pl.BlockSpec((width, LANES), lambda j: (0, 0)),
-        ],
-        out_specs=[
-            pl.BlockSpec((rows, block), lambda j: (0, j)),
-            pl.BlockSpec((rows, LANES), lambda j: (0, 0)),
-            pl.BlockSpec((rows, width), lambda j: (0, 0)),
-        ],
-        out_shape=[
-            jax.ShapeDtypeStruct((rows, cols), BF16),
-            jax.ShapeDtypeStruct((rows, LANES), F32),
-            jax.ShapeDtypeStruct((rows, width), BF16),
-        ],
-        compiler_params=params(),
-        cost_estimate=cost(2 * rows * width * cols, 2 * width * cols + 2 * rows * cols),
-        name="project",
-    )(x_ext, gain, w_qkv, w_gates)
-
-
 def outgate_kernel(h_ref, w_ref, g_ref):
     g_ref[...] = mm(h_ref[HALO:, :], w_ref[...])
 
 
-def outgate(hidden, w_og):
+def outgate(hidden, weights):
     rows, width = hidden.shape
-    cols = w_og.shape[1]
+    cols = H * DV
     block = 512
     return pl.pallas_call(
         outgate_kernel,
         grid=(cols // block,),
         in_specs=[
             pl.BlockSpec((rows, width), lambda j: (0, 0)),
-            pl.BlockSpec((width, block), lambda j: (0, j)),
+            pl.BlockSpec((width, block), lambda j: (0, j + AT_GATE // block)),
         ],
         out_specs=pl.BlockSpec((rows - HALO, block), lambda j: (0, j)),
         out_shape=jax.ShapeDtypeStruct((rows - HALO, cols), F32),
         compiler_params=params(),
         cost_estimate=cost(2 * rows * width * cols, 2 * width * cols + 4 * rows * cols),
         name="outgate",
-    )(hidden, w_og)
-
-
-def outer_kernel(left_ref, right_ref, out_ref, *, skip_left, skip_right):
-    out_ref[...] = mm(left_ref[skip_left:, :], right_ref[skip_right:, :], TN).astype(BF16)
-
-
-def outer(left, right, block=512, skip_left=0, skip_right=0):
-    rows, width = left.shape
-    cols = right.shape[1]
-    block = min(block, cols)
+    )(hidden, weights)
+
+
+def outer_kernel(*refs, skips, parts):
+    pairs = len(skips)
+    lefts, rights = refs[:pairs], refs[pairs : 2 * pairs]
+    outs, turned = refs[2 * pairs : -pairs], refs[-pairs:]
+
+    @pl.when(pl.program_id(0) == 0)
+    def _():
+        for left, scratch, (skip, _) in zip(lefts, turned, skips):
+            scratch[...] = jnp.transpose(left[skip:, :])
+
+    total = None
+    for scratch, right, (_, skip) in zip(turned, rights, skips):
+        term = mm(scratch[...], right[skip:, :])
+        total = term if total is None else total + term
+    total = total.astype(BF16)
+    for out, blocks in zip(outs, parts):
+        for slot, block in enumerate(blocks):
+            out[slot * LANES : (slot + 1) * LANES, :] = total[block * LANES : (block + 1) * LANES]
+
+
+def outer(lefts, rights, wide_rows, parts, skip_left=0, skip_right=0):
+    cols = rights[0].shape[1]
+    block = next(b for b in (512, 256, 128) if cols % b == 0)
+    if cols == 1152:
+        block = 384
+    rows = [array.shape[0] for array, _ in lefts]
+    kept = rows[0] - skip_left
     return pl.pallas_call(
-        functools.partial(outer_kernel, skip_left=skip_left, skip_right=skip_right),
+        functools.partial(outer_kernel, skips=[(skip_left, skip_right)] * len(lefts), parts=parts),
         grid=(cols // block,),
         in_specs=[
-            pl.BlockSpec((rows, width), lambda j: (0, 0)),
-            pl.BlockSpec((right.shape[0], block), lambda j: (0, j)),
-        ],
-        out_specs=pl.BlockSpec((width, block), lambda j: (0, j)),
-        out_shape=jax.ShapeDtypeStruct((width, cols), BF16),
+            pl.BlockSpec((n, wide_rows), lambda j, at=at: (0, at)) for n, (_, at) in zip(rows, lefts)
+        ]
+        + [pl.BlockSpec((right.shape[0], block), lambda j: (0, j)) for right in rights],
+        out_specs=[pl.BlockSpec((LANES * len(p), block), lambda j: (0, j)) for p in parts],
+        out_shape=[jax.ShapeDtypeStruct((LANES * len(p), cols), BF16) for p in parts],
+        scratch_shapes=[pltpu.VMEM((wide_rows, kept), BF16) for _ in lefts],
         compiler_params=params(),
-        cost_estimate=cost(2 * rows * width * cols, 2 * width * cols + 2 * rows * cols),
+        cost_estimate=cost(
+            2 * len(lefts) * kept * wide_rows * cols, 2 * (wide_rows + sum(rows)) * cols
+        ),
         name="outer",
-    )(left, right)
+    )(*[array for array, _ in lefts], *rights)
 
 
 def gate_tables(logit_ref, par_ref, beta_ref, decay_ref, cum_ref):
@@ -212,21 +200,208 @@
     return found
 
 
-def forward_kernel(
-    p_ref, taps_ref, logit_ref, par_ref, cols_ref, segr_ref,
-    part_ref, resp_ref, map_ref, sum_ref, inv_ref, upd_ref, st_ref, stm_ref, amap_ref, rmap_ref,
-    beta_ref, decay_ref, cum_ref, pf_ref, mix_ref,
-):
+def device(planes=0, core=0, spot=0):
+    place, here = lax.axis_index("dp"), lax.axis_index("seq")
+    z = lax.rem(place // CORES + planes, PLANES)
+    flip = lambda value, bits: value + sum(
+        bit * (1 - 2 * lax.rem(value // bit, 2)) for bit in (1, 2) if bits & bit
+    )
+    return {"dp": z * CORES + flip(lax.rem(place, CORES), core), "seq": flip(here, spot)}
+
+
+def greet(partners):
+    barrier = pltpu.get_barrier_semaphore()
+    for partner in partners:
+        pl.semaphore_signal(barrier, inc=1, device_id=device(**partner), device_id_type=pl.DeviceIdType.MESH)
+    pl.semaphore_wait(barrier, len(partners))
+
+
+def gather_spans(inner):
+    spans = [((H - 1) * HC, HC + LANES), ((H - 2) * HC, HC)]
+    spans += [(h * HC, 2 * HC) for h in (4, 2, 0)]
+    for at, size in ((AT_GATE, H * DV), (AT_OUT, H * DV)) + tuple((AT_FFN + i * inner, inner) for i in range(3)):
+        spans += [(at + low, min(1024, size - low)) for low in range(0, size, 1024)]
+    return spans
+
+
+class Gathering:
+    STAGES = (0, 1, 2, 3, 5, 7, 8)
+    FIRST = ((0, 1, 2, 3, 4, 5, 6), (0, 1, 2, 3, 4, 6, 7))
+
+    def __init__(self, spans, shard_ref, full_ref, sems):
+        self.spans, self.shard, self.full = spans, shard_ref, full_ref
+        self.send_sem, self.recv_sem, self.local_sem = sems
+        self.piece = shard_ref.shape[0] // SPOTS
+        self.half = full_ref.shape[0] // CORES
+        self.z = lax.axis_index("dp") // CORES
+
+    def own(self):
+        piece = self.piece
+        return [
+            pltpu.make_async_copy(
+                self.shard.at[q * piece : (q + 1) * piece],
+                self.full.at[q * PLANES * piece : (q * PLANES + 1) * piece],
+                self.local_sem.at[q],
+            )
+            for q in range(SPOTS)
+        ]
+
+    def copy(self, group, kind):
+        at, size = self.spans[group]
+        cols = pl.ds(at, size)
+        piece, full = self.piece, self.full
+        block = PLANES * piece
+        rows = lambda quarter: pl.ds(quarter * block + piece, block - piece)
+        if kind < 6:
+            read, step, written = ((0, 1, 1), (0, -1, 3), (1, 1, 2), (3, -1, 2), (2, 1, 3), (2, -1, 1))[kind]
+            source = self.shard.at[0:piece, cols] if read == 0 else full.at[read * piece : (read + 1) * piece, cols]
+            target = full.at[written * piece : (written + 1) * piece, cols]
+            to, arrival = device(planes=step % PLANES), written - 1
+        elif kind < 8:
+            source = full.at[rows(0), cols]
+            target = full.at[rows(kind - 5), cols]
+            to, arrival = device(spot=kind - 5), kind - 3
+        elif kind == 8:
+            by = 1 + group % 2
+            source = full.at[rows(by), cols]
+            target = full.at[rows(3), cols]
+            to, arrival = device(spot=3 - by), 5
+        else:
+            source = full.at[0 : self.half, cols]
+            target = full.at[self.half : 2 * self.half, cols]
+            to, arrival = device(core=1), 6
+        return pltpu.make_async_remote_copy(
+            src_ref=source,
+            dst_ref=target,
+            send_sem=self.send_sem.at[group, kind],
+            recv_sem=self.recv_sem.at[group, arrival],
+            device_id=to,
+            device_id_type=pl.DeviceIdType.MESH,
+        )
+
+    def sends(self, kind):
+        z = self.z
+        return (z < 3, z > 0, (z > 0) & (z < 3), (z > 0) & (z < 3), z == 2, z == 1)[kind]
+
+    def start(self, group, kind):
+        @pl.when(self.sends(kind))
+        def _():
+            self.copy(group, kind).start()
+
+    def arrive(self, group, kind, condition):
+        @pl.when(condition)
+        def _():
+            self.copy(group, kind).wait_recv()
+
+    def tick(self, at):
+        z = self.z
+        due = []
+        for group in range(len(self.spans)):
+            stages = (self.FIRST + (self.STAGES,) * len(self.spans))[group]
+            due += [(stage, group) for stage in range(len(stages)) if group + stages[stage] == at]
+        for stage, group in sorted(due, reverse=True):
+            by = 1 + group % 2
+            if stage == 0:
+                self.start(group, 0)
+                self.start(group, 1)
+            elif stage == 1:
+                self.arrive(group, 0, z > 0)
+                self.start(group, 2)
+                self.arrive(group, 1, z < 3)
+                self.start(group, 3)
+            elif stage == 2:
+                self.copy(group, 2).wait_recv()
+                self.start(group, 4)
+                self.start(group, 5)
+            elif stage == 3:
+                self.arrive(group, 0, z == 0)
+                self.arrive(group, 1, z == 3)
+                self.copy(group, 5 + by).start()
+                self.copy(group, 8 - by).start()
+            elif stage == 4:
+                self.copy(group, 5 + by).wait_recv()
+                self.copy(group, 8).start()
+            elif stage == 5:
+                self.copy(group, 8 - by).wait_recv()
+                self.copy(group, 8).wait_recv()
+                if group == 0:
+                    for local in self.own():
+                        local.wait()
+                self.copy(group, 9).start()
+            else:
+                self.copy(group, 9).wait_recv()
+
+    def finish(self):
+        for group in range(len(self.spans)):
+            for kind in range(6):
+
+                @pl.when(self.sends(kind))
+                def _(group=group, kind=kind):
+                    self.copy(group, kind).wait_send()
+
+            for kind in range(6, 10):
+                self.copy(group, kind).wait_send()
+
+
+def forward_kernel(*refs, planned, spans):
+    h_ref, shard_ref, taps_ref, par_ref, cols_ref, segr_ref = refs[:6]
+    refs = refs[6:]
+    full_ref = shard_ref
+    if planned:
+        full_ref, refs = refs[0], refs[1:]
+    (
+        p_ref, logit_ref, part_ref, resp_ref, exch_ref, inv_ref, upd_ref, st_ref, stm_ref, amap_ref, rmap_ref,
+        beta_ref, decay_ref, cum_ref, pf_ref, mix_ref, w_ref, wl_ref, load_sem,
+    ) = refs[:19]
     head = pl.program_id(0)
+
+    def load(slot, at, size, to):
+        return pltpu.make_async_copy(full_ref.at[:, pl.ds(at, size)], to, load_sem.at[slot])
+
+    if planned:
+        stage_ref, send_sem, recv_sem, local_sem, exch_send, exch_recv, exch_local = refs[19:]
+        gathering = Gathering(spans, shard_ref, full_ref, (send_sem, recv_sem, local_sem))
+        lead = gathering.FIRST[0][-1] + 1
+        final_tick = len(spans) + gathering.STAGES[-1]
+
+        @pl.when(head == 0)
+        def _():
+            greet([dict(planes=d) for d in (1, 2, 3)] + [dict(spot=s) for s in (1, 2, 3)] + [dict(core=1)])
+            for local in gathering.own():
+                local.start()
+            for at in range(lead):
+                gathering.tick(at)
+
+        for h in range(1, H):
+
+            @pl.when(head == h)
+            def _(h=h):
+                gathering.tick(lead + 2 * h - 1)
+
+    mine = load(0, pl.multiple_of((H - 1 - head) * HC, HC), HC, w_ref)
+    mine.start()
 
     @pl.when(head == 0)
     def _():
+        gates = load(1, AT_LOGIT, LANES, wl_ref)
+        gates.start()
+        gates.wait()
+        logit_ref[...] = mm(h_ref[...], wl_ref[...])
         gate_tables(logit_ref, par_ref, beta_ref, decay_ref, cum_ref)
 
+    mine.wait()
+    p_ref[...] = mm(h_ref[...], w_ref[...]).astype(BF16)
     cols = cols_ref[...]
     tokens = cols.shape[0]
     total = mix_taps(p_ref, taps_ref, cols, pf_ref)
     mix_ref[...] = total * jax.nn.sigmoid(total)
+    if planned:
+        for h in range(H):
+
+            @pl.when(head == h)
+            def _(h=h):
+                gathering.tick(lead + 2 * h)
+
     beta = lane(beta_ref[...], head + H)
     chunks = range(tokens // CHUNK)
     tables, lows, keys, queries = [], [], [], []
@@ -274,76 +449,129 @@
             state = moved[:DK] + jnp.concatenate(
                 [both[:DK, :DV], jnp.zeros((DK, DK), F32)], axis=1
             )
-    map_ref[0] = state[:, DV:].astype(BF16)
-    sum_ref[0] = state[:, :DV].astype(BF16)
-
-
-def delta_forward(proj, taps, logits, par, cols, segr):
-    rows = proj.shape[0]
+    if not planned:
+        exch_ref[0, 0] = state.astype(BF16)
+        return
+    stage_ref[head] = state.astype(BF16)
+
+    def keep(h):
+        return pltpu.make_async_copy(stage_ref.at[h], exch_ref.at[0, h], exch_local.at[h])
+
+    def give(h, spot):
+        return pltpu.make_async_remote_copy(
+            src_ref=stage_ref.at[h],
+            dst_ref=exch_ref.at[spot, h],
+            send_sem=exch_send.at[spot - 1, h],
+            recv_sem=exch_recv.at[spot - 1, h],
+            device_id=device(spot=spot),
+            device_id_type=pl.DeviceIdType.MESH,
+        )
+
+    keep(head).start()
+    for spot in range(1, SPOTS):
+        give(head, spot).start()
+
+    @pl.when(head == H - 1)
+    def _():
+        for at in range(lead + 2 * H - 1, final_tick):
+            gathering.tick(at)
+        gathering.finish()
+        for h in range(H):
+            keep(h).wait()
+            for spot in range(1, SPOTS):
+                give(h, spot).wait()
+
+
+def delta_forward(hidden, weights, taps, par, cols, segr, planned, inner):
+    rows, width = hidden.shape
     tokens = rows - HALO
     chunks = tokens // CHUNK
     whole = lambda shape: pl.BlockSpec(shape, lambda h: (0,) * len(shape))
     by_head = lambda shape: pl.BlockSpec(shape, lambda h: (h,) + (0,) * (len(shape) - 1))
+    anywhere = pl.BlockSpec(memory_space=pl.ANY)
+    spans = gather_spans(inner)
+    out_specs = [
+        pl.BlockSpec((rows, HC), lambda h: (0, h)),
+        whole((rows, LANES)),
+        pl.BlockSpec((tokens, DV), lambda h: (0, h)),
+        pl.BlockSpec((tokens, DK), lambda h: (0, h)),
+        anywhere if planned else pl.BlockSpec((1, 1, DK, DV + DK), lambda h: (0, h, 0, 0)),
+        by_head((1, chunks, CHUNK, CHUNK)),
+        by_head((1, tokens, DV + DK)),
+        by_head((1, chunks, DK, DV)),
+        by_head((1, chunks, DK, DK)),
+        by_head((1, chunks, DK, DK)),
+        by_head((1, chunks, CHUNK, DK)),
+    ]
+    out_shape = [
+        jax.ShapeDtypeStruct((rows, H * HC), BF16),
+        jax.ShapeDtypeStruct((rows, LANES), F32),
+        jax.ShapeDtypeStruct((tokens, H * DV), F32),
+        jax.ShapeDtypeStruct((tokens, H * DK), BF16),
+        jax.ShapeDtypeStruct((SPOTS if planned else 1, H, DK, DV + DK), BF16),
+        jax.ShapeDtypeStruct((H, chunks, CHUNK, CHUNK), BF16),
+        jax.ShapeDtypeStruct((H, tokens, DV + DK), F32),
+        jax.ShapeDtypeStruct((H, chunks, DK, DV), F32),
+        jax.ShapeDtypeStruct((H, chunks, DK, DK), BF16),
+        jax.ShapeDtypeStruct((H, chunks, DK, DK), BF16),
+        jax.ShapeDtypeStruct((H, chunks, CHUNK, DK), BF16),
+    ]
+    scratch = [
+        pltpu.VMEM((tokens, LANES), F32),
+        pltpu.VMEM((tokens, LANES), F32),
+        pltpu.VMEM((tokens, LANES), F32),
+        pltpu.VMEM((rows, HC), F32),
+        pltpu.VMEM((tokens, HC), F32),
+        pltpu.VMEM((width, HC), BF16),
+        pltpu.VMEM((width, LANES), BF16),
+        pltpu.SemaphoreType.DMA((2,)),
+    ]
+    more = {}
+    if planned:
+        out_specs = [anywhere] + out_specs
+        out_shape = [jax.ShapeDtypeStruct((width, weights.shape[1]), BF16)] + out_shape
+        scratch += [
+            pltpu.VMEM((H, DK, DV + DK), BF16),
+            pltpu.SemaphoreType.DMA((len(spans), 10)),
+            pltpu.SemaphoreType.DMA((len(spans), 7)),
+            pltpu.SemaphoreType.DMA((SPOTS,)),
+            pltpu.SemaphoreType.DMA((SPOTS - 1, H)),
+            pltpu.SemaphoreType.DMA((SPOTS - 1, H)),
+            pltpu.SemaphoreType.DMA((H,)),
+        ]
+        more = dict(collective_id=0, has_side_effects=True)
     return pl.pallas_call(
-        forward_kernel,
+        functools.partial(forward_kernel, planned=planned, spans=spans),
         grid=(H,),
         in_specs=[
-            pl.BlockSpec((rows, HC), lambda h: (0, h)),
+            whole((rows, width)),
+            pl.BlockSpec(memory_space=pltpu.VMEM) if planned else anywhere,
             pl.BlockSpec((8, HC), lambda h: (0, h)),
-            whole((rows, LANES)),
             whole((8, LANES)),
             whole((tokens, LANES)),
             whole((8, tokens)),
         ],
-        out_specs=[
-            pl.BlockSpec((tokens, DV), lambda h: (0, h)),
-            pl.BlockSpec((tokens, DK), lambda h: (0, h)),
-            by_head((1, DK, DK)),
-            by_head((1, DK, DV)),
-            by_head((1, chunks, CHUNK, CHUNK)),
-            by_head((1, tokens, DV + DK)),
-            by_head((1, chunks, DK, DV)),
-            by_head((1, chunks, DK, DK)),
-            by_head((1, chunks, DK, DK)),
-            by_head((1, chunks, CHUNK, DK)),
-        ],
-        out_shape=[
-            jax.ShapeDtypeStruct((tokens, H * DV), F32),
-            jax.ShapeDtypeStruct((tokens, H * DK), BF16),
-            jax.ShapeDtypeStruct((H, DK, DK), BF16),
-            jax.ShapeDtypeStruct((H, DK, DV), BF16),
-            jax.ShapeDtypeStruct((H, chunks, CHUNK, CHUNK), BF16),
-            jax.ShapeDtypeStruct((H, tokens, DV + DK), F32),
-            jax.ShapeDtypeStruct((H, chunks, DK, DV), F32),
-            jax.ShapeDtypeStruct((H, chunks, DK, DK), BF16),
-            jax.ShapeDtypeStruct((H, chunks, DK, DK), BF16),
-            jax.ShapeDtypeStruct((H, chunks, CHUNK, DK), BF16),
-        ],
-        scratch_shapes=[
-            pltpu.VMEM((tokens, LANES), F32),
-            pltpu.VMEM((tokens, LANES), F32),
-            pltpu.VMEM((tokens, LANES), F32),
-            pltpu.VMEM((rows, HC), F32),
-            pltpu.VMEM((tokens, HC), F32),
-        ],
-        compiler_params=params(),
-        cost_estimate=cost(3e10, 3e7),
+        out_specs=out_specs,
+        out_shape=out_shape,
+        scratch_shapes=scratch,
+        compiler_params=params(**more),
+        cost_estimate=cost(6e9 * H, 5e6 * H),
         name="delta_forward",
-    )(proj, taps, logits, par, cols, segr)
+    )(hidden, weights, taps, par, cols, segr)
 
 
 def backward_kernel(
-    place_ref, p_ref, taps_ref, logit_ref, par_ref, cols_ref, back_ref, segr_ref,
-    dattn_ref, sin_ref, maps_ref, grads_ref,
+    place_ref, slot_ref, p_ref, taps_ref, logit_ref, par_ref, cols_ref, back_ref, segr_ref,
+    dattn_ref, sin_ref, exch_ref, grads_ref,
     inv_ref, upd_ref, st_ref, stm_ref, amap_ref, rmap_ref,
     dp_ref, dlogit_ref, dtaps_ref, dpar_ref,
-    beta_ref, decay_ref, cum_ref, pf_ref, pre_ref, dmix_ref,
+    beta_ref, decay_ref, cum_ref, pf_ref, pre_ref, dmix_ref, *, first
 ):
-    head = pl.program_id(0)
+    head = pl.program_id(0) + first
     place = place_ref[0]
-    places = maps_ref.shape[0]
-
-    @pl.when(head == 0)
+    places = exch_ref.shape[0]
+
+    @pl.when(pl.program_id(0) == 0)
     def _():
         gate_tables(logit_ref, par_ref, beta_ref, decay_ref, cum_ref)
         dlogit_ref[...] = jnp.zeros_like(dlogit_ref)
@@ -358,9 +586,10 @@
 
     def behind(lap, grad):
         source = places - 1 - lap
+        slot = slot_ref[source]
         return jnp.where(
             source > place,
-            grads_ref[source, 0].astype(F32) + mm(maps_ref[source, 0], grad, TN),
+            grads_ref[slot, 0].astype(F32) + mm(exch_ref[slot, 0], grad, TN),
             grad,
         )
 
@@ -483,29 +712,32 @@
     dp_ref[...] = total.astype(BF16)
 
 
-def delta_backward(place, proj, taps, logits, par, cols, back, segr, d_attn, state_in, maps, grads, saved):
+def delta_backward(
+    first, heads, place, slots, proj, taps, logits, par, cols, back, segr, d_attn, state_in, exch, grads, saved
+):
     rows = proj.shape[0]
     tokens = rows - HALO
     chunks = tokens // CHUNK
-    places = maps.shape[0]
+    places = exch.shape[0]
     whole = lambda shape: pl.BlockSpec(shape, lambda h: (0,) * len(shape))
-    by_head = lambda shape: pl.BlockSpec(shape, lambda h: (h,) + (0,) * (len(shape) - 1))
+    by_head = lambda shape: pl.BlockSpec(shape, lambda h: (h + first,) + (0,) * (len(shape) - 1))
     return pl.pallas_call(
-        backward_kernel,
-        grid=(H,),
+        functools.partial(backward_kernel, first=first),
+        grid=(heads,),
         in_specs=[
             pl.BlockSpec(memory_space=pltpu.SMEM),
-            pl.BlockSpec((rows, HC), lambda h: (0, h)),
-            pl.BlockSpec((8, HC), lambda h: (0, h)),
+            pl.BlockSpec(memory_space=pltpu.SMEM),
+            pl.BlockSpec((rows, HC), lambda h: (0, h + first)),
+            pl.BlockSpec((8, HC), lambda h: (0, h + first)),
             whole((rows, LANES)),
             whole((8, LANES)),
             whole((tokens, LANES)),
             whole((rows, LANES)),
             whole((8, tokens)),
-            pl.BlockSpec((tokens, DV), lambda h: (0, h)),
+            pl.BlockSpec((tokens, DV), lambda h: (0, h + first)),
             by_head((1, DK, DV)),
-            pl.BlockSpec((places, 1, DK, DK), lambda h: (0, h, 0, 0)),
-            pl.BlockSpec((places, 1, DK, DV), lambda h: (0, h, 0, 0)),
+            pl.BlockSpec((places, 1, DK, DK), lambda h: (0, h + first, 0, DV // DK)),
+            pl.BlockSpec((places, 1, DK, DV), lambda h: (0, h + first, 0, 0)),
             by_head((1, chunks, CHUNK, CHUNK)),
             by_head((1, tokens, DV + DK)),
             by_head((1, chunks, DK, DV)),
@@ -520,9 +752,9 @@
             whole((8, LANES)),
         ],
         out_shape=[
-            jax.ShapeDtypeStruct((rows, H * HC), BF16),
+            jax.ShapeDtypeStruct((rows, heads * HC), BF16),
             jax.ShapeDtypeStruct((tokens, LANES), F32),
-            jax.ShapeDtypeStruct((8, H * HC), F32),
+            jax.ShapeDtypeStruct((8, heads * HC), F32),
             jax.ShapeDtypeStruct((8, LANES), F32),
         ],
         scratch_shapes=[
@@ -534,23 +766,24 @@
             pltpu.VMEM((rows + 8, HC), F32),
         ],
         compiler_params=params(),
-        cost_estimate=cost(4e10, 4e7),
+        cost_estimate=cost(8e9 * heads, 5e6 * heads),
         name="delta_backward",
-    )(place, proj, taps, logits, par, cols, back, segr, d_attn, state_in, maps, grads, *saved)
+    )(place, slots, proj, taps, logits, par, cols, back, segr, d_attn, state_in, exch, grads, *saved)
 
 
 def mixer_kernel(
-    place_ref, part_ref, resp_ref, maps_ref, sums_ref, gpre_ref, gain_ref, w_ref, x_ref, gain2_ref,
+    place_ref, slot_ref, part_ref, resp_ref, exch_ref, gpre_ref, gain_ref, w_ref, x_ref, gain2_ref,
     sin_ref, attn_ref, gated_ref, y_ref, h_ref,
 ):
     head = pl.program_id(0)
     place = place_ref[0]
-    places = maps_ref.shape[0]
+    places = exch_ref.shape[0]
 
     def ahead(source, state):
+        slot = slot_ref[source]
         return jnp.where(
             source < place,
-            sums_ref[source, 0].astype(F32) + mm(maps_ref[source, 0], state),
+            exch_ref[slot, 0, :, :DV].astype(F32) + mm(exch_ref[slot, 0, :, DV:], state),
             state,
         )
 
@@ -567,7 +800,7 @@
     def _():
         y_ref[...] = x_ref[...].astype(F32)
 
-    y_ref[...] += mm(gated, w_ref[...])
+    y_ref[...] += mm(gated, w_ref[...], NT)
 
     @pl.when(head == pl.num_programs(0) - 1)
     def _():
@@ -576,22 +809,22 @@
         h_ref[...] = (value * size * gain2_ref[...]).astype(BF16)
 
 
-def mixer_out(place, part, resp, maps, sums, gpre, gain, w_out, x, gain2):
+def mixer_out(place, slots, part, resp, exch, gpre, gain, weights, x, gain2):
     tokens, width = x.shape
-    places = maps.shape[0]
+    places = exch.shape[0]
     whole = lambda shape: pl.BlockSpec(shape, lambda h: (0,) * len(shape))
     return pl.pallas_call(
         mixer_kernel,
         grid=(H,),
         in_specs=[
             pl.BlockSpec(memory_space=pltpu.SMEM),
+            pl.BlockSpec(memory_space=pltpu.SMEM),
             pl.BlockSpec((tokens, DV), lambda h: (0, h)),
             pl.BlockSpec((tokens, DK), lambda h: (0, h)),
-            pl.BlockSpec((places, 1, DK, DK), lambda h: (0, h, 0, 0)),
-            pl.BlockSpec((places, 1, DK, DV), lambda h: (0, h, 0, 0)),
+            pl.BlockSpec((places, 1, DK, DV + DK), lambda h: (0, h, 0, 0)),
             pl.BlockSpec((tokens, DV), lambda h: (0, h)),
             whole((1, DV)),
-            pl.BlockSpec((DV, width), lambda h: (h, 0)),
+            pl.BlockSpec((width, DV), lambda h: (0, h + AT_OUT // DV)),
             whole((tokens, width)),
             whole((1, width)),
         ],
@@ -612,7 +845,7 @@
         compiler_params=params(),
         cost_estimate=cost(2 * tokens * width * H * DV, 2e7),
         name="mixer_out",
-    )(place, part, resp, maps, sums, gpre, gain, w_out, x, gain2)
+    )(place, slots, part, resp, exch, gpre, gain, weights, x, gain2)
 
 
 def mixer_back_kernel(
@@ -623,7 +856,7 @@
     def _():
         dgain_ref[...] = jnp.zeros_like(dgain_ref)
 
-    d_gated = mm(dmix_ref[...], w_ref[...], NT)
+    d_gated = mm(dmix_ref[...], w_ref[...])
     attn = attn_ref[...]
     size = lax.rsqrt(jnp.mean(attn * attn, axis=-1, keepdims=True) + 1e-05)
     unit = attn * size
@@ -641,7 +874,7 @@
     grad_ref[0] = mm(resp_ref[...], d_attn, TN).astype(BF16)
 
 
-def mixer_back(d_mixer, w_out, attn, gpre, gain, resp):
+def mixer_back(d_mixer, weights, attn, gpre, gain, resp):
     tokens, width = d_mixer.shape
     whole = lambda shape: pl.BlockSpec(shape, lambda h: (0,) * len(shape))
     return pl.pallas_call(
@@ -649,7 +882,7 @@
         grid=(H,),
         in_specs=[
             whole((tokens, width)),
-            pl.BlockSpec((DV, width), lambda h: (h, 0)),
+            pl.BlockSpec((width, DV), lambda h: (0, h + AT_OUT // DV)),
             pl.BlockSpec((tokens, DV), lambda h: (0, h)),
             pl.BlockSpec((tokens, DV), lambda h: (0, h)),
             whole((1, DV)),
@@ -670,7 +903,7 @@
         compiler_params=params(),
         cost_estimate=cost(2 * tokens * width * H * DV, 2e7),
         name="mixer_back",
-    )(d_mixer, w_out, attn, gpre, gain, resp)
+    )(d_mixer, weights, attn, gpre, gain, resp)
 
 
 def ffn_kernel(
@@ -685,9 +918,10 @@
         dh_ref[...] = jnp.zeros_like(dh_ref)
 
     hidden = h_ref[...]
-    gate = mm(hidden, wg_ref[...])
-    up = mm(hidden, wu_ref[...])
-    d_act = mm(dout_ref[...], wd_ref[...], NT)
+    w_gate, w_up, w_down = wg_ref[...], wu_ref[...], wd_ref[...]
+    gate = mm(hidden, w_gate)
+    up = mm(hidden, w_up)
+    d_act = mm(dout_ref[...], w_down)
     slope = jax.nn.sigmoid(gate)
     swish = gate * slope
     act = (swish * up).astype(BF16)
@@ -696,8 +930,8 @@
     d_up = (d_act * swish).astype(BF16)
     dg_ref[...] = d_gate
     du_ref[...] = d_up
-    res_ref[...] += mm(act, wd_ref[...])
-    dh_ref[...] += mm(d_gate, wg_ref[...], NT) + mm(d_up, wu_ref[...], NT)
+    res_ref[...] += mm(act, w_down, NT)
+    dh_ref[...] += mm(d_gate, w_gate, NT) + mm(d_up, w_up, NT)
 
     @pl.when(step == pl.num_programs(0) - 1)
     def _():
@@ -716,10 +950,10 @@
         dmix_ref[...] = d_y.astype(BF16)
 
 
-def feed_forward(hidden, d_out, y1, gain, w_gate, w_up, w_down):
+def feed_forward(hidden, d_out, y1, gain, weights, inner):
     tokens, width = hidden.shape
-    inner = w_down.shape[0]
     block = 256
+    weight = lambda at: pl.BlockSpec((width, block), lambda j: (0, j + at // block))
     whole = lambda shape: pl.BlockSpec(shape, lambda j: (0,) * len(shape))
     across = pl.BlockSpec((tokens, block), lambda j: (0, j))
     return pl.pallas_call(
@@ -730,10 +964,8 @@
             whole((tokens, width)),
             whole((tokens, width)),
             whole((1, width)),
-            pl.BlockSpec((width, block), lambda j: (0, j)),
-            pl.BlockSpec((width, block), lambda j: (0, j)),
-            pl.BlockSpec((block, width), lambda j: (j, 0)),
-        ],
+        ]
+        + [weight(AT_FFN + i * inner) for i in range(3)],
         out_specs=[
             whole((tokens, width)), across, across, across,
             whole((tokens, width)), whole((tokens, width)), whole((8, width)),
@@ -751,26 +983,28 @@
         compiler_params=params(),
         cost_estimate=cost(12 * tokens * width * inner, 3e7),
         name="feed_forward",
-    )(hidden, d_out, y1, gain, w_gate, w_up, w_down)
-
-
-def input_grad_kernel(
-    dp_ref, dg_ref, dl_ref, wq_ref, wo_ref, wl_ref, x_ref, gain_ref, dy_ref,
-    out_ref, dgain_ref, acc_ref, *, first,
-):
+    )(hidden, d_out, y1, gain, weights, weights, weights)
+
+
+def input_grad_kernel(*refs, groups, per_group):
+    dps, refs = refs[:groups], refs[groups:]
+    (dg_ref, dl_ref, w_ref, wl_ref, x_ref, gain_ref, dy_ref, turn_ref) = refs[:8]
+    out_ref, dgain_ref, acc_ref = refs[8:]
     step = pl.program_id(0)
 
     @pl.when(step == 0)
     def _():
         acc_ref[...] = mm(dl_ref[...], wl_ref[...], NT)
 
-    @pl.when(step < first)
+    for g in range(groups):
+
+        @pl.when(step // per_group == g)
+        def _(g=g):
+            acc_ref[...] += mm(dps[g][HALO:, :], w_ref[...], NT)
+
+    @pl.when(step >= groups * per_group)
     def _():
-        acc_ref[...] += mm(dp_ref[HALO:, :], wq_ref[...], NT)
-
-    @pl.when(step >= first)
-    def _():
-        acc_ref[...] += mm(dg_ref[...], wo_ref[...], NT)
+        acc_ref[...] += mm(dg_ref[...], w_ref[...], NT)
 
     @pl.when(step == pl.num_programs(0) - 1)
     def _():
@@ -781,33 +1015,39 @@
         dgain_ref[...] = jnp.zeros_like(dgain_ref)
         dgain_ref[0:1, :] = jnp.sum(d_hidden * unit, axis=0, keepdims=True)
         d_unit = d_hidden * gain_ref[...]
-        out_ref[...] = dy_ref[...] + size * (
+        total = dy_ref[...] + size * (
             d_unit - unit * jnp.mean(d_unit * unit, axis=-1, keepdims=True)
         )
-
-
-def input_grad(d_proj, d_gpre, d_logit, w_qkv, w_og, w_gates, x, gain, d_y):
+        high, low = halves(total)
+        out_ref[...] = mm(high, turn_ref[...], NT) + mm(low, turn_ref[...], NT)
+
+
+def input_grad(d_projs, d_gpre, d_logit, weights, x, gain, d_y, turn):
     tokens, width = x.shape
-    rows = d_proj.shape[0]
-    block = 512
-    first, second = w_qkv.shape[1] // block, w_og.shape[1] // block
+    rows = d_projs[0].shape[0]
+    block = HC
+    groups = len(d_projs)
+    per_group, second = d_projs[0].shape[1] // block, d_gpre.shape[1] // block
+    steps = H + second
     whole = lambda shape: pl.BlockSpec(shape, lambda j: (0,) * len(shape))
-    early = lambda j: (0, jnp.minimum(j, first - 1))
-    late = lambda j: (0, jnp.maximum(j - first, 0))
+    at = lambda g: lambda j: (0, jnp.clip(j - g * per_group, 0, per_group - 1))
+    late = lambda j: (0, jnp.maximum(j - H, 0))
+    weight = lambda j: (0, jnp.where(j < H, H - 1 - j, j - H + AT_GATE // block))
+    in_specs = [pl.BlockSpec((rows, block), at(g)) for g in range(groups)]
+    in_specs += [
+        pl.BlockSpec((tokens, block), late),
+        whole((tokens, LANES)),
+        pl.BlockSpec((width, block), weight),
+        pl.BlockSpec((width, LANES), lambda j: (0, AT_LOGIT // LANES)),
+        whole((tokens, width)),
+        whole((1, width)),
+        whole((tokens, width)),
+        whole((width, width)),
+    ]
     return pl.pallas_call(
-        functools.partial(input_grad_kernel, first=first),
-        grid=(first + second,),
-        in_specs=[
-            pl.BlockSpec((rows, block), early),
-            pl.BlockSpec((tokens, block), late),
-            whole((tokens, LANES)),
-            pl.BlockSpec((width, block), early),
-            pl.BlockSpec((width, block), late),
-            whole((width, LANES)),
-            whole((tokens, width)),
-            whole((1, width)),
-            whole((tokens, width)),
-        ],
+        functools.partial(input_grad_kernel, groups=groups, per_group=per_group),
+        grid=(steps,),
+        in_specs=in_specs,
         out_specs=[whole((tokens, width)), whole((8, width))],
         out_shape=[
             jax.ShapeDtypeStruct((tokens, width), F32),
@@ -815,15 +1055,133 @@
         ],
         scratch_shapes=[pltpu.VMEM((tokens, width), F32)],
         compiler_params=params(),
-        cost_estimate=cost(2 * tokens * width * (first + second) * block, 3e7),
+        cost_estimate=cost(2 * tokens * width * steps * block, 3e7),
         name="input_grad",
-    )(d_proj, d_gpre, d_logit, w_qkv, w_og, w_gates, x, gain, d_y)
+    )(*d_projs, d_gpre, d_logit, weights, weights, x, gain, d_y, turn)
 
 
 def shifted(block, axis, distance):
     devices = range(lax.axis_size(axis))
     route = [(i - distance, i) for i in devices if i - distance in devices]
     return lax.ppermute(block, axis, route)
+
+
+def send(value, planes=0, core=0, spot=0):
+    route = []
+    for z in range(PLANES):
+        for c in range(CORES):
+            for s in range(SPOTS):
+                target = (((z + planes) % PLANES) * CORES + (c ^ core)) * SPOTS + (s ^ spot)
+                route.append(((z * CORES + c) * SPOTS + s, target))
+    return lax.ppermute(value, ("dp", "seq"), route)
+
+
+def flipped(stack, spot):
+    pairs = stack.reshape((2, 2) + stack.shape[1:])
+    pairs = jnp.where(spot % 2 == 1, pairs[:, ::-1], pairs)
+    pairs = jnp.where(spot // 2 == 1, pairs[::-1], pairs)
+    return pairs.reshape(stack.shape)
+
+
+class Torus:
+    def __init__(self, spot, width):
+        self.spot = spot
+        place = lax.axis_index("dp")
+        z, c = place // CORES, place % CORES
+        piece = width // (PLANES * CORES * SPOTS)
+        at = jnp.arange(width)
+        core, rest = at // (width // 2), at % (width // 2)
+        quarter, plane, low = rest // (PLANES * piece), rest // piece % PLANES, rest % piece
+        self.order = (
+            ((z - plane) % PLANES * CORES + (c ^ core)) * SPOTS + (spot ^ quarter)
+        ) * piece + low
+        self.turn = (jnp.arange(width)[:, None] == self.order[None, :]).astype(BF16)
+        self.slots = jnp.arange(SPOTS, dtype=jnp.int32) ^ spot
+
+    def mine(self, value):
+        return lax.dot(value, self.turn, preferred_element_type=BF16)
+
+    def natural(self, value):
+        return lax.dot_general(value, self.turn, (NT, ((), ())), preferred_element_type=BF16)
+
+    def vector(self, value):
+        return jnp.take(value, self.order)
+
+    def vector_back(self, value):
+        return jnp.dot(value[None], self.turn.T.astype(F32), precision=lax.Precision.HIGHEST)[0]
+
+    def share(self, shard):
+        rows, cols = shard.shape
+        return flipped(shard.reshape(SPOTS, rows // SPOTS, cols), self.spot).reshape(rows, cols)
+
+    def others(self, value):
+        return send(value, core=1)
+
+    def left(self, value):
+        half = value.shape[1] // 2
+        return [(value, 0), (self.others(value[:, half:]), 0)]
+
+    def right(self, value):
+        return [value, self.others(value)]
+
+    def reduce(self, left, right, turned, skip_left=0, skip_right=0):
+        first, second = (1, 2) if turned else (2, 1)
+        width = left[0][0].shape[1] // 2
+        kept, sent = outer(left, right, width, [(0, second), (first, 3)], skip_left, skip_right)
+        size = kept.shape[0] // 2
+        total = kept.astype(F32) + send(sent, spot=first).astype(F32)
+        near, far = total[:size].astype(BF16), total[size:].astype(BF16)
+        total = near.astype(F32) + send(far, spot=second).astype(F32)
+        piece = size // PLANES
+        parts = [total[d * piece : (d + 1) * piece] for d in range(PLANES)]
+        total = parts[0]
+        for d in range(1, PLANES):
+            total += send(parts[d].astype(BF16), planes=-d).astype(F32)
+        total = total.astype(BF16)
+        spread = [total] + [send(total, spot=s) for s in range(1, SPOTS)]
+        stack = flipped(jnp.stack(spread), self.spot)
+        return stack.reshape(SPOTS * piece, -1).astype(F32)
+
+    def along(self, value):
+        return jnp.stack([value] + [send(value, spot=s) for s in range(1, SPOTS)])
+
+    def total(self, value):
+        value = value + send(value, core=1)
+        value = value + send(value, spot=1)
+        value = value + send(value, spot=2)
+        return value + (send(value, planes=1) + send(value, planes=2) + send(value, planes=3))
+
+
+class Plain:
+    def __init__(self, spot, width):
+        self.turn = jnp.eye(width, dtype=BF16)
+        self.slots = jnp.arange(lax.axis_size("seq"), dtype=jnp.int32)
+
+    def mine(self, value):
+        return value
+
+    natural = vector = vector_back = mine
+
+    def share(self, shard):
+        return lax.all_gather(shard, "dp", axis=0, tiled=True)
+
+    def left(self, value):
+        return [(value, 0)]
+
+    def right(self, value):
+        return [value]
+
+    def reduce(self, left, right, turned, skip_left=0, skip_right=0):
+        width = left[0][0].shape[1]
+        (full,) = outer(left, right, width, [tuple(range(width // LANES))], skip_left, skip_right)
+        part = lax.psum_scatter(full, "dp", scatter_dimension=0, tiled=True)
+        return lax.psum(part, "seq").astype(F32)
+
+    def along(self, value):
+        return lax.all_gather(value, "seq")
+
+    def total(self, value):
+        return lax.psum(value, ("dp", "seq"))
 
 
 def by_heads(query, key, value):
@@ -872,79 +1230,100 @@
     inputs, segments, cotangent, norm_gain_mix, w_query, w_key, w_value, w_outgate, w_gates,
     conv_weight, decay_log, dt_bias, out_norm_gain, w_out, norm_gain_ffn, w_ffn_gate, w_ffn_up, w_ffn_down,
 ):
-    x, d_out = inputs[0], cotangent[0]
-    tokens = x.shape[0]
+    tokens, width = inputs.shape[1:]
     place = lax.axis_index("seq")
     place_arr = place.reshape((1,)).astype(jnp.int32)
+    planned = (lax.axis_size("dp"), lax.axis_size("seq")) == (PLANES * CORES, SPOTS)
+    comm = (Torus if planned else Plain)(place, width)
+    slots = comm.slots
     low = lambda a: a.astype(BF16)
-    gather = lambda a, axis: lax.all_gather(a, "dp", axis=axis, tiled=True)
-
-    qkv_w = gather(
-        jnp.concatenate([by_heads(low(w_query), low(w_key), low(w_value)), wide(low(w_gates))], axis=1), 0
+
+    qkv = by_heads(low(w_query), low(w_key), low(w_value))
+    qkv = jnp.concatenate([qkv[:, h * HC : (h + 1) * HC] for h in reversed(range(H))], axis=1)
+    shard = jnp.concatenate(
+        [
+            qkv, jnp.pad(low(w_gates), ((0, 0), (0, AT_GATE - AT_LOGIT - 2 * H))), low(w_outgate), low(w_out).T,
+            low(w_ffn_gate), low(w_ffn_up), low(w_ffn_down).T,
+        ],
+        axis=1,
     )
-    gates_w = qkv_w[:, H * HC :]
-    qkv_w = qkv_w[:, : H * HC]
-    og_w = gather(low(w_outgate), 0)
-    out_w = gather(low(w_out), 1)
-    gate_w = gather(low(w_ffn_gate), 0)
-    up_w = gather(low(w_ffn_up), 0)
-    down_w = gather(low(w_ffn_down), 1)
-
-    gain_mix, gain_ffn, gain_out = norm_gain_mix[None], norm_gain_ffn[None], out_norm_gain[None]
+    inner = w_ffn_gate.shape[1]
+    weights = comm.share(shard)
+
+    gain_mix, gain_ffn = comm.vector(norm_gain_mix)[None], comm.vector(norm_gain_ffn)[None]
+    gain_out = out_norm_gain[None]
     taps_parts = by_heads(conv_weight[:, : H * DK], conv_weight[:, H * DK : 2 * H * DK], conv_weight[:, 2 * H * DK :])
     taps = jnp.pad(taps_parts, ((0, 8 - CONV), (0, 0)))
     par = jnp.pad(jnp.stack([decay_log, dt_bias]), ((0, 6), (0, LANES - H)))
     cols, back, segr = token_tables(segments[0], place, tokens)
 
-    x_ext = jnp.concatenate([shifted(x[tokens - HALO :], "seq", 1), x], axis=0)
-    proj, logits, hidden = project(x_ext, gain_mix, qkv_w, gates_w)
-    gpre = outgate(hidden, og_w)
-    part, resp, step_map, step_sum, *saved = delta_forward(proj, taps, logits, par, cols, segr)
-    maps = lax.all_gather(step_map, "seq")
-    sums = lax.all_gather(step_sum, "seq")
+    halo = shifted(inputs[0, tokens - HALO :], "seq", 1)
+    x_ext = comm.mine(jnp.concatenate([halo, inputs[0]], axis=0))
+    x = x_ext[HALO:]
+    d_out = comm.mine(cotangent[0])
+    value = x_ext.astype(F32)
+    size = lax.rsqrt(jnp.mean(value * value, axis=-1, keepdims=True) + 1e-06)
+    hidden = low(value * size * gain_mix)
+
+    outs = delta_forward(hidden, weights, taps, par, cols, segr, planned, inner)
+    if planned:
+        weights, outs = outs[0], outs[1:]
+    proj, logits, part, resp, exch, *saved = outs
+    if not planned:
+        exch = comm.along(exch[0])
+    gpre = outgate(hidden, weights)
     state_in, attn, gated, y1, hidden_mid = mixer_out(
-        place_arr, part, resp, maps, sums, gpre, gain_out, out_w, x, gain_ffn
+        place_arr, slots, part, resp, exch, gpre, gain_out, weights, x, gain_ffn
     )
     result, act, d_gate, d_up, d_y, d_mixer, d_gain_ffn = feed_forward(
-        hidden_mid, d_out, y1, gain_ffn, gate_w, up_w, down_w
+        hidden_mid, d_out, y1, gain_ffn, weights, inner
     )
-    d_attn, d_gpre, local_grad, d_gain_out = mixer_back(d_mixer, out_w, attn, gpre, gain_out, resp)
-    grads = lax.all_gather(local_grad, "seq")
-
-    def scattered(grad, axis):
-        part_sum = lax.psum_scatter(grad, "dp", scatter_dimension=axis, tiled=True)
-        return lax.psum(part_sum, "seq").astype(F32)
-
-    g_down = scattered(outer(act, d_out), 1)
-    g_gate = scattered(outer(hidden_mid, d_gate, 256), 0)
-    g_up = scattered(outer(hidden_mid, d_up, 256), 0)
-    g_out = scattered(outer(gated, d_mixer), 1)
-    g_og = scattered(outer(hidden, d_gpre, 512, HALO, 0), 0)
-    d_proj, d_logits, d_taps, d_par = delta_backward(
-        place_arr, proj, taps, logits, par, cols, back, segr, d_attn, state_in, maps, grads, saved
+    d_attn, d_gpre, local_grad, d_gain_out = mixer_back(d_mixer, weights, attn, gpre, gain_out, resp)
+    grads = comm.along(local_grad)
+
+    left_mid, left_out = comm.left(hidden_mid), comm.left(d_out)
+    g_down = comm.reduce(left_out, comm.right(act), True)
+    g_gate = comm.reduce(left_mid, comm.right(d_gate), False)
+    g_up = comm.reduce(left_mid, comm.right(d_up), True)
+    g_out = comm.reduce(comm.left(d_mixer), comm.right(gated), False)
+    left_in = comm.left(hidden)
+    g_og = comm.reduce(left_in, comm.right(d_gpre), True, HALO, 0)
+    heads = 2
+    groups = H // heads
+    d_projs, d_taps, d_logits, d_par, g_heads = [], [], 0.0, 0.0, []
+    for g in range(groups):
+        d_proj, d_logit, d_tap, d_pars = delta_backward(
+            g * heads, heads, place_arr, slots, proj, taps, logits, par, cols, back, segr,
+            d_attn, state_in, exch, grads, saved,
+        )
+        sent_back = shifted(d_proj[:HALO], "seq", -1)
+        d_proj = d_proj.at[tokens:].add(sent_back)
+        d_projs.append(d_proj)
+        d_taps.append(d_tap)
+        d_logits, d_par = d_logits + d_logit, d_par + d_pars
+        g_heads.append(comm.reduce(left_in, comm.right(d_proj), g % 2 == 0, HALO, HALO))
+    d_logit = low(d_logits)
+    g_gates = comm.reduce(left_in, comm.right(d_logit), False, HALO, 0)
+    d_inputs, d_gain_mix = input_grad(
+        d_projs, d_gpre, d_logit, weights, x, gain_mix, d_y, comm.turn
     )
-    sent_back = shifted(d_proj[:HALO], "seq", -1)
-    d_proj = d_proj.at[tokens:].add(sent_back)
-    d_logit = low(d_logits)
-    g_qkv = scattered(outer(hidden, d_proj, 512, HALO, HALO), 0)
-    g_gates = scattered(outer(hidden, d_logit, 128, HALO, 0), 0)
-    d_inputs, d_gain_mix = input_grad(d_proj, d_gpre, d_logit, qkv_w, og_w, gates_w, x, gain_mix, d_y)
-
-    g_query, g_key, g_value = from_heads(g_qkv)
-    small = lax.psum(
-        (
-            d_gain_mix[0],
-            jnp.concatenate(from_heads(d_taps[:CONV]), axis=1),
-            d_par[0, :H],
-            d_par[1, :H],
-            d_gain_out[0],
-            d_gain_ffn[0],
-        ),
-        ("dp", "seq"),
-    )
+
+    g_query, g_key, g_value = from_heads(jnp.concatenate(g_heads, axis=1))
+    d_conv = jnp.concatenate(from_heads(jnp.concatenate(d_taps, axis=1)[:CONV]), axis=1)
+    pieces = [
+        comm.vector_back(d_gain_mix[0]), d_conv.reshape(-1), d_par[0, :H], d_par[1, :H],
+        d_gain_out[0], comm.vector_back(d_gain_ffn[0]),
+    ]
+    flat = jnp.concatenate(pieces)
+    flat = comm.total(jnp.pad(flat, (0, -flat.shape[0] % 1024)).reshape(-1, LANES)).reshape(-1)
+    small, at = [], 0
+    for one in pieces:
+        small.append(flat[at : at + one.shape[0]])
+        at += one.shape[0]
     return (
-        result[None], d_inputs[None], small[0], g_query, g_key, g_value, g_og, g_gates[:, : 2 * H],
-        small[1], small[2], small[3], small[4], g_out, small[5], g_gate, g_up, g_down,
+        comm.natural(result)[None], d_inputs[None], small[0], g_query, g_key, g_value, g_og,
+        g_gates[:, : 2 * H], small[1].reshape(d_conv.shape), small[2], small[3], small[4], g_out.T,
+        small[5], g_gate, g_up, g_down.T,
     )
 
 

time: 1190 us -> 806 us (0.68)
  waiting for transfers between devices: 786 us -> 174 us
  Pallas kernels: 244 us -> 379 us
  starting transfers between devices: 6.09 us -> 135 us
  blocking collectives: 59.8 us -> 0 us
  other arithmetic: 17.6 us -> 43.6 us
  between operations: 14.9 us -> 2.86 us
  matrix products: 0 us -> 11.9 us
    all_gather x9 -> x0, waiting for transfers between devices: 329 us -> none  [the longest x6 257 us: local(): gather = lambda a, axis: lax.all_gather(a, 'dp', axis=axis, tiled=True)]
    reduce_scatter x5 -> x0, waiting for transfers between devices: 267 us -> none  [scattered(): part_sum = lax.psum_scatter(grad, 'dp', scatter_dimension=axis, tiled=True)]
    psum x2 -> x0, waiting for transfers between devices: 179 us -> none  [the longest x1 115 us: local(): lax.psum((d_gain_mix[0], jnp.concatenate(from_heads(d_taps[:CONV]), axis=...]
    ppermute x0 -> x103, waiting for transfers between devices: none -> 169 us  [send(): return lax.ppermute(value, ('dp', 'seq'), route)]
    pallas_call x11 -> x16, Pallas kernels: 181 us -> 315 us  [the longest x1 165 us: delta_forward(): pl.pallas_call(functools.partial(forward_kernel, planned=planned, spans=s...]
    ppermute x0 -> x103, starting transfers between devices: none -> 126 us  [send(): return lax.ppermute(value, ('dp', 'seq'), route)]
    psum x2 -> x0, blocking collectives: 59.8 us -> none  [the longest x1 42.4 us: local(): lax.psum((d_gain_mix[0], jnp.concatenate(from_heads(d_taps[:CONV]), axis=...]
    another operation x0 -> x31, other arithmetic: none -> 12.5 us
  transfers between devices with their start and end apart: 20 -> 108, of which waited for: 16 -> 51; matrix products, arithmetic and copies ran while one was open for 5% -> 12% of each run, Pallas kernels for 17% -> 19%
where the time goes in v2:
time: 806 us; the launch traced here: 796 us
  Pallas kernels  379 us (47%)
  waiting for transfers between devices  174 us (22%)
  starting transfers between devices  135 us (17%)
  local copies, waits for them, and re-layouts  50.3 us (6%)
  other arithmetic  43.6 us (5%)
  matrix products  11.9 us (1%)
    ppermute x103, waiting for transfers between devices, send(): return lax.ppermute(value, ('dp', 'seq'), route)  169 us
    pallas_call x1, Pallas kernels, delta_forward(): pl.pallas_call(functools.partial(forward_kernel, planned=planned, spans=s...  165 us
    ppermute x103, starting transfers between devices, send(): return lax.ppermute(value, ('dp', 'seq'), route)  126 us
    pallas_call x4, Pallas kernels, delta_backward(): pl.pallas_call(functools.partial(backward_kernel, first=first), grid=(hea...  65.3 us
    pallas_call x10, Pallas kernels, outer(): pl.pallas_call(functools.partial(outer_kernel, skips=[(skip_left, skip_ri...  63.2 us
    pallas_call x1, Pallas kernels, feed_forward(): pl.pallas_call(ffn_kernel, grid=(inner // block,), in_specs=[whole((token...  28.4 us
    pallas_call x1, Pallas kernels, input_grad(): pl.pallas_call(functools.partial(input_grad_kernel, groups=groups, per_gr...  21.7 us
    unnamed x143, local copies, waits for them, and re-layouts  19.7 us
  transfers between devices with their start and end apart: 108, of which 51 were waited for; matrix products, arithmetic and copies ran while one was open for 12% of the time, Pallas kernels for 19%

profile of v2, /device:TPU:8, one launch (start us, length us, event | category | flops | bytes accessed | tf_op | source)
XLA Modules:
  0.0 796.2 jit_solution(3998353503276889609)
XLA Ops:
  1.5 3.4 collective-permute-start
  6.8 4.5 gather_fusion.1
  11.3 4.5 gather_fusion
  31.3 4.6 reverse_select_fusion.1
  35.9 2.8 reverse_select_fusion
  39.5 2.3 fusion.14.dout_ref.refs_0_
  45.8 2.7 fusion.6
  51.4 165.2 %delta_forward.1 = (bf16[1024,17152]{1,0:T(8,128)(2,1)}, bf16[528,4096]{1,0:T(8,128)(2,1)}, f32[528,128]{1,0:T(8,128)}, f32[512,2048]{1,0:T(8,128)}, bf16[512,10...) custom-call(bf16[528,1024]{1,0:T(8,128)(2,1)} %fusion.8.refs_0_.h_re, ...), custom_call_target="tpu_custom_call" | custom-call | flops 48000000000 | bytes 40000000 | tf_op jit(solution)/shard_map/delta_forward/pallas_call | solution.py:543
  216.6 6.5 outgate.1.gpre_ref
  223.1 16.8 %mixer_out.1 = (f32[8,128,256]{2,1,0:T(8,128)}, f32[512,2048]{1,0:T(8,128)}, bf16[512,2048]{1,0:T(8,128)(2,1)}, f32[512,1024]{1,0:T(8,128)}, bf16[512,1024]{1,0:T(8,128)(2,1)}) custom-call(s32[1]{0:T(128)} %bitcast.place_ref, s32[4]{0:T(128)} %iota_xor_fusion.slot_ref, f32[512,2048]{1,0:T(8,128)} %get-tuple-element.132.part_ref, ...), custom_call_target="tpu_custom_call" | custom-call | flops 2147483648 | bytes 20000000 | tf_op jit(solution)/shard_map/mixer_out/pallas_call | solution.py:816
  240.0 28.4 %feed_forward.1 = (bf16[512,1024]{1,0:T(8,128)(2,1)}, bf16[512,2816]{1,0:T(8,128)(2,1)}, bf16[512,2816]{1,0:T(8,128)(2,1)}, bf16[512,2816]{1,0:T(8,128)(2,1)}, f...) custom-call(bf16[512,1024]{1,0:T(8,128)(2,1)} %get-tuple-element.136.h_ref.refs_0_, ...), custom_call_target="tpu_custom_call" | custom-call | flops 17716740096 | bytes 30000000 | tf_op jit(solution)/shard_map/feed_forward/pallas_call | solution.py:959
  268.4 11.8 %mixer_back.1 = (bf16[512,2048]{1,0:T(8,128)(2,1)}, bf16[512,2048]{1,0:T(8,128)(2,1)}, bf16[8,128,256]{2,1,0:T(8,128)(2,1)}, f32[8,256]{1,0:T(8,128)}) custom-call(bf16[512,1024]{1,0:T(8,128)(2,1)} %get-tuple-element.141.dmix_ref.refs_0_, bf16[1024,17152]{1,0:T(8,128)(2,1)} %get-tuple-element.135.w_ref.wg_ref.wu_ref.wd_ref.refs_6_.refs_7_, ...), custom_call_target="tpu_custom_call" | custom-call | flops 2147483648 | bytes 20000000 | tf_op jit(solution)/shard_map/mixer_back/pallas_call | solution.py:880
  281.4 3.1 collective-permute-start.2
  286.7 2.4 stack.276.back_ref
  296.2 10.9 %collective-permute-done.2 = bf16[8,128,256]{2,1,0:T(8,128)(2,1)} collective-permute-done((bf16[8,128,256]{2,1,0:T(8,128)(2,1)}, bf16[8,128,256]{2,1,0:T(8,128)(2,1)}, u32[]{:S(2)}, u32[]{:S(2)}) %collective-permute-start.2) | collective-permute-done | bytes 524320 | tf_op jit(solution)/shard_map/ppermute | solution.py:1076
  307.5 3.0 pad_maximum_fusion.grads_ref
  310.5 16.3 %delta_backward.4 = (bf16[528,1024]{1,0:T(8,128)(2,1)}, f32[512,128]{1,0:T(8,128)}, f32[8,1024]{1,0:T(8,128)}, f32[8,128]{1,0:T(8,128)}) custom-call(s32[1]{0:T(128)} %bitcast.place_ref, s32[4]{0:T(128)} %iota_xor_fusion.slot_ref, bf16[528,4096]{1,0:T(8,128)(2,1)} %get-tuple-element.139.p_ref, f32[8,4096]{1,0:T(8,128)} %pad.25.refs_2_.taps_ref, ...), custom_call_target="tpu_custom_call" | custom-call | flops 16000000000 | bytes 10000000 | tf_op jit(solution)/shard_map/delta_backward/pallas_call | solution.py:724
  326.8 16.1 %delta_backward.5 = (bf16[528,1024]{1,0:T(8,128)(2,1)}, f32[512,128]{1,0:T(8,128)}, f32[8,1024]{1,0:T(8,128)}, f32[8,128]{1,0:T(8,128)}) custom-call(s32[1]{0:T(128)} %bitcast.place_ref, s32[4]{0:T(128)} %iota_xor_fusion.slot_ref, bf16[528,4096]{1,0:T(8,128)(2,1)} %get-tuple-element.139.p_ref, f32[8,4096]{1,0:T(8,128)} %pad.25.refs_2_.taps_ref, ...), custom_call_target="tpu_custom_call" | custom-call | flops 16000000000 | bytes 10000000 | tf_op jit(solution)/shard_map/delta_backward/pallas_call | solution.py:724
  343.0 16.6 %delta_backward.6 = (bf16[528,1024]{1,0:T(8,128)(2,1)}, f32[512,128]{1,0:T(8,128)}, f32[8,1024]{1,0:T(8,128)}, f32[8,128]{1,0:T(8,128)}) custom-call(s32[1]{0:T(128)} %bitcast.place_ref, s32[4]{0:T(128)} %iota_xor_fusion.slot_ref, bf16[528,4096]{1,0:T(8,128)(2,1)} %get-tuple-element.139.p_ref, f32[8,4096]{1,0:T(8,128)} %pad.25.refs_2_.taps_ref, ...), custom_call_target="tpu_custom_call" | custom-call | flops 16000000000 | bytes 10000000 | tf_op jit(solution)/shard_map/delta_backward/pallas_call | solution.py:724
  359.7 16.2 %delta_backward.7 = (bf16[528,1024]{1,0:T(8,128)(2,1)}, f32[512,128]{1,0:T(8,128)}, f32[8,1024]{1,0:T(8,128)}, f32[8,128]{1,0:T(8,128)}) custom-call(s32[1]{0:T(128)} %bitcast.place_ref, s32[4]{0:T(128)} %iota_xor_fusion.slot_ref, bf16[528,4096]{1,0:T(8,128)(2,1)} %get-tuple-element.139.p_ref, f32[8,4096]{1,0:T(8,128)} %pad.25.refs_2_.taps_ref, ...), custom_call_target="tpu_custom_call" | custom-call | flops 16000000000 | bytes 10000000 | tf_op jit(solution)/shard_map/delta_backward/pallas_call | solution.py:724
  388.4 5.0 collective-permute-done.7
  398.1 21.7 %input_grad.1 = (f32[512,1024]{1,0:T(8,128)}, f32[8,1024]{1,0:T(8,128)}) custom-call(bf16[528,1024]{1,0:T(8,128)(2,1)} %add_dynamic-update-slice_fusion.3.refs_0_.refs_2_, bf16[528,1024]{1,0:T(8,128)(2,1)} %add_dynamic-update-slice_fusion.2.refs_1_.refs_2_, bf16[528,1024]{1,0:T(8,128)(2,1)} %add_dynamic-update-slice_fusion.1.refs_2_, ...), custom_call_target="tpu_custom_call" | custom-call | flops 6442450944 | bytes 30000000 | tf_op jit(solution)/shard_map/input_grad/pallas_call | solution.py:1047
  421.3 2.4 outer.15
  423.7 3.5 collective-permute-start.61
  427.2 2.7 fusion.1
  432.0 2.8 collective-permute-done.62
  435.1 4.2 collective-permute-start.64
  444.2 2.3 fusion.15
  452.6 2.9 collective-permute-done.10
  463.8 3.6 collective-permute-done.12
  471.8 4.0 outer.13
  475.8 4.1 outer.12
  481.5 4.1 outer.11
  485.8 4.1 outer.10
  490.8 6.2 outer.14
  499.0 6.2 outer.16
  508.1 3.8 collective-permute-done.25
  513.3 2.6 collective-permute-done.16
  516.8 4.7 collective-permute-done.44
  523.5 3.7 collective-permute-start.46
  527.3 2.4 collective-permute-start.45
  530.1 3.5 collective-permute-start.37
  537.8 3.7 collective-permute-start.27
  542.3 3.1 collective-permute-start.19
  567.7 2.6 collective-permute-done.21
  578.8 10.7 %outer.17 = (bf16[256,2816]{1,0:T(8,128)(2,1)}, bf16[256,2816]{1,0:T(8,128)(2,1)}) custom-call(bf16[512,1024]{1,0:T(8,128)(2,1)} %get-tuple-element.136.h_ref.refs_0_, bf16[512,512]{1,0:T(8,128)(2,1)} %copy-done.47, bf16[512,2816]{1,0:T(8,128)(2,1)} %get-tuple-element.189.refs_2_, bf16[512,2816]{1,0:T(8,128)(2,1)} %collective-permute-done.80.refs_3_), custom_call_target="tpu_custom_call" | custom-call | flops 2952790016 | bytes 8650752 | tf_op jit(solution)/shard_map/outer/pallas_call | solution.py:135
  589.6 10.7 %outer.18 = (bf16[256,2816]{1,0:T(8,128)(2,1)}, bf16[256,2816]{1,0:T(8,128)(2,1)}) custom-call(bf16[512,1024]{1,0:T(8,128)(2,1)} %get-tuple-element.136.h_ref.refs_0_, bf16[512,512]{1,0:T(8,128)(2,1)} %copy-done.47, bf16[512,2816]{1,0:T(8,128)(2,1)} %get-tuple-element.192.refs_2_, bf16[512,2816]{1,0:T(8,128)(2,1)} %collective-permute-done.89.refs_3_), custom_call_target="tpu_custom_call" | custom-call | flops 2952790016 | bytes 8650752 | tf_op jit(solution)/shard_map/outer/pallas_call | solution.py:135
  601.5 10.8 %outer.19 = (bf16[256,2816]{1,0:T(8,128)(2,1)}, bf16[256,2816]{1,0:T(8,128)(2,1)}) custom-call(bf16[512,1024]{1,0:T(8,128)(2,1)} %fusion.14.dout_ref.refs_0_, bf16[512,512]{1,0:T(8,128)(2,1)} %copy-done.53, bf16[512,2816]{1,0:T(8,128)(2,1)} %get-tuple-element.195.refs_2_, bf16[512,2816]{1,0:T(8,128)(2,1)} %collective-permute-done.99.refs_3_), custom_call_target="tpu_custom_call" | custom-call | flops 2952790016 | bytes 8650752 | tf_op jit(solution)/shard_map/outer/pallas_call | solution.py:135
  616.1 29.3 %collective-permute-done.72 = bf16[128,2048]{1,0:T(8,128)(2,1)S(1)} collective-permute-done((bf16[128,2048]{1,0:T(8,128)(2,1)S(1)}, bf16[128,2048]{1,0:T(8,128)(2,1)S(1)}, u32[]{:S(2)}, u32[]{:S(2)}) %collective-permute-start.72) | collective-permute-done | bytes 524320 | tf_op jit(solution)/shard_map/ppermute | solution.py:1076
  646.7 3.3 collective-permute-start.74
  652.3 6.2 collective-permute-done.74
  658.5 3.8 collective-permute-start.55
  662.3 4.7 collective-permute-done.73
  681.9 2.3 collective-permute-done.57
  692.8 22.5 %collective-permute-done.100 = bf16[256,2816]{1,0:T(8,128)(2,1)} collective-permute-done((bf16[256,2816]{1,0:T(8,128)(2,1)}, bf16[256,2816]{1,0:T(8,128)(2,1)}, u32[]{:S(2)}, u32[]{:S(2)}) %collective-permute-start.100) | collective-permute-done | bytes 1441824 | tf_op jit(solution)/shard_map/ppermute | solution.py:1076
  718.9 9.5 %collective-permute-done.82 = bf16[128,2816]{1,0:T(8,128)(2,1)S(1)} collective-permute-done((bf16[128,2816]{1,0:T(8,128)(2,1)S(1)}, bf16[128,2816]{1,0:T(8,128)(2,1)S(1)}, u32[]{:S(2)}, u32[]{:S(2)}) %collective-permute-start.82) | collective-permute-done | bytes 720928 | tf_op jit(solution)/shard_map/ppermute | solution.py:1076
  728.6 2.6 collective-permute-start.85
  735.2 3.3 collective-permute-start.93
  738.7 4.7 collective-permute-done.85
  743.4 10.2 %collective-permute-done.84 = bf16[32,2816]{1,0:T(8,128)(2,1)S(1)} collective-permute-done((bf16[32,2816]{1,0:T(8,128)(2,1)S(1)}, bf16[32,2816]{1,0:T(8,128)(2,1)S(1)}, u32[]{:S(2)}, u32[]{:S(2)}) %collective-permute-start.84) | collective-permute-done | bytes 180256 | tf_op jit(solution)/shard_map/ppermute | solution.py:1076
  759.3 9.9 %collective-permute-done.93 = bf16[32,2816]{1,0:T(8,128)(2,1)S(1)} collective-permute-done((bf16[32,2816]{1,0:T(8,128)(2,1)S(1)}, bf16[32,2816]{1,0:T(8,128)(2,1)S(1)}, u32[]{:S(2)}, u32[]{:S(2)}) %collective-permute-start.93) | collective-permute-done | bytes 180256 | tf_op jit(solution)/shard_map/ppermute | solution.py:1076
  769.2 2.3 collective-permute-start.88
  774.4 2.9 collective-permute-start.97
  786.4 2.3 collective-permute-done.96
  (503 shorter events, 193.5 us)
Async XLA Ops:
  1.5 44.2 %collective-permute-start = (bf16[16,1024]{1,0:T(8,128)(2,1)S(1)}, bf16[16,1024]{1,0:T(8,128)(2,1)S(1)}, u32[]{:S(2)}, u32[]{:S(2)}) collective-permute-start(bf16[16,1024]{1,0:T(8,128)(2,1)S(1)} %slice_bitcast_fusion.1), channel_id=1, source_target_pairs={{0,1},{1,2},{2,3},{4,5},{5,6},{6,7},{8,9},{9,10},{10,11},{12,13},{... | collective-permute-start | bytes 98312 | tf_op jit(solution)/shard_map/ppermute | solution.py:1066
  280.2 16.0 %collective-permute-start.3 = (bf16[8,128,256]{2,1,0:T(8,128)(2,1)}, bf16[8,128,256]{2,1,0:T(8,128)(2,1)}, u32[]{:S(2)}, u32[]{:S(2)}) collective-permute-start(bf16[8,128,256]{2,1,0:T(8,128)(2,1)} %get-tuple-element.145), channel_id=1, source_target_pairs={{0,3},{1,2},{2,1},{3,0},{4,7},{5,6},{6,5},{7,4},{8,11},{9,10},{10,... | collective-permute-start | bytes 1572872 | tf_op jit(solution)/shard_map/ppermute | solution.py:1076
  281.4 25.7 %collective-permute-start.2 = (bf16[8,128,256]{2,1,0:T(8,128)(2,1)}, bf16[8,128,256]{2,1,0:T(8,128)(2,1)}, u32[]{:S(2)}, u32[]{:S(2)}) collective-permute-start(bf16[8,128,256]{2,1,0:T(8,128)(2,1)} %get-tuple-element.145), channel_id=1, source_target_pairs={{0,2},{1,3},{2,0},{3,1},{4,6},{5,7},{6,4},{7,5},{8,10},{9,11},{10,... | collective-permute-start | bytes 1572872 | tf_op jit(solution)/shard_map/ppermute | solution.py:1076
  284.5 23.0 %collective-permute-start.1 = (bf16[8,128,256]{2,1,0:T(8,128)(2,1)}, bf16[8,128,256]{2,1,0:T(8,128)(2,1)}, u32[]{:S(2)}, u32[]{:S(2)}) collective-permute-start(bf16[8,128,256]{2,1,0:T(8,128)(2,1)} %get-tuple-element.145), channel_id=1, source_target_pairs={{0,1},{1,0},{2,3},{3,2},{4,5},{5,4},{6,7},{7,6},{8,9},{9,8},{10,11... | collective-permute-start | bytes 1572872 | tf_op jit(solution)/shard_map/ppermute | solution.py:1076
  292.0 127.8 %collective-permute-start.14 = (bf16[528,512]{1,0:T(8,128)(2,1)S(1)}, bf16[528,512]{1,0:T(8,128)(2,1)S(1)}, u32[]{:S(2)}, u32[]{:S(2)}) collective-permute-start(bf16[528,512]{1,0:T(8,128)(2,1)S(1)} %slice.598), channel_id=1, source_target_pairs={{0,4},{1,5},{2,6},{3,7},{4,0},{5,1},{6,2},{7,3},{8,12},{9,13},{10,... | collective-permute-start | bytes 1622024 | tf_op jit(solution)/shard_map/ppermute | solution.py:1076
  292.0 197.8 %collective-permute-start.51 = (bf16[512,2048]{1,0:T(8,128)(2,1)}, bf16[512,2048]{1,0:T(8,128)(2,1)}, u32[]{:S(2)}, u32[]{:S(2)}) collective-permute-start(bf16[512,2048]{1,0:T(8,128)(2,1)} %get-tuple-element.156.refs_4_.refs_2_), channel_id=1, source_target_pairs={{0,4},{1,5},{2,6},{3,7},{4,0},{5,1},{6,2},{7,3},{8,12},{9,13},{10,... | collective-permute-start | bytes 6291464 | tf_op jit(solution)/shard_map/ppermute | solution.py:1076
  379.6 15.2 %collective-permute-start.5 = (bf16[16,1024]{1,0:T(8,128)(2,1)S(1)}, bf16[16,1024]{1,0:T(8,128)(2,1)S(1)}, u32[]{:S(2)}, u32[]{:S(2)}) collective-permute-start(bf16[16,1024]{1,0:T(8,128)(2,1)S(1)} %slice.491), channel_id=1, source_target_pairs={{1,0},{2,1},{3,2},{5,4},{6,5},{7,6},{9,8},{10,9},{11,10},{13,12},{... | collective-permute-start | bytes 98312 | tf_op jit(solution)/shard_map/ppermute | solution.py:1066
  381.8 14.9 %collective-permute-start.6 = (bf16[16,1024]{1,0:T(8,128)(2,1)S(1)}, bf16[16,1024]{1,0:T(8,128)(2,1)S(1)}, u32[]{:S(2)}, u32[]{:S(2)}) collective-permute-start(bf16[16,1024]{1,0:T(8,128)(2,1)S(1)} %slice.493), channel_id=1, source_target_pairs={{1,0},{2,1},{3,2},{5,4},{6,5},{7,6},{9,8},{10,9},{11,10},{13,12},{... | collective-permute-start | bytes 98312 | tf_op jit(solution)/shard_map/ppermute | solution.py:1066
  393.5 26.4 %collective-permute-start.60 = (bf16[512,128]{1,0:T(8,128)(2,1)S(1)}, bf16[512,128]{1,0:T(8,128)(2,1)S(1)}, u32[]{:S(2)}, u32[]{:S(2)}) collective-permute-start(bf16[512,128]{1,0:T(8,128)(2,1)S(1)} %add_convert_fusion.9.refs_5_.refs_2_), channel_id=1, source_target_pairs={{0,4},{1,5},{2,6},{3,7},{4,0},{5,1},{6,2},{7,3},{8,12},{9,13},{10,... | collective-permute-start | bytes 393224 | tf_op jit(solution)/shard_map/ppermute | solution.py:1076
  394.8 72.5 %collective-permute-start.42 = (bf16[528,1024]{1,0:T(8,128)(2,1)}, bf16[528,1024]{1,0:T(8,128)(2,1)}, u32[]{:S(2)}, u32[]{:S(2)}) collective-permute-start(bf16[528,1024]{1,0:T(8,128)(2,1)} %add_dynamic-update-slice_fusion.refs_3_.refs_2_), channel_id=1, source_target_pairs={{0,4},{1,5},{2,6},{3,7},{4,0},{5,1},{6,2},{7,3},{8,12},{9,13},{10,... | collective-permute-start | bytes 3244040 | tf_op jit(solution)/shard_map/ppermute | solution.py:1076
  447.4 51.4 %collective-permute-start.70 = (bf16[512,2048]{1,0:T(8,128)(2,1)}, bf16[512,2048]{1,0:T(8,128)(2,1)}, u32[]{:S(2)}, u32[]{:S(2)}) collective-permute-start(bf16[512,2048]{1,0:T(8,128)(2,1)} %get-tuple-element.186.refs_2_), channel_id=1, source_target_pairs={{0,4},{1,5},{2,6},{3,7},{4,0},{5,1},{6,2},{7,3},{8,12},{9,13},{10,... | collective-permute-start | bytes 6291464 | tf_op jit(solution)/shard_map/ppermute | solution.py:1076
  460.0 11.7 %collective-permute-start.33 = (bf16[528,1024]{1,0:T(8,128)(2,1)S(1)}, bf16[528,1024]{1,0:T(8,128)(2,1)}, u32[]{:S(2)}, u32[]{:S(2)}) collective-permute-start(bf16[528,1024]{1,0:T(8,128)(2,1)S(1)} %copy-done.13), channel_id=1, source_target_pairs={{0,4},{1,5},{2,6},{3,7},{4,0},{5,1},{6,2},{7,3},{8,12},{9,13},{10,... | collective-permute-start | bytes 3244040 | tf_op jit(solution)/shard_map/ppermute | solution.py:1076
  467.3 12.6 %collective-permute-start.24 = (bf16[528,1024]{1,0:T(8,128)(2,1)S(1)}, bf16[528,1024]{1,0:T(8,128)(2,1)}, u32[]{:S(2)}, u32[]{:S(2)}) collective-permute-start(bf16[528,1024]{1,0:T(8,128)(2,1)S(1)} %copy-done.14), channel_id=1, source_target_pairs={{0,4},{1,5},{2,6},{3,7},{4,0},{5,1},{6,2},{7,3},{8,12},{9,13},{10,... | collective-permute-start | bytes 3244040 | tf_op jit(solution)/shard_map/ppermute | solution.py:1076
  467.3 18.2 %collective-permute-start.15 = (bf16[528,1024]{1,0:T(8,128)(2,1)}, bf16[528,1024]{1,0:T(8,128)(2,1)}, u32[]{:S(2)}, u32[]{:S(2)}) collective-permute-start(bf16[528,1024]{1,0:T(8,128)(2,1)} %add_dynamic-update-slice_fusion.3.refs_0_.refs_2_), channel_id=1, source_target_pairs={{0,4},{1,5},{2,6},{3,7},{4,0},{5,1},{6,2},{7,3},{8,12},{9,13},{10,... | collective-permute-start | bytes 3244040 | tf_op jit(solution)/shard_map/ppermute | solution.py:1076
  471.7 25.4 %collective-permute-start.69 = (bf16[512,512]{1,0:T(8,128)(2,1)S(1)}, bf16[512,512]{1,0:T(8,128)(2,1)S(1)}, u32[]{:S(2)}, u32[]{:S(2)}) collective-permute-start(bf16[512,512]{1,0:T(8,128)(2,1)S(1)} %slice.553), channel_id=1, source_target_pairs={{0,4},{1,5},{2,6},{3,7},{4,0},{5,1},{6,2},{7,3},{8,12},{9,13},{10,... | collective-permute-start | bytes 1572872 | tf_op jit(solution)/shard_map/ppermute | solution.py:1076
  479.9 25.3 %collective-permute-start.43 = (bf16[256,1024]{1,0:T(8,128)(2,1)S(1)}, bf16[256,1024]{1,0:T(8,128)(2,1)S(1)}, u32[]{:S(2)}, u32[]{:S(2)}) collective-permute-start(bf16[256,1024]{1,0:T(8,128)(2,1)S(1)} %copy-done.52), channel_id=1, source_target_pairs={{0,2},{1,3},{2,0},{3,1},{4,6},{5,7},{6,4},{7,5},{8,10},{9,11},{10,... | collective-permute-start | bytes 1572872 | tf_op jit(solution)/shard_map/ppermute | solution.py:1076
  485.5 91.6 %collective-permute-start.80 = (bf16[512,2816]{1,0:T(8,128)(2,1)}, bf16[512,2816]{1,0:T(8,128)(2,1)}, u32[]{:S(2)}, u32[]{:S(2)}) collective-permute-start(bf16[512,2816]{1,0:T(8,128)(2,1)} %get-tuple-element.189.refs_2_), channel_id=1, source_target_pairs={{0,4},{1,5},{2,6},{3,7},{4,0},{5,1},{6,2},{7,3},{8,12},{9,13},{10,... | collective-permute-start | bytes 8650760 | tf_op jit(solution)/shard_map/ppermute | solution.py:1076
  489.9 17.6 %collective-permute-start.34 = (bf16[256,1024]{1,0:T(8,128)(2,1)S(1)}, bf16[256,1024]{1,0:T(8,128)(2,1)S(1)}, u32[]{:S(2)}, u32[]{:S(2)}) collective-permute-start(bf16[256,1024]{1,0:T(8,128)(2,1)S(1)} %copy-done.50), channel_id=1, source_target_pairs={{0,1},{1,0},{2,3},{3,2},{4,5},{5,4},{6,7},{7,6},{8,9},{9,8},{10,11... | collective-permute-start | bytes 1572872 | tf_op jit(solution)/shard_map/ppermute | solution.py:1076
  497.1 14.8 %collective-permute-start.25 = (bf16[256,1024]{1,0:T(8,128)(2,1)S(1)}, bf16[256,1024]{1,0:T(8,128)(2,1)S(1)}, u32[]{:S(2)}, u32[]{:S(2)}) collective-permute-start(bf16[256,1024]{1,0:T(8,128)(2,1)S(1)} %copy-done.49), channel_id=1, source_target_pairs={{0,2},{1,3},{2,0},{3,1},{4,6},{5,7},{6,4},{7,5},{8,10},{9,11},{10,... | collective-permute-start | bytes 1572872 | tf_op jit(solution)/shard_map/ppermute | solution.py:1076
  498.8 17.1 %collective-permute-start.16 = (bf16[256,1024]{1,0:T(8,128)(2,1)S(1)}, bf16[256,1024]{1,0:T(8,128)(2,1)S(1)}, u32[]{:S(2)}, u32[]{:S(2)}) collective-permute-start(bf16[256,1024]{1,0:T(8,128)(2,1)S(1)} %copy-done.48), channel_id=1, source_target_pairs={{0,1},{1,0},{2,3},{3,2},{4,5},{5,4},{6,7},{7,6},{8,9},{9,8},{10,11... | collective-permute-start | bytes 1572872 | tf_op jit(solution)/shard_map/ppermute | solution.py:1076
  505.4 16.1 %collective-permute-start.44 = (bf16[128,1024]{1,0:T(8,128)(2,1)S(1)}, bf16[128,1024]{1,0:T(8,128)(2,1)S(1)}, u32[]{:S(2)}, u32[]{:S(2)}) collective-permute-start(bf16[128,1024]{1,0:T(8,128)(2,1)S(1)} %slice.618), channel_id=1, source_target_pairs={{0,1},{1,0},{2,3},{3,2},{4,5},{5,4},{6,7},{7,6},{8,9},{9,8},{10,11... | collective-permute-start | bytes 786440 | tf_op jit(solution)/shard_map/ppermute | solution.py:1076
  507.7 15.8 %collective-permute-start.35 = (bf16[128,1024]{1,0:T(8,128)(2,1)S(1)}, bf16[128,1024]{1,0:T(8,128)(2,1)S(1)}, u32[]{:S(2)}, u32[]{:S(2)}) collective-permute-start(bf16[128,1024]{1,0:T(8,128)(2,1)S(1)} %slice.612), channel_id=1, source_target_pairs={{0,2},{1,3},{2,0},{3,1},{4,6},{5,7},{6,4},{7,5},{8,10},{9,11},{10,... | collective-permute-start | bytes 786440 | tf_op jit(solution)/shard_map/ppermute | solution.py:1076
  512.1 15.2 %collective-permute-start.26 = (bf16[128,1024]{1,0:T(8,128)(2,1)S(1)}, bf16[128,1024]{1,0:T(8,128)(2,1)S(1)}, u32[]{:S(2)}, u32[]{:S(2)}) collective-permute-start(bf16[128,1024]{1,0:T(8,128)(2,1)S(1)} %slice.606), channel_id=1, source_target_pairs={{0,1},{1,0},{2,3},{3,2},{4,5},{5,4},{6,7},{7,6},{8,9},{9,8},{10,11... | collective-permute-start | bytes 786440 | tf_op jit(solution)/shard_map/ppermute | solution.py:1076
  516.1 13.8 %collective-permute-start.17 = (bf16[128,1024]{1,0:T(8,128)(2,1)S(1)}, bf16[128,1024]{1,0:T(8,128)(2,1)S(1)}, u32[]{:S(2)}, u32[]{:S(2)}) collective-permute-start(bf16[128,1024]{1,0:T(8,128)(2,1)S(1)} %slice.600), channel_id=1, source_target_pairs={{0,2},{1,3},{2,0},{3,1},{4,6},{5,7},{6,4},{7,5},{8,10},{9,11},{10,... | collective-permute-start | bytes 786440 | tf_op jit(solution)/shard_map/ppermute | solution.py:1076
  523.5 10.1 %collective-permute-start.46 = (bf16[32,1024]{1,0:T(8,128)(2,1)S(1)}, bf16[32,1024]{1,0:T(8,128)(2,1)S(1)}, u32[]{:S(2)}, u32[]{:S(2)}) collective-permute-start(bf16[32,1024]{1,0:T(8,128)(2,1)S(1)} %get-tuple-element.295), channel_id=1, source_target_pairs={{0,16},{1,17},{2,18},{3,19},{4,20},{5,21},{6,22},{7,23},{8,24},{9,... | collective-permute-start | bytes 196616 | tf_op jit(solution)/shard_map/ppermute | solution.py:1076
  533.6 8.6 %collective-permute-start.36 = (bf16[32,1024]{1,0:T(8,128)(2,1)S(1)}, bf16[32,1024]{1,0:T(8,128)(2,1)S(1)}, u32[]{:S(2)}, u32[]{:S(2)}) collective-permute-start(bf16[32,1024]{1,0:T(8,128)(2,1)S(1)} %get-tuple-element.290), channel_id=1, source_target_pairs={{0,24},{1,25},{2,26},{3,27},{4,28},{5,29},{6,30},{7,31},{8,0},{9,1... | collective-permute-start | bytes 196616 | tf_op jit(solution)/shard_map/ppermute | solution.py:1076
  533.7 8.6 %collective-permute-start.29 = (bf16[32,1024]{1,0:T(8,128)(2,1)S(1)}, bf16[32,1024]{1,0:T(8,128)(2,1)S(1)}, u32[]{:S(2)}, u32[]{:S(2)}) collective-permute-start(bf16[32,1024]{1,0:T(8,128)(2,1)S(1)} %get-tuple-element.288), channel_id=1, source_target_pairs={{0,8},{1,9},{2,10},{3,11},{4,12},{5,13},{6,14},{7,15},{8,16},{9,17... | collective-permute-start | bytes 196616 | tf_op jit(solution)/shard_map/ppermute | solution.py:1076
  535.7 9.6 %collective-permute-start.28 = (bf16[32,1024]{1,0:T(8,128)(2,1)S(1)}, bf16[32,1024]{1,0:T(8,128)(2,1)S(1)}, u32[]{:S(2)}, u32[]{:S(2)}) collective-permute-start(bf16[32,1024]{1,0:T(8,128)(2,1)S(1)} %get-tuple-element.289), channel_id=1, source_target_pairs={{0,16},{1,17},{2,18},{3,19},{4,20},{5,21},{6,22},{7,23},{8,24},{9,... | collective-permute-start | bytes 196616 | tf_op jit(solution)/shard_map/ppermute | solution.py:1076
  537.8 8.6 %collective-permute-start.27 = (bf16[32,1024]{1,0:T(8,128)(2,1)S(1)}, bf16[32,1024]{1,0:T(8,128)(2,1)S(1)}, u32[]{:S(2)}, u32[]{:S(2)}) collective-permute-start(bf16[32,1024]{1,0:T(8,128)(2,1)S(1)} %get-tuple-element.287), channel_id=1, source_target_pairs={{0,24},{1,25},{2,26},{3,27},{4,28},{5,29},{6,30},{7,31},{8,0},{9,1... | collective-permute-start | bytes 196616 | tf_op jit(solution)/shard_map/ppermute | solution.py:1076
  552.2 37.3 %collective-permute-start.89 = (bf16[512,2816]{1,0:T(8,128)(2,1)}, bf16[512,2816]{1,0:T(8,128)(2,1)}, u32[]{:S(2)}, u32[]{:S(2)}) collective-permute-start(bf16[512,2816]{1,0:T(8,128)(2,1)} %get-tuple-element.192.refs_2_), channel_id=1, source_target_pairs={{0,4},{1,5},{2,6},{3,7},{4,0},{5,1},{6,2},{7,3},{8,12},{9,13},{10,... | collective-permute-start | bytes 8650760 | tf_op jit(solution)/shard_map/ppermute | solution.py:1076
  563.2 38.3 %collective-permute-start.99 = (bf16[512,2816]{1,0:T(8,128)(2,1)}, bf16[512,2816]{1,0:T(8,128)(2,1)}, u32[]{:S(2)}, u32[]{:S(2)}) collective-permute-start(bf16[512,2816]{1,0:T(8,128)(2,1)} %get-tuple-element.195.refs_2_), channel_id=1, source_target_pairs={{0,4},{1,5},{2,6},{3,7},{4,0},{5,1},{6,2},{7,3},{8,12},{9,13},{10,... | collective-permute-start | bytes 8650760 | tf_op jit(solution)/shard_map/ppermute | solution.py:1076
  567.7 9.4 %collective-permute-start.79 = (bf16[512,512]{1,0:T(8,128)(2,1)S(1)}, bf16[512,512]{1,0:T(8,128)(2,1)S(1)}, u32[]{:S(2)}, u32[]{:S(2)}) collective-permute-start(bf16[512,512]{1,0:T(8,128)(2,1)S(1)} %copy-done.29), channel_id=1, source_target_pairs={{0,4},{1,5},{2,6},{3,7},{4,0},{5,1},{6,2},{7,3},{8,12},{9,13},{10,... | collective-permute-start | bytes 1572872 | tf_op jit(solution)/shard_map/ppermute | solution.py:1076
  570.3 42.0 %collective-permute-start.71 = (bf16[256,2048]{1,0:T(8,128)(2,1)}, bf16[256,2048]{1,0:T(8,128)(2,1)S(1)}, u32[]{:S(2)}, u32[]{:S(2)}) collective-permute-start(bf16[256,2048]{1,0:T(8,128)(2,1)} %get-tuple-element.188), channel_id=1, source_target_pairs={{0,2},{1,3},{2,0},{3,1},{4,6},{5,7},{6,4},{7,5},{8,10},{9,11},{10,... | collective-permute-start | bytes 3145736 | tf_op jit(solution)/shard_map/ppermute | solution.py:1076
  577.1 23.2 %collective-permute-start.98 = (bf16[512,512]{1,0:T(8,128)(2,1)S(1)}, bf16[512,512]{1,0:T(8,128)(2,1)S(1)}, u32[]{:S(2)}, u32[]{:S(2)}) collective-permute-start(bf16[512,512]{1,0:T(8,128)(2,1)S(1)} %copy-done.28), channel_id=1, source_target_pairs={{0,4},{1,5},{2,6},{3,7},{4,0},{5,1},{6,2},{7,3},{8,12},{9,13},{10,... | collective-permute-start | bytes 1572872 | tf_op jit(solution)/shard_map/ppermute | solution.py:1076
  577.2 36.5 %collective-permute-start.52 = (bf16[256,2048]{1,0:T(8,128)(2,1)S(1)}, bf16[256,2048]{1,0:T(8,128)(2,1)S(1)}, u32[]{:S(2)}, u32[]{:S(2)}) collective-permute-start(bf16[256,2048]{1,0:T(8,128)(2,1)S(1)} %copy-done.45), channel_id=1, source_target_pairs={{0,1},{1,0},{2,3},{3,2},{4,5},{5,4},{6,7},{7,6},{8,9},{9,8},{10,11... | collective-permute-start | bytes 3145736 | tf_op jit(solution)/shard_map/ppermute | solution.py:1076
  589.4 97.5 %collective-permute-start.81 = (bf16[256,2816]{1,0:T(8,128)(2,1)}, bf16[256,2816]{1,0:T(8,128)(2,1)}, u32[]{:S(2)}, u32[]{:S(2)}) collective-permute-start(bf16[256,2816]{1,0:T(8,128)(2,1)} %get-tuple-element.191), channel_id=1, source_target_pairs={{0,2},{1,3},{2,0},{3,1},{4,6},{5,7},{6,4},{7,5},{8,10},{9,11},{10,... | collective-permute-start | bytes 4325384 | tf_op jit(solution)/shard_map/ppermute | solution.py:1076
  600.3 89.5 %collective-permute-start.90 = (bf16[256,2816]{1,0:T(8,128)(2,1)}, bf16[256,2816]{1,0:T(8,128)(2,1)}, u32[]{:S(2)}, u32[]{:S(2)}) collective-permute-start(bf16[256,2816]{1,0:T(8,128)(2,1)} %get-tuple-element.194), channel_id=1, source_target_pairs={{0,1},{1,0},{2,3},{3,2},{4,5},{5,4},{6,7},{7,6},{8,9},{9,8},{10,11... | collective-permute-start | bytes 4325384 | tf_op jit(solution)/shard_map/ppermute | solution.py:1076
  612.7 32.7 %collective-permute-start.72 = (bf16[128,2048]{1,0:T(8,128)(2,1)S(1)}, bf16[128,2048]{1,0:T(8,128)(2,1)S(1)}, u32[]{:S(2)}, u32[]{:S(2)}) collective-permute-start(bf16[128,2048]{1,0:T(8,128)(2,1)S(1)} %slice.641), channel_id=1, source_target_pairs={{0,1},{1,0},{2,3},{3,2},{4,5},{5,4},{6,7},{7,6},{8,9},{9,8},{10,11... | collective-permute-start | bytes 1572872 | tf_op jit(solution)/shard_map/ppermute | solution.py:1076
  614.2 35.9 %collective-permute-start.53 = (bf16[128,2048]{1,0:T(8,128)(2,1)S(1)}, bf16[128,2048]{1,0:T(8,128)(2,1)S(1)}, u32[]{:S(2)}, u32[]{:S(2)}) collective-permute-start(bf16[128,2048]{1,0:T(8,128)(2,1)S(1)} %slice.624), channel_id=1, source_target_pairs={{0,2},{1,3},{2,0},{3,1},{4,6},{5,7},{6,4},{7,5},{8,10},{9,11},{10,... | collective-permute-start | bytes 1572872 | tf_op jit(solution)/shard_map/ppermute | solution.py:1076
  646.7 11.8 %collective-permute-start.74 = (bf16[32,2048]{1,0:T(8,128)(2,1)S(1)}, bf16[32,2048]{1,0:T(8,128)(2,1)S(1)}, u32[]{:S(2)}, u32[]{:S(2)}) collective-permute-start(bf16[32,2048]{1,0:T(8,128)(2,1)S(1)} %get-tuple-element.280), channel_id=1, source_target_pairs={{0,16},{1,17},{2,18},{3,19},{4,20},{5,21},{6,22},{7,23},{8,24},{9,... | collective-permute-start | bytes 393224 | tf_op jit(solution)/shard_map/ppermute | solution.py:1076
  650.0 16.9 %collective-permute-start.73 = (bf16[32,2048]{1,0:T(8,128)(2,1)S(1)}, bf16[32,2048]{1,0:T(8,128)(2,1)S(1)}, u32[]{:S(2)}, u32[]{:S(2)}) collective-permute-start(bf16[32,2048]{1,0:T(8,128)(2,1)S(1)} %get-tuple-element.278), channel_id=1, source_target_pairs={{0,24},{1,25},{2,26},{3,27},{4,28},{5,29},{6,30},{7,31},{8,0},{9,1... | collective-permute-start | bytes 393224 | tf_op jit(solution)/shard_map/ppermute | solution.py:1076
  651.3 15.7 %collective-permute-start.56 = (bf16[32,2048]{1,0:T(8,128)(2,1)S(1)}, bf16[32,2048]{1,0:T(8,128)(2,1)S(1)}, u32[]{:S(2)}, u32[]{:S(2)}) collective-permute-start(bf16[32,2048]{1,0:T(8,128)(2,1)S(1)} %get-tuple-element.282), channel_id=1, source_target_pairs={{0,8},{1,9},{2,10},{3,11},{4,12},{5,13},{6,14},{7,15},{8,16},{9,17... | collective-permute-start | bytes 393224 | tf_op jit(solution)/shard_map/ppermute | solution.py:1076
  658.5 10.4 %collective-permute-start.55 = (bf16[32,2048]{1,0:T(8,128)(2,1)S(1)}, bf16[32,2048]{1,0:T(8,128)(2,1)S(1)}, u32[]{:S(2)}, u32[]{:S(2)}) collective-permute-start(bf16[32,2048]{1,0:T(8,128)(2,1)S(1)} %get-tuple-element.283), channel_id=1, source_target_pairs={{0,16},{1,17},{2,18},{3,19},{4,20},{5,21},{6,22},{7,23},{8,24},{9,... | collective-permute-start | bytes 393224 | tf_op jit(solution)/shard_map/ppermute | solution.py:1076
  680.4 34.8 %collective-permute-start.100 = (bf16[256,2816]{1,0:T(8,128)(2,1)}, bf16[256,2816]{1,0:T(8,128)(2,1)}, u32[]{:S(2)}, u32[]{:S(2)}) collective-permute-start(bf16[256,2816]{1,0:T(8,128)(2,1)} %get-tuple-element.197), channel_id=1, source_target_pairs={{0,1},{1,0},{2,3},{3,2},{4,5},{5,4},{6,7},{7,6},{8,9},{9,8},{10,11... | collective-permute-start | bytes 4325384 | tf_op jit(solution)/shard_map/ppermute | solution.py:1076
  688.7 39.6 %collective-permute-start.82 = (bf16[128,2816]{1,0:T(8,128)(2,1)S(1)}, bf16[128,2816]{1,0:T(8,128)(2,1)S(1)}, u32[]{:S(2)}, u32[]{:S(2)}) collective-permute-start(bf16[128,2816]{1,0:T(8,128)(2,1)S(1)} %slice.648), channel_id=1, source_target_pairs={{0,1},{1,0},{2,3},{3,2},{4,5},{5,4},{6,7},{7,6},{8,9},{9,8},{10,11... | collective-permute-start | bytes 2162696 | tf_op jit(solution)/shard_map/ppermute | solution.py:1076
  691.7 41.2 %collective-permute-start.91 = (bf16[128,2816]{1,0:T(8,128)(2,1)S(1)}, bf16[128,2816]{1,0:T(8,128)(2,1)S(1)}, u32[]{:S(2)}, u32[]{:S(2)}) collective-permute-start(bf16[128,2816]{1,0:T(8,128)(2,1)S(1)} %slice.654), channel_id=1, source_target_pairs={{0,2},{1,3},{2,0},{3,1},{4,6},{5,7},{6,4},{7,5},{8,10},{9,11},{10,... | collective-permute-start | bytes 2162696 | tf_op jit(solution)/shard_map/ppermute | solution.py:1076
  717.1 18.1 %collective-permute-start.101 = (bf16[128,2816]{1,0:T(8,128)(2,1)S(1)}, bf16[128,2816]{1,0:T(8,128)(2,1)S(1)}, u32[]{:S(2)}, u32[]{:S(2)}) collective-permute-start(bf16[128,2816]{1,0:T(8,128)(2,1)S(1)} %slice.661), channel_id=1, source_target_pairs={{0,2},{1,3},{2,0},{3,1},{4,6},{5,7},{6,4},{7,5},{8,10},{9,11},{10,... | collective-permute-start | bytes 2162696 | tf_op jit(solution)/shard_map/ppermute | solution.py:1076
  728.6 14.9 %collective-permute-start.85 = (bf16[32,2816]{1,0:T(8,128)(2,1)S(1)}, bf16[32,2816]{1,0:T(8,128)(2,1)S(1)}, u32[]{:S(2)}, u32[]{:S(2)}) collective-permute-start(bf16[32,2816]{1,0:T(8,128)(2,1)S(1)} %get-tuple-element.276), channel_id=1, source_target_pairs={{0,8},{1,9},{2,10},{3,11},{4,12},{5,13},{6,14},{7,15},{8,16},{9,17... | collective-permute-start | bytes 540680 | tf_op jit(solution)/shard_map/ppermute | solution.py:1076
  731.1 22.5 %collective-permute-start.84 = (bf16[32,2816]{1,0:T(8,128)(2,1)S(1)}, bf16[32,2816]{1,0:T(8,128)(2,1)S(1)}, u32[]{:S(2)}, u32[]{:S(2)}) collective-permute-start(bf16[32,2816]{1,0:T(8,128)(2,1)S(1)} %get-tuple-element.277), channel_id=1, source_target_pairs={{0,16},{1,17},{2,18},{3,19},{4,20},{5,21},{6,22},{7,23},{8,24},{9,... | collective-permute-start | bytes 540680 | tf_op jit(solution)/shard_map/ppermute | solution.py:1076
  732.6 23.0 %collective-permute-start.83 = (bf16[32,2816]{1,0:T(8,128)(2,1)S(1)}, bf16[32,2816]{1,0:T(8,128)(2,1)S(1)}, u32[]{:S(2)}, u32[]{:S(2)}) collective-permute-start(bf16[32,2816]{1,0:T(8,128)(2,1)S(1)} %get-tuple-element.275), channel_id=1, source_target_pairs={{0,24},{1,25},{2,26},{3,27},{4,28},{5,29},{6,30},{7,31},{8,0},{9,1... | collective-permute-start | bytes 540680 | tf_op jit(solution)/shard_map/ppermute | solution.py:1076
  733.2 25.8 %collective-permute-start.94 = (bf16[32,2816]{1,0:T(8,128)(2,1)S(1)}, bf16[32,2816]{1,0:T(8,128)(2,1)S(1)}, u32[]{:S(2)}, u32[]{:S(2)}) collective-permute-start(bf16[32,2816]{1,0:T(8,128)(2,1)S(1)} %get-tuple-element.273), channel_id=1, source_target_pairs={{0,8},{1,9},{2,10},{3,11},{4,12},{5,13},{6,14},{7,15},{8,16},{9,17... | collective-permute-start | bytes 540680 | tf_op jit(solution)/shard_map/ppermute | solution.py:1076
  735.2 34.0 %collective-permute-start.93 = (bf16[32,2816]{1,0:T(8,128)(2,1)S(1)}, bf16[32,2816]{1,0:T(8,128)(2,1)S(1)}, u32[]{:S(2)}, u32[]{:S(2)}) collective-permute-start(bf16[32,2816]{1,0:T(8,128)(2,1)S(1)} %get-tuple-element.274), channel_id=1, source_target_pairs={{0,16},{1,17},{2,18},{3,19},{4,20},{5,21},{6,22},{7,23},{8,24},{9,... | collective-permute-start | bytes 540680 | tf_op jit(solution)/shard_map/ppermute | solution.py:1076
  743.4 28.1 %collective-permute-start.92 = (bf16[32,2816]{1,0:T(8,128)(2,1)S(1)}, bf16[32,2816]{1,0:T(8,128)(2,1)S(1)}, u32[]{:S(2)}, u32[]{:S(2)}) collective-permute-start(bf16[32,2816]{1,0:T(8,128)(2,1)S(1)} %get-tuple-element.272), channel_id=1, source_target_pairs={{0,24},{1,25},{2,26},{3,27},{4,28},{5,29},{6,30},{7,31},{8,0},{9,1... | collective-permute-start | bytes 540680 | tf_op jit(solution)/shard_map/ppermute | solution.py:1076
  753.6 18.8 %collective-permute-start.104 = (bf16[32,2816]{1,0:T(8,128)(2,1)S(1)}, bf16[32,2816]{1,0:T(8,128)(2,1)S(1)}, u32[]{:S(2)}, u32[]{:S(2)}) collective-permute-start(bf16[32,2816]{1,0:T(8,128)(2,1)S(1)} %get-tuple-element.270), channel_id=1, source_target_pairs={{0,8},{1,9},{2,10},{3,11},{4,12},{5,13},{6,14},{7,15},{8,16},{9,17... | collective-permute-start | bytes 540680 | tf_op jit(solution)/shard_map/ppermute | solution.py:1076
  755.5 18.8 %collective-permute-start.103 = (bf16[32,2816]{1,0:T(8,128)(2,1)S(1)}, bf16[32,2816]{1,0:T(8,128)(2,1)S(1)}, u32[]{:S(2)}, u32[]{:S(2)}) collective-permute-start(bf16[32,2816]{1,0:T(8,128)(2,1)S(1)} %get-tuple-element.271), channel_id=1, source_target_pairs={{0,16},{1,17},{2,18},{3,19},{4,20},{5,21},{6,22},{7,23},{8,24},{9,... | collective-permute-start | bytes 540680 | tf_op jit(solution)/shard_map/ppermute | solution.py:1076
  759.0 18.2 %collective-permute-start.102 = (bf16[32,2816]{1,0:T(8,128)(2,1)S(1)}, bf16[32,2816]{1,0:T(8,128)(2,1)S(1)}, u32[]{:S(2)}, u32[]{:S(2)}) collective-permute-start(bf16[32,2816]{1,0:T(8,128)(2,1)S(1)} %get-tuple-element.269), channel_id=1, source_target_pairs={{0,24},{1,25},{2,26},{3,27},{4,28},{5,29},{6,30},{7,31},{8,0},{9,1... | collective-permute-start | bytes 540680 | tf_op jit(solution)/shard_map/ppermute | solution.py:1076
  769.2 9.3 %collective-permute-start.88 = (bf16[32,2816]{1,0:T(8,128)(2,1)S(1)}, bf16[32,2816]{1,0:T(8,128)(2,1)S(1)}, u32[]{:S(2)}, u32[]{:S(2)}) collective-permute-start(bf16[32,2816]{1,0:T(8,128)(2,1)S(1)} %fusion.29), channel_id=1, source_target_pairs={{0,3},{1,2},{2,1},{3,0},{4,7},{5,6},{6,5},{7,4},{8,11},{9,10},{10,... | collective-permute-start | bytes 540680 | tf_op jit(solution)/shard_map/ppermute | solution.py:1076
  771.5 9.0 %collective-permute-start.87 = (bf16[32,2816]{1,0:T(8,128)(2,1)S(1)}, bf16[32,2816]{1,0:T(8,128)(2,1)S(1)}, u32[]{:S(2)}, u32[]{:S(2)}) collective-permute-start(bf16[32,2816]{1,0:T(8,128)(2,1)S(1)} %fusion.29), channel_id=1, source_target_pairs={{0,2},{1,3},{2,0},{3,1},{4,6},{5,7},{6,4},{7,5},{8,10},{9,11},{10,... | collective-permute-start | bytes 540680 | tf_op jit(solution)/shard_map/ppermute | solution.py:1076
  774.4 10.1 %collective-permute-start.97 = (bf16[32,2816]{1,0:T(8,128)(2,1)S(1)}, bf16[32,2816]{1,0:T(8,128)(2,1)S(1)}, u32[]{:S(2)}, u32[]{:S(2)}) collective-permute-start(bf16[32,2816]{1,0:T(8,128)(2,1)S(1)} %fusion.26), channel_id=1, source_target_pairs={{0,3},{1,2},{2,1},{3,0},{4,7},{5,6},{6,5},{7,4},{8,11},{9,10},{10,... | collective-permute-start | bytes 540680 | tf_op jit(solution)/shard_map/ppermute | solution.py:1076
  777.3 11.4 %collective-permute-start.96 = (bf16[32,2816]{1,0:T(8,128)(2,1)S(1)}, bf16[32,2816]{1,0:T(8,128)(2,1)S(1)}, u32[]{:S(2)}, u32[]{:S(2)}) collective-permute-start(bf16[32,2816]{1,0:T(8,128)(2,1)S(1)} %fusion.26), channel_id=1, source_target_pairs={{0,2},{1,3},{2,0},{3,1},{4,6},{5,7},{6,4},{7,5},{8,10},{9,11},{10,... | collective-permute-start | bytes 540680 | tf_op jit(solution)/shard_map/ppermute | solution.py:1076
  778.6 10.1 %collective-permute-start.95 = (bf16[32,2816]{1,0:T(8,128)(2,1)S(1)}, bf16[32,2816]{1,0:T(8,128)(2,1)S(1)}, u32[]{:S(2)}, u32[]{:S(2)}) collective-permute-start(bf16[32,2816]{1,0:T(8,128)(2,1)S(1)} %fusion.26), channel_id=1, source_target_pairs={{0,1},{1,0},{2,3},{3,2},{4,5},{5,4},{6,7},{7,6},{8,9},{9,8},{10,11... | collective-permute-start | bytes 540680 | tf_op jit(solution)/shard_map/ppermute | solution.py:1076
  780.5 11.7 %collective-permute-start.107 = (bf16[32,2816]{1,0:T(8,128)(2,1)S(1)}, bf16[32,2816]{1,0:T(8,128)(2,1)S(1)}, u32[]{:S(2)}, u32[]{:S(2)}) collective-permute-start(bf16[32,2816]{1,0:T(8,128)(2,1)S(1)} %fusion.23), channel_id=1, source_target_pairs={{0,3},{1,2},{2,1},{3,0},{4,7},{5,6},{6,5},{7,4},{8,11},{9,10},{10,... | collective-permute-start | bytes 540680 | tf_op jit(solution)/shard_map/ppermute | solution.py:1076
  781.0 12.7 %collective-permute-start.106 = (bf16[32,2816]{1,0:T(8,128)(2,1)S(1)}, bf16[32,2816]{1,0:T(8,128)(2,1)S(1)}, u32[]{:S(2)}, u32[]{:S(2)}) collective-permute-start(bf16[32,2816]{1,0:T(8,128)(2,1)S(1)} %fusion.23), channel_id=1, source_target_pairs={{0,2},{1,3},{2,0},{3,1},{4,6},{5,7},{6,4},{7,5},{8,10},{9,11},{10,... | collective-permute-start | bytes 540680 | tf_op jit(solution)/shard_map/ppermute | solution.py:1076
  784.5 9.2 %collective-permute-start.105 = (bf16[32,2816]{1,0:T(8,128)(2,1)S(1)}, bf16[32,2816]{1,0:T(8,128)(2,1)S(1)}, u32[]{:S(2)}, u32[]{:S(2)}) collective-permute-start(bf16[32,2816]{1,0:T(8,128)(2,1)S(1)} %fusion.23), channel_id=1, source_target_pairs={{0,1},{1,0},{2,3},{3,2},{4,5},{5,4},{6,7},{7,6},{8,9},{9,8},{10,11... | collective-permute-start | bytes 540680 | tf_op jit(solution)/shard_map/ppermute | solution.py:1076
  (100 other events, 814.3 us)

commit v3 on v2

--- a/solution.py
+++ b/solution.py
@@ -105,49 +105,32 @@
     )(hidden, weights)
 
 
-def outer_kernel(*refs, skips, parts):
-    pairs = len(skips)
-    lefts, rights = refs[:pairs], refs[pairs : 2 * pairs]
-    outs, turned = refs[2 * pairs : -pairs], refs[-pairs:]
-
+def outer_kernel(left_ref, right_ref, out_ref, turn_ref, *, skip):
     @pl.when(pl.program_id(0) == 0)
     def _():
-        for left, scratch, (skip, _) in zip(lefts, turned, skips):
-            scratch[...] = jnp.transpose(left[skip:, :])
-
-    total = None
-    for scratch, right, (_, skip) in zip(turned, rights, skips):
-        term = mm(scratch[...], right[skip:, :])
-        total = term if total is None else total + term
-    total = total.astype(BF16)
-    for out, blocks in zip(outs, parts):
-        for slot, block in enumerate(blocks):
-            out[slot * LANES : (slot + 1) * LANES, :] = total[block * LANES : (block + 1) * LANES]
-
-
-def outer(lefts, rights, wide_rows, parts, skip_left=0, skip_right=0):
-    cols = rights[0].shape[1]
+        turn_ref[...] = jnp.transpose(left_ref[skip:, :])
+
+    out_ref[...] = mm(turn_ref[...], right_ref[...]).astype(BF16)
+
+
+def outer(left, right, skip):
+    rows, width = left.shape
+    cols = right.shape[1]
     block = next(b for b in (512, 256, 128) if cols % b == 0)
-    if cols == 1152:
-        block = 384
-    rows = [array.shape[0] for array, _ in lefts]
-    kept = rows[0] - skip_left
     return pl.pallas_call(
-        functools.partial(outer_kernel, skips=[(skip_left, skip_right)] * len(lefts), parts=parts),
+        functools.partial(outer_kernel, skip=skip),
         grid=(cols // block,),
         in_specs=[
-            pl.BlockSpec((n, wide_rows), lambda j, at=at: (0, at)) for n, (_, at) in zip(rows, lefts)
-        ]
-        + [pl.BlockSpec((right.shape[0], block), lambda j: (0, j)) for right in rights],
-        out_specs=[pl.BlockSpec((LANES * len(p), block), lambda j: (0, j)) for p in parts],
-        out_shape=[jax.ShapeDtypeStruct((LANES * len(p), cols), BF16) for p in parts],
-        scratch_shapes=[pltpu.VMEM((wide_rows, kept), BF16) for _ in lefts],
+            pl.BlockSpec((rows, width), lambda j: (0, 0)),
+            pl.BlockSpec((rows - skip, block), lambda j: (0, j)),
+        ],
+        out_specs=pl.BlockSpec((width, block), lambda j: (0, j)),
+        out_shape=jax.ShapeDtypeStruct((width, cols), BF16),
+        scratch_shapes=[pltpu.VMEM((width, rows - skip), BF16)],
         compiler_params=params(),
-        cost_estimate=cost(
-            2 * len(lefts) * kept * wide_rows * cols, 2 * (wide_rows + sum(rows)) * cols
-        ),
+        cost_estimate=cost(2 * rows * width * cols, 2 * width * cols + 2 * rows * cols),
         name="outer",
-    )(*[array for array, _ in lefts], *rights)
+    )(left, right)
 
 
 def gate_tables(logit_ref, par_ref, beta_ref, decay_ref, cum_ref):
@@ -560,18 +543,33 @@
     )(hidden, weights, taps, par, cols, segr)
 
 
-def backward_kernel(
-    place_ref, slot_ref, p_ref, taps_ref, logit_ref, par_ref, cols_ref, back_ref, segr_ref,
-    dattn_ref, sin_ref, exch_ref, grads_ref,
+def backward_kernel(place_ref, slot_ref, *refs):
+    grads_ref, refs = refs[10], refs[:10] + refs[11:]
+    exch_ref = refs[9]
+
+    def behind(source, grad):
+        slot = slot_ref[source]
+        return jnp.where(
+            source > place_ref[0],
+            grads_ref[slot, 0].astype(F32) + mm(exch_ref[slot, 0], grad, TN),
+            grad,
+        )
+
+    places = exch_ref.shape[0]
+    d_state = lax.fori_loop(
+        0, places - 1, lambda lap, grad: behind(places - 1 - lap, grad), jnp.zeros((DK, DV), F32)
+    )
+    backward_head(pl.program_id(0), d_state, *refs)
+
+
+def backward_head(
+    head, d_state, p_ref, taps_ref, logit_ref, par_ref, cols_ref, back_ref, segr_ref,
+    dattn_ref, sin_ref, exch_ref,
     inv_ref, upd_ref, st_ref, stm_ref, amap_ref, rmap_ref,
     dp_ref, dlogit_ref, dtaps_ref, dpar_ref,
-    beta_ref, decay_ref, cum_ref, pf_ref, pre_ref, dmix_ref, *, first
+    beta_ref, decay_ref, cum_ref, pf_ref, pre_ref, dmix_ref,
 ):
-    head = pl.program_id(0) + first
-    place = place_ref[0]
-    places = exch_ref.shape[0]
-
-    @pl.when(pl.program_id(0) == 0)
+    @pl.when(head == 0)
     def _():
         gate_tables(logit_ref, par_ref, beta_ref, decay_ref, cum_ref)
         dlogit_ref[...] = jnp.zeros_like(dlogit_ref)
@@ -584,16 +582,6 @@
     pre_ref[...] = pre
     beta = lane(beta_ref[...], head + H)
 
-    def behind(lap, grad):
-        source = places - 1 - lap
-        slot = slot_ref[source]
-        return jnp.where(
-            source > place,
-            grads_ref[slot, 0].astype(F32) + mm(exch_ref[slot, 0], grad, TN),
-            grad,
-        )
-
-    d_state = lax.fori_loop(0, places - 1, behind, jnp.zeros((DK, DV), F32))
     state_in = sin_ref[0]
     d_states = [None] * len(chunks)
     for c in reversed(chunks):
@@ -713,31 +701,31 @@
 
 
 def delta_backward(
-    first, heads, place, slots, proj, taps, logits, par, cols, back, segr, d_attn, state_in, exch, grads, saved
+    place, slots, proj, taps, logits, par, cols, back, segr, d_attn, state_in, exch, grads, saved
 ):
     rows = proj.shape[0]
     tokens = rows - HALO
     chunks = tokens // CHUNK
     places = exch.shape[0]
     whole = lambda shape: pl.BlockSpec(shape, lambda h: (0,) * len(shape))
-    by_head = lambda shape: pl.BlockSpec(shape, lambda h: (h + first,) + (0,) * (len(shape) - 1))
+    by_head = lambda shape: pl.BlockSpec(shape, lambda h: (h,) + (0,) * (len(shape) - 1))
     return pl.pallas_call(
-        functools.partial(backward_kernel, first=first),
-        grid=(heads,),
+        backward_kernel,
+        grid=(H,),
         in_specs=[
             pl.BlockSpec(memory_space=pltpu.SMEM),
             pl.BlockSpec(memory_space=pltpu.SMEM),
-            pl.BlockSpec((rows, HC), lambda h: (0, h + first)),
-            pl.BlockSpec((8, HC), lambda h: (0, h + first)),
+            pl.BlockSpec((rows, HC), lambda h: (0, h)),
+            pl.BlockSpec((8, HC), lambda h: (0, h)),
             whole((rows, LANES)),
             whole((8, LANES)),
             whole((tokens, LANES)),
             whole((rows, LANES)),
             whole((8, tokens)),
-            pl.BlockSpec((tokens, DV), lambda h: (0, h + first)),
+            pl.BlockSpec((tokens, DV), lambda h: (0, h)),
             by_head((1, DK, DV)),
-            pl.BlockSpec((places, 1, DK, DK), lambda h: (0, h + first, 0, DV // DK)),
-            pl.BlockSpec((places, 1, DK, DV), lambda h: (0, h + first, 0, 0)),
+            pl.BlockSpec((places, 1, DK, DK), lambda h: (0, h, 0, DV // DK)),
+            pl.BlockSpec((places, 1, DK, DV), lambda h: (0, h, 0, 0)),
             by_head((1, chunks, CHUNK, CHUNK)),
             by_head((1, tokens, DV + DK)),
             by_head((1, chunks, DK, DV)),
@@ -752,9 +740,9 @@
             whole((8, LANES)),
         ],
         out_shape=[
-            jax.ShapeDtypeStruct((rows, heads * HC), BF16),
+            jax.ShapeDtypeStruct((rows, H * HC), BF16),
             jax.ShapeDtypeStruct((tokens, LANES), F32),
-            jax.ShapeDtypeStruct((8, heads * HC), F32),
+            jax.ShapeDtypeStruct((8, H * HC), F32),
             jax.ShapeDtypeStruct((8, LANES), F32),
         ],
         scratch_shapes=[
@@ -766,7 +754,7 @@
             pltpu.VMEM((rows + 8, HC), F32),
         ],
         compiler_params=params(),
-        cost_estimate=cost(8e9 * heads, 5e6 * heads),
+        cost_estimate=cost(8e9 * H, 5e6 * H),
         name="delta_backward",
     )(place, slots, proj, taps, logits, par, cols, back, segr, d_attn, state_in, exch, grads, *saved)
 
@@ -908,7 +896,7 @@
 
 def ffn_kernel(
     h_ref, dout_ref, y_ref, gain_ref, wg_ref, wu_ref, wd_ref,
-    out_ref, act_ref, dg_ref, du_ref, dy_ref, dmix_ref, dgain_ref, res_ref, dh_ref,
+    out_ref, act_ref, dgu_ref, dy_ref, dmix_ref, dgain_ref, res_ref, dh_ref,
 ):
     step = pl.program_id(0)
 
@@ -928,8 +916,8 @@
     act_ref[...] = act
     d_gate = (d_act * up * slope * (1.0 + gate * (1.0 - slope))).astype(BF16)
     d_up = (d_act * swish).astype(BF16)
-    dg_ref[...] = d_gate
-    du_ref[...] = d_up
+    dgu_ref[0] = d_gate
+    dgu_ref[1] = d_up
     res_ref[...] += mm(act, w_down, NT)
     dh_ref[...] += mm(d_gate, w_gate, NT) + mm(d_up, w_up, NT)
 
@@ -967,14 +955,13 @@
         ]
         + [weight(AT_FFN + i * inner) for i in range(3)],
         out_specs=[
-            whole((tokens, width)), across, across, across,
+            whole((tokens, width)), across, pl.BlockSpec((2, tokens, block), lambda j: (0, 0, j)),
             whole((tokens, width)), whole((tokens, width)), whole((8, width)),
         ],
         out_shape=[
             jax.ShapeDtypeStruct((tokens, width), BF16),
             jax.ShapeDtypeStruct((tokens, inner), BF16),
-            jax.ShapeDtypeStruct((tokens, inner), BF16),
-            jax.ShapeDtypeStruct((tokens, inner), BF16),
+            jax.ShapeDtypeStruct((2, tokens, inner), BF16),
             jax.ShapeDtypeStruct((tokens, width), F32),
             jax.ShapeDtypeStruct((tokens, width), BF16),
             jax.ShapeDtypeStruct((8, width), F32),
@@ -986,23 +973,438 @@
     )(hidden, d_out, y1, gain, weights, weights, weights)
 
 
-def input_grad_kernel(*refs, groups, per_group):
-    dps, refs = refs[:groups], refs[groups:]
-    (dg_ref, dl_ref, w_ref, wl_ref, x_ref, gain_ref, dy_ref, turn_ref) = refs[:8]
-    out_ref, dgain_ref, acc_ref = refs[8:]
+BLOCK = HC
+LEAD, EVERY = 4, 3
+
+
+def other_index(step):
+    return step - jnp.clip((step - LEAD + EVERY - 1) // EVERY, 0, H)
+
+
+class Blocks:
+    def __init__(self, inner):
+        self.ups, self.downs = inner // (BLOCK // 2), inner // BLOCK
+        self.outs = H * DV // BLOCK
+        self.others = self.ups + self.downs + 2 * self.outs
+        self.count = self.others + H + 1
+        self.starts = [0, self.ups, self.ups + self.downs, self.ups + self.downs + self.outs, self.others]
+        self.tail = inner - self.downs * BLOCK
+        heads = [LEAD + EVERY * h for h in range(H)]
+        rest = [n for n in range(self.count - 1) if n not in heads]
+        parts = [rest[low:high] for low, high in zip(self.starts, self.starts[1:])]
+        self.up_at, self.down_at, self.out_at, self.gate_at = parts
+        self.head_at = heads
+
+    def index(self, kind):
+        low, high = self.starts[kind], self.starts[kind + 1]
+        return lambda s: jnp.clip(other_index(s) - low, 0, high - low - 1)
+
+
+def dot_blocks(left, right):
+    return lax.dot_general(left, right, (NN, ((), ())), preferred_element_type=F32)
+
+
+def flip_to(bit):
+    here = lax.axis_index("seq")
+    along_x = here + 1 - 2 * lax.rem(here, 2)
+    along_y = here + 2 - 4 * (here // 2)
+    return {"dp": lax.axis_index("dp"), "seq": (2 - bit) * along_x + (bit - 1) * along_y}
+
+
+def reduce_kernel(
+    dout_ref, hmid_ref, dres_ref, hidden_ref, act_ref, tail_ref, dgu_ref, gated_ref, dgpre_ref, lgrad_ref,
+    p_ref, taps_ref, logit_ref, par_ref, cols_ref, back_ref, segr_ref, dattn_ref, sin_ref, exch_ref,
+    inv_ref, upd_ref, st_ref, stm_ref, amap_ref, rmap_ref,
+    sum_ref, dp_ref, dlogit_ref, dtaps_ref, dpar_ref,
+    beta_ref, decay_ref, cum_ref, pf_ref, pre_ref, dmix_ref,
+    turn_ref, dps_ref, halo_ref, grads_ref,
+    core_keep, core_send, core_recv, near_keep, near_send, near_recv,
+    far_keep, far_send, far_recv, z_keep, z_send, z_recv, done_ref,
+    core_ss, core_rs, near_ss, near_rs, far_ss, far_rs, z_ss, z_rs, done_ss, done_rs, own_sem,
+    halo_ss, halo_rs, grads_ss, grads_rs, *, blocks,
+):
     step = pl.program_id(0)
+    steps = pl.num_programs(0)
+    place = lax.axis_index("seq")
+    count = blocks.count
+    half = core_keep.shape[1] * core_keep.shape[2]
+    quarter = half // SPOTS
+    piece = quarter // PLANES
+    mesh = dict(device_id_type=pl.DeviceIdType.MESH)
+
+    def remote(source, target, send, recv, to):
+        return pltpu.make_async_remote_copy(
+            src_ref=source, dst_ref=target, send_sem=send, recv_sem=recv, device_id=to, **mesh
+        )
+
+    def to_core(n):
+        slot = lax.rem(n, 2)
+        return remote(core_send.at[slot], core_recv.at[slot], core_ss.at[slot], core_rs.at[slot], device(core=1))
+
+    def to_near(n):
+        slot = lax.rem(n, 4)
+        return remote(
+            near_send.at[slot], near_recv.at[slot], near_ss.at[slot], near_rs.at[slot], flip_to(1 + lax.rem(n, 2))
+        )
+
+    def to_far(n):
+        slot = lax.rem(n, 4)
+        return remote(
+            far_send.at[slot], far_recv.at[slot], far_ss.at[slot], far_rs.at[slot], flip_to(2 - lax.rem(n, 2))
+        )
+
+    def along_z(n, d):
+        slot = lax.rem(n, 4)
+        return remote(
+            z_send.at[slot, d - 1], z_recv.at[slot, d - 1], z_ss.at[slot, d - 1], z_rs.at[slot, d - 1],
+            device(planes=PLANES - d),
+        )
+
+    def target(n):
+        return sum_ref.at[
+            pl.ds(pl.multiple_of(place * piece, piece), piece), pl.ds(pl.multiple_of(n * BLOCK, BLOCK), BLOCK)
+        ]
+
+    def spread(n, spot):
+        slot = lax.rem(n, 4)
+        return remote(
+            done_ref.at[slot], target(n), done_ss.at[slot, spot - 1], done_rs.at[n, spot - 1], device(spot=spot)
+        )
+
+    def keep(n):
+        slot = lax.rem(n, 4)
+        return pltpu.make_async_copy(done_ref.at[slot], target(n), own_sem.at[slot])
+
+    def give_grads(spot):
+        return remote(
+            lgrad_ref, grads_ref.at[spot - 1], grads_ss.at[spot - 1], grads_rs.at[spot - 1], device(spot=spot)
+        )
+
+    def give_halo(head):
+        to = {"dp": lax.axis_index("dp"), "seq": lax.rem(place + SPOTS - 1, SPOTS)}
+        return remote(dps_ref.at[0:HALO], halo_ref.at[head], halo_ss.at[head], halo_rs.at[head], to)
 
     @pl.when(step == 0)
     def _():
+        greet([dict(planes=d) for d in (1, 2, 3)] + [dict(spot=s) for s in (1, 2, 3)] + [dict(core=1)])
+        for spot in range(1, SPOTS):
+            give_grads(spot).start()
+        for at, ref in enumerate((dout_ref, hmid_ref, dres_ref)):
+            turn_ref[at] = jnp.transpose(ref[...])
+        turn_ref[3] = jnp.transpose(hidden_ref[HALO:, :])
+
+    def at_stage(lag, sent):
+        n = step - lag
+
+        def run(body):
+            @pl.when((n >= 0) & (n < count))
+            def _():
+                @pl.when(n >= sent)
+                def _():
+                    body(n, True)
+
+                body(n, False)
+
+        return run
+
+    @at_stage(7, 4)
+    def _(n, free):
+        if free:
+            for spot in range(1, SPOTS):
+                spread(n - 4, spot).wait_send()
+            keep(n - 4).wait()
+            return
+        slot = lax.rem(n, 4)
+        total = z_keep[slot]
+        for d in range(1, PLANES):
+            along_z(n, d).wait_recv()
+            total += z_recv[slot, d - 1].astype(F32)
+        done_ref[slot] = total.astype(BF16)
+        keep(n).start()
+        for spot in range(1, SPOTS):
+            spread(n, spot).start()
+
+    @at_stage(5, 4)
+    def _(n, free):
+        if free:
+            for d in range(1, PLANES):
+                along_z(n - 4, d).wait_send()
+            return
+        slot = lax.rem(n, 4)
+        to_far(n).wait_recv()
+        total = far_keep[slot] + far_recv[slot].astype(F32)
+        z_keep[slot] = total[:piece]
+        for d in range(1, PLANES):
+            z_send[slot, d - 1] = total[d * piece : (d + 1) * piece].astype(BF16)
+            along_z(n, d).start()
+
+    @at_stage(3, 4)
+    def _(n, free):
+        if free:
+            to_far(n - 4).wait_send()
+            return
+        slot = lax.rem(n, 4)
+        to_near(n).wait_recv()
+        far_keep[slot] = near_keep[slot, 0] + near_recv[slot, 0].astype(F32)
+        far_send[slot] = (near_keep[slot, 1] + near_recv[slot, 1].astype(F32)).astype(BF16)
+        to_far(n).start()
+
+    @at_stage(1, 4)
+    def _(n, free):
+        if free:
+            to_near(n - 4).wait_send()
+            return
+        slot, pair = lax.rem(n, 4), lax.rem(n, 2)
+        first = 1 + pair
+        to_core(n).wait_recv()
+        whole = lambda quarter: core_keep[pair, quarter] + core_recv[pair, quarter].astype(F32)
+        near_keep[slot, 0] = whole(0)
+        near_keep[slot, 1] = whole(3 - first)
+        near_send[slot, 0] = whole(first).astype(BF16)
+        near_send[slot, 1] = whole(3).astype(BF16)
+        to_near(n).start()
+
+    since = step - LEAD
+    heads_turn = (since >= 0) & (since < EVERY * H) & (lax.rem(jnp.maximum(since, 0), EVERY) == 0)
+    other = other_index(step)
+
+    def put(product):
+        pair = lax.rem(step, 2)
+
+        @pl.when(step >= 2)
+        def _():
+            to_core(step - 2).wait_send()
+
+        for q in range(SPOTS):
+            core_keep[pair, q] = product[q * quarter : (q + 1) * quarter]
+            core_send[pair, q] = product[half + q * quarter : half + (q + 1) * quarter].astype(BF16)
+        to_core(step).start()
+
+    def on(kind):
+        low, high = blocks.starts[kind], blocks.starts[kind + 1]
+        return pl.when((other >= low) & (other < high) & jnp.logical_not(heads_turn))
+
+    @on(0)
+    def _():
+        put(dot_blocks(turn_ref[1], jnp.concatenate([dgu_ref[0], dgu_ref[1]], axis=1)))
+
+    @on(1)
+    def _():
+        put(dot_blocks(turn_ref[0], act_ref[...]))
+
+    @on(2)
+    def _():
+        put(dot_blocks(turn_ref[2], gated_ref[...]))
+
+    @on(3)
+    def _():
+        put(dot_blocks(turn_ref[3], dgpre_ref[...]))
+
+    @pl.when(step == count - 1)
+    def _():
+        down = dot_blocks(turn_ref[0], tail_ref[...])
+        gates = dot_blocks(turn_ref[3], dlogit_ref[...].astype(BF16))
+        rest = jnp.zeros((down.shape[0], BLOCK - down.shape[1] - LANES), F32)
+        put(jnp.concatenate([down, gates, rest], axis=1))
+
+    @pl.when(heads_turn)
+    def _():
+        head = since // EVERY
+
+        @pl.when(place > 0)
+        def _():
+            give_halo(head).wait_send()
+
+        @pl.when(place < SPOTS - 1)
+        def _():
+            give_halo(head).wait_recv()
+            tokens = dps_ref.shape[0] - HALO
+            dps_ref[tokens:, :] = (
+                dps_ref[tokens:, :].astype(F32) + halo_ref[head].astype(F32)
+            ).astype(BF16)
+
+        value = dps_ref[HALO:, :]
+        dp_ref[...] = value
+        put(dot_blocks(turn_ref[3], value))
+
+    @pl.when((since >= -1) & (since < EVERY * H - 1) & (lax.rem(jnp.maximum(since + 1, 0), EVERY) == 0))
+    def _():
+        head = (since + 1) // EVERY
+
+        @pl.when(head == 0)
+        def _():
+            for spot in range(1, SPOTS):
+                give_grads(spot).wait()
+
+        d_state = jnp.zeros((DK, DV), F32)
+        for source in range(SPOTS - 1, 0, -1):
+            low = lax.rem(place, 2) * (1 - 2 * (source % 2)) + source % 2
+            high = (place // 2) * (1 - 2 * (source // 2)) + source // 2
+            slot = low + 2 * high
+            grads = grads_ref[jnp.maximum(slot - 1, 0), head].astype(F32)
+            d_state = jnp.where(source > place, grads + mm(exch_ref[slot, 0], d_state, TN), d_state)
+        backward_head(
+            head, d_state, p_ref, taps_ref, logit_ref, par_ref, cols_ref, back_ref, segr_ref,
+            dattn_ref, sin_ref, exch_ref, inv_ref, upd_ref, st_ref, stm_ref, amap_ref, rmap_ref,
+            dps_ref, dlogit_ref, dtaps_ref, dpar_ref, beta_ref, decay_ref, cum_ref, pf_ref, pre_ref, dmix_ref,
+        )
+
+        @pl.when(place > 0)
+        def _():
+            give_halo(head).start()
+
+    @pl.when(step == steps - 1)
+    def _():
+        for n in range(count - 4, count):
+            if n >= count - 2:
+                to_core(n).wait_send()
+            to_near(n).wait_send()
+            to_far(n).wait_send()
+            for d in range(1, PLANES):
+                along_z(n, d).wait_send()
+            for spot in range(1, SPOTS):
+                spread(n, spot).wait_send()
+            keep(n).wait()
+
+        def arrived(n, carry):
+            for spot in range(1, SPOTS):
+                spread(n, spot).wait_recv()
+            return carry
+
+        lax.fori_loop(0, count, arrived, 0)
+
+
+def reduce_gradients(
+    d_out, hidden_mid, d_mixer, hidden, act, d_gu, gated, d_gpre, local_grad,
+    proj, taps, logits, par, cols, back, segr, d_attn, state_in, exch, saved,
+):
+    tokens, width = d_out.shape
+    rows = hidden.shape[0]
+    chunks = tokens // CHUNK
+    blocks = Blocks(act.shape[1])
+    half = width // CORES
+    quarter = half // SPOTS
+    piece = quarter // PLANES
+    whole = lambda shape: pl.BlockSpec(shape, lambda s: (0,) * len(shape))
+    coming = lambda s: jnp.clip((s + EVERY - LEAD) // EVERY, 0, H - 1)
+    running = lambda s: jnp.clip((s + 1 - LEAD) // EVERY, 0, H - 1)
+    leaving = lambda s: jnp.clip((s - LEAD) // EVERY, 0, H - 1)
+    by_head = lambda shape: pl.BlockSpec(shape, lambda s: (coming(s),) + (0,) * (len(shape) - 1))
+    across = lambda shape, at: pl.BlockSpec(shape, lambda s: (0, at(s)))
+    sem = pltpu.SemaphoreType.DMA
+    up, down, out, gate = (blocks.index(kind) for kind in range(4))
+    return blocks, pl.pallas_call(
+        functools.partial(reduce_kernel, blocks=blocks),
+        grid=(blocks.count + 7,),
+        in_specs=[
+            whole((tokens, width)),
+            whole((tokens, width)),
+            whole((tokens, width)),
+            whole((rows, width)),
+            across((tokens, BLOCK), down),
+            pl.BlockSpec((tokens, blocks.tail), lambda s: (0, blocks.downs * BLOCK // blocks.tail)),
+            pl.BlockSpec((2, tokens, BLOCK // 2), lambda s: (0, 0, up(s))),
+            across((tokens, BLOCK), out),
+            across((tokens, BLOCK), gate),
+            whole((H, DK, DV)),
+            across((rows, HC), coming),
+            across((8, HC), coming),
+            whole((rows, LANES)),
+            whole((8, LANES)),
+            whole((tokens, LANES)),
+            whole((rows, LANES)),
+            whole((8, tokens)),
+            across((tokens, DV), coming),
+            by_head((1, DK, DV)),
+            pl.BlockSpec((SPOTS, 1, DK, DK), lambda s: (0, coming(s), 0, DV // DK)),
+            by_head((1, chunks, CHUNK, CHUNK)),
+            by_head((1, tokens, DV + DK)),
+            by_head((1, chunks, DK, DV)),
+            by_head((1, chunks, DK, DK)),
+            by_head((1, chunks, DK, DK)),
+            by_head((1, chunks, CHUNK, DK)),
+        ],
+        out_specs=[
+            pl.BlockSpec(memory_space=pl.ANY),
+            across((tokens, HC), leaving),
+            whole((tokens, LANES)),
+            across((8, HC), running),
+            whole((8, LANES)),
+        ],
+        out_shape=[
+            jax.ShapeDtypeStruct((SPOTS * piece, blocks.count * BLOCK), BF16),
+            jax.ShapeDtypeStruct((tokens, H * HC), BF16),
+            jax.ShapeDtypeStruct((tokens, LANES), F32),
+            jax.ShapeDtypeStruct((8, H * HC), F32),
+            jax.ShapeDtypeStruct((8, LANES), F32),
+        ],
+        scratch_shapes=[
+            pltpu.VMEM((tokens, LANES), F32),
+            pltpu.VMEM((tokens, LANES), F32),
+            pltpu.VMEM((tokens, LANES), F32),
+            pltpu.VMEM((rows, HC), F32),
+            pltpu.VMEM((tokens, HC), F32),
+            pltpu.VMEM((rows + 8, HC), F32),
+            pltpu.VMEM((4, width, tokens), BF16),
+            pltpu.VMEM((rows, HC), BF16),
+            pltpu.VMEM((H, HALO, HC), BF16),
+            pltpu.VMEM((SPOTS - 1, H, DK, DV), BF16),
+            pltpu.VMEM((2, SPOTS, quarter, BLOCK), F32),
+            pltpu.VMEM((2, SPOTS, quarter, BLOCK), BF16),
+            pltpu.VMEM((2, SPOTS, quarter, BLOCK), BF16),
+            pltpu.VMEM((4, 2, quarter, BLOCK), F32),
+            pltpu.VMEM((4, 2, quarter, BLOCK), BF16),
+            pltpu.VMEM((4, 2, quarter, BLOCK), BF16),
+            pltpu.VMEM((4, quarter, BLOCK), F32),
+            pltpu.VMEM((4, quarter, BLOCK), BF16),
+            pltpu.VMEM((4, quarter, BLOCK), BF16),
+            pltpu.VMEM((4, piece, BLOCK), F32),
+            pltpu.VMEM((4, PLANES - 1, piece, BLOCK), BF16),
+            pltpu.VMEM((4, PLANES - 1, piece, BLOCK), BF16),
+            pltpu.VMEM((4, piece, BLOCK), BF16),
+            sem((2,)), sem((2,)), sem((4,)), sem((4,)), sem((4,)), sem((4,)),
+            sem((4, PLANES - 1)), sem((4, PLANES - 1)),
+            sem((4, SPOTS - 1)), sem((blocks.count, SPOTS - 1)), sem((4,)),
+            sem((H,)), sem((H,)), sem((SPOTS - 1,)), sem((SPOTS - 1,)),
+        ],
+        compiler_params=params(collective_id=1, has_side_effects=True),
+        cost_estimate=cost(1e11, 1e8),
+        name="reduce_gradients",
+    )(
+        d_out, hidden_mid, d_mixer, hidden, act, act, d_gu, gated, d_gpre, local_grad,
+        proj, taps, logits, par, cols, back, segr, d_attn, state_in, exch, *saved,
+    )
+
+
+def unpack_gradients(blocks, sums):
+    sums = sums.astype(F32)
+    part = lambda n, low, high: sums[:, n * BLOCK + low : n * BLOCK + high]
+    join = lambda at, low=0, high=BLOCK: jnp.concatenate([part(n, low, high) for n in at], axis=1)
+    last = blocks.count - 1
+    heads = [from_heads(part(n, 0, BLOCK), 1) for n in blocks.head_at]
+    query, key, value = (jnp.concatenate(parts, axis=1) for parts in zip(*heads))
+    down = jnp.concatenate([join(blocks.down_at), part(last, 0, blocks.tail)], axis=1)
+    logits = part(last, blocks.tail, blocks.tail + 2 * H)
+    return (
+        query, key, value, join(blocks.gate_at), logits, join(blocks.out_at),
+        join(blocks.up_at, 0, BLOCK // 2), join(blocks.up_at, BLOCK // 2, BLOCK), down,
+    )
+
+
+def input_grad_kernel(
+    dp_ref, dg_ref, dl_ref, w_ref, wl_ref, x_ref, gain_ref, dy_ref, turn_ref, out_ref, dgain_ref, acc_ref
+):
+    step = pl.program_id(0)
+
+    @pl.when(step == 0)
+    def _():
         acc_ref[...] = mm(dl_ref[...], wl_ref[...], NT)
 
-    for g in range(groups):
-
-        @pl.when(step // per_group == g)
-        def _(g=g):
-            acc_ref[...] += mm(dps[g][HALO:, :], w_ref[...], NT)
-
-    @pl.when(step >= groups * per_group)
+    @pl.when(step < H)
+    def _():
+        acc_ref[...] += mm(dp_ref[...], w_ref[...], NT)
+
+    @pl.when(step >= H)
     def _():
         acc_ref[...] += mm(dg_ref[...], w_ref[...], NT)
 
@@ -1022,19 +1424,16 @@
         out_ref[...] = mm(high, turn_ref[...], NT) + mm(low, turn_ref[...], NT)
 
 
-def input_grad(d_projs, d_gpre, d_logit, weights, x, gain, d_y, turn):
+def input_grad(d_proj, d_gpre, d_logit, weights, x, gain, d_y, turn):
     tokens, width = x.shape
-    rows = d_projs[0].shape[0]
     block = HC
-    groups = len(d_projs)
-    per_group, second = d_projs[0].shape[1] // block, d_gpre.shape[1] // block
+    second = d_gpre.shape[1] // block
     steps = H + second
     whole = lambda shape: pl.BlockSpec(shape, lambda j: (0,) * len(shape))
-    at = lambda g: lambda j: (0, jnp.clip(j - g * per_group, 0, per_group - 1))
     late = lambda j: (0, jnp.maximum(j - H, 0))
     weight = lambda j: (0, jnp.where(j < H, H - 1 - j, j - H + AT_GATE // block))
-    in_specs = [pl.BlockSpec((rows, block), at(g)) for g in range(groups)]
-    in_specs += [
+    in_specs = [
+        pl.BlockSpec((tokens, block), lambda j: (0, jnp.minimum(j, H - 1))),
         pl.BlockSpec((tokens, block), late),
         whole((tokens, LANES)),
         pl.BlockSpec((width, block), weight),
@@ -1045,7 +1444,7 @@
         whole((width, width)),
     ]
     return pl.pallas_call(
-        functools.partial(input_grad_kernel, groups=groups, per_group=per_group),
+        input_grad_kernel,
         grid=(steps,),
         in_specs=in_specs,
         out_specs=[whole((tokens, width)), whole((8, width))],
@@ -1057,7 +1456,7 @@
         compiler_params=params(),
         cost_estimate=cost(2 * tokens * width * steps * block, 3e7),
         name="input_grad",
-    )(*d_projs, d_gpre, d_logit, weights, weights, x, gain, d_y, turn)
+    )(d_proj, d_gpre, d_logit, weights, weights, x, gain, d_y, turn)
 
 
 def shifted(block, axis, distance):
@@ -1114,37 +1513,6 @@
         rows, cols = shard.shape
         return flipped(shard.reshape(SPOTS, rows // SPOTS, cols), self.spot).reshape(rows, cols)
 
-    def others(self, value):
-        return send(value, core=1)
-
-    def left(self, value):
-        half = value.shape[1] // 2
-        return [(value, 0), (self.others(value[:, half:]), 0)]
-
-    def right(self, value):
-        return [value, self.others(value)]
-
-    def reduce(self, left, right, turned, skip_left=0, skip_right=0):
-        first, second = (1, 2) if turned else (2, 1)
-        width = left[0][0].shape[1] // 2
-        kept, sent = outer(left, right, width, [(0, second), (first, 3)], skip_left, skip_right)
-        size = kept.shape[0] // 2
-        total = kept.astype(F32) + send(sent, spot=first).astype(F32)
-        near, far = total[:size].astype(BF16), total[size:].astype(BF16)
-        total = near.astype(F32) + send(far, spot=second).astype(F32)
-        piece = size // PLANES
-        parts = [total[d * piece : (d + 1) * piece] for d in range(PLANES)]
-        total = parts[0]
-        for d in range(1, PLANES):
-            total += send(parts[d].astype(BF16), planes=-d).astype(F32)
-        total = total.astype(BF16)
-        spread = [total] + [send(total, spot=s) for s in range(1, SPOTS)]
-        stack = flipped(jnp.stack(spread), self.spot)
-        return stack.reshape(SPOTS * piece, -1).astype(F32)
-
-    def along(self, value):
-        return jnp.stack([value] + [send(value, spot=s) for s in range(1, SPOTS)])
-
     def total(self, value):
         value = value + send(value, core=1)
         value = value + send(value, spot=1)
@@ -1165,15 +1533,8 @@
     def share(self, shard):
         return lax.all_gather(shard, "dp", axis=0, tiled=True)
 
-    def left(self, value):
-        return [(value, 0)]
-
-    def right(self, value):
-        return [value]
-
-    def reduce(self, left, right, turned, skip_left=0, skip_right=0):
-        width = left[0][0].shape[1]
-        (full,) = outer(left, right, width, [tuple(range(width // LANES))], skip_left, skip_right)
+    def reduce(self, left, right, skip_left=0):
+        full = outer(left, right, skip_left)
         part = lax.psum_scatter(full, "dp", scatter_dimension=0, tiled=True)
         return lax.psum(part, "seq").astype(F32)
 
@@ -1190,13 +1551,13 @@
     return jnp.concatenate(parts, axis=-1).reshape(lead + (H * HC,))
 
 
-def from_heads(value):
+def from_heads(value, heads=H):
     lead = value.shape[:-1]
-    parts = value.reshape(lead + (H, HC))
+    parts = value.reshape(lead + (heads, HC))
     return (
-        parts[..., :DK].reshape(lead + (H * DK,)),
-        parts[..., DK : 2 * DK].reshape(lead + (H * DK,)),
-        parts[..., 2 * DK :].reshape(lead + (H * DV,)),
+        parts[..., :DK].reshape(lead + (heads * DK,)),
+        parts[..., DK : 2 * DK].reshape(lead + (heads * DK,)),
+        parts[..., 2 * DK :].reshape(lead + (heads * DV,)),
     )
 
 
@@ -1275,41 +1636,38 @@
     state_in, attn, gated, y1, hidden_mid = mixer_out(
         place_arr, slots, part, resp, exch, gpre, gain_out, weights, x, gain_ffn
     )
-    result, act, d_gate, d_up, d_y, d_mixer, d_gain_ffn = feed_forward(
+    result, act, d_gu, d_y, d_mixer, d_gain_ffn = feed_forward(
         hidden_mid, d_out, y1, gain_ffn, weights, inner
     )
     d_attn, d_gpre, local_grad, d_gain_out = mixer_back(d_mixer, weights, attn, gpre, gain_out, resp)
-    grads = comm.along(local_grad)
-
-    left_mid, left_out = comm.left(hidden_mid), comm.left(d_out)
-    g_down = comm.reduce(left_out, comm.right(act), True)
-    g_gate = comm.reduce(left_mid, comm.right(d_gate), False)
-    g_up = comm.reduce(left_mid, comm.right(d_up), True)
-    g_out = comm.reduce(comm.left(d_mixer), comm.right(gated), False)
-    left_in = comm.left(hidden)
-    g_og = comm.reduce(left_in, comm.right(d_gpre), True, HALO, 0)
-    heads = 2
-    groups = H // heads
-    d_projs, d_taps, d_logits, d_par, g_heads = [], [], 0.0, 0.0, []
-    for g in range(groups):
-        d_proj, d_logit, d_tap, d_pars = delta_backward(
-            g * heads, heads, place_arr, slots, proj, taps, logits, par, cols, back, segr,
-            d_attn, state_in, exch, grads, saved,
+    if planned:
+        blocks, outs = reduce_gradients(
+            d_out, hidden_mid, d_mixer, hidden, act, d_gu, gated, d_gpre, local_grad,
+            proj, taps, logits, par, cols, back, segr, d_attn, state_in, exch, saved,
+        )
+        sums, d_proj, d_logits, d_taps, d_par = outs
+        d_logit = low(d_logits)
+        g_query, g_key, g_value, g_og, g_gates, g_out, g_gate, g_up, g_down = unpack_gradients(blocks, sums)
+    else:
+        grads = comm.along(local_grad)
+        d_proj, d_logits, d_taps, d_par = delta_backward(
+            place_arr, slots, proj, taps, logits, par, cols, back, segr, d_attn, state_in, exch, grads, saved
         )
         sent_back = shifted(d_proj[:HALO], "seq", -1)
-        d_proj = d_proj.at[tokens:].add(sent_back)
-        d_projs.append(d_proj)
-        d_taps.append(d_tap)
-        d_logits, d_par = d_logits + d_logit, d_par + d_pars
-        g_heads.append(comm.reduce(left_in, comm.right(d_proj), g % 2 == 0, HALO, HALO))
-    d_logit = low(d_logits)
-    g_gates = comm.reduce(left_in, comm.right(d_logit), False, HALO, 0)
+        d_proj = d_proj.at[tokens:].add(sent_back)[HALO:]
+        d_logit = low(d_logits)
+        g_down = comm.reduce(d_out, act)
+        g_gate = comm.reduce(hidden_mid, d_gu[0])
+        g_up = comm.reduce(hidden_mid, d_gu[1])
+        g_out = comm.reduce(d_mixer, gated)
+        g_og = comm.reduce(hidden, d_gpre, HALO)
+        g_query, g_key, g_value = from_heads(comm.reduce(hidden, d_proj, HALO))
+        g_gates = comm.reduce(hidden, d_logit, HALO)[:, : 2 * H]
     d_inputs, d_gain_mix = input_grad(
-        d_projs, d_gpre, d_logit, weights, x, gain_mix, d_y, comm.turn
+        d_proj, d_gpre, d_logit, weights, x, gain_mix, d_y, comm.turn
     )
 
-    g_query, g_key, g_value = from_heads(jnp.concatenate(g_heads, axis=1))
-    d_conv = jnp.concatenate(from_heads(jnp.concatenate(d_taps, axis=1)[:CONV]), axis=1)
+    d_conv = jnp.concatenate(from_heads(d_taps[:CONV]), axis=1)
     pieces = [
         comm.vector_back(d_gain_mix[0]), d_conv.reshape(-1), d_par[0, :H], d_par[1, :H],
         d_gain_out[0], comm.vector_back(d_gain_ffn[0]),
@@ -1322,7 +1680,7 @@
         at += one.shape[0]
     return (
         comm.natural(result)[None], d_inputs[None], small[0], g_query, g_key, g_value, g_og,
-        g_gates[:, : 2 * H], small[1].reshape(d_conv.shape), small[2], small[3], small[4], g_out.T,
+        g_gates, small[1].reshape(d_conv.shape), small[2], small[3], small[4], g_out.T,
         small[5], g_gate, g_up, g_down.T,
     )
 

time: 806 us -> 629 us (0.78)
  waiting for transfers between devices: 174 us -> 6.45 us
  starting transfers between devices: 135 us -> 10 us
  Pallas kernels: 379 us -> 498 us
  other arithmetic: 43.6 us -> 20.6 us
  local copies, waits for them, and re-layouts: 50.3 us -> 67.5 us
    ppermute x103 -> x6, waiting for transfers between devices: 169 us -> 6.45 us  [send(): return lax.ppermute(value, ('dp', 'seq'), route)]
    ppermute x103 -> x6, starting transfers between devices: 126 us -> 6.64 us  [send(): return lax.ppermute(value, ('dp', 'seq'), route)]
    pallas_call x15 -> x2, Pallas kernels: 150 us -> 260 us  [the longest x1 239 us: reduce_gradients(): pl.pallas_call(functools.partial(reduce_kernel, blocks=blocks), grid=(blo...]
    another operation x31 -> x0, other arithmetic: 12.5 us -> none
    unnamed x143 -> x144, local copies, waits for them, and re-layouts: 19.7 us -> 30.9 us
    pallas_call x1, Pallas kernels: 165 us -> 175 us  [delta_forward(): pl.pallas_call(functools.partial(forward_kernel, planned=planned, spans=s...]
  transfers between devices with their start and end apart: 108 -> 7, of which waited for: 51 -> 2; matrix products, arithmetic and copies ran while one was open for 12% -> 11% of each run, Pallas kernels for 19% -> 0%
where the time goes in v3:
time: 629 us; the launch traced here: 617 us
  Pallas kernels  498 us (79%)
  local copies, waits for them, and re-layouts  67.5 us (11%)
  other arithmetic  20.6 us (3%)
  matrix products  12.1 us (2%)
  starting transfers between devices  10 us (2%)
  waiting for transfers between devices  6.45 us (1%)
    pallas_call x1, Pallas kernels, reduce_gradients(): pl.pallas_call(functools.partial(reduce_kernel, blocks=blocks), grid=(blo...  239 us
    pallas_call x1, Pallas kernels, delta_forward(): pl.pallas_call(functools.partial(forward_kernel, planned=planned, spans=s...  175 us
    unnamed x144, local copies, waits for them, and re-layouts  30.9 us
    pallas_call x1, Pallas kernels, feed_forward(): pl.pallas_call(ffn_kernel, grid=(inner // block,), in_specs=[whole((token...  28.2 us
    pallas_call x1, Pallas kernels, input_grad(): pl.pallas_call(input_grad_kernel, grid=(steps,), in_specs=in_specs, out_s...  21.2 us
    pallas_call x1, Pallas kernels, mixer_out(): pl.pallas_call(mixer_kernel, grid=(H,), in_specs=[pl.BlockSpec(memory_spa...  16.8 us
  transfers between devices with their start and end apart: 7, of which 2 were waited for; matrix products, arithmetic and copies ran while one was open for 11% of the time, Pallas kernels for 0%

profile of v3, /device:TPU:8, one launch (start us, length us, event | category | flops | bytes accessed | tf_op | source)
XLA Modules:
  0.0 616.8 jit_solution(3865060618862148602)
XLA Ops:
  0.7 0.9 slice_bitcast_fusion.33
  1.6 3.4 collective-permute-start
  5.0 0.8 concatenate.50
  7.0 1.3 convert_element_type.80
  14.9 1.6 copy.80
  16.7 4.5 gather_fusion
  21.3 4.5 gather_fusion.1
  25.9 2.2 fusion.2.turn_ref
  28.1 2.3 fusion.14.dout_ref
  31.0 0.9 convert_dynamic-update-slice_fusion.2
  31.9 0.8 bitcast_dynamic-update-slice_fusion.1
  32.8 1.0 convert_dynamic-update-slice_fusion.1
  33.7 1.0 convert_dynamic-update-slice_fusion
  34.7 1.0 bitcast_dynamic-update-slice_fusion
  35.7 4.6 reverse_select_fusion.1
  40.3 2.8 reverse_select_fusion
  45.3 0.9 copy.86
  46.2 0.9 copy.87
  47.1 0.9 copy.82
  49.2 1.5 stack.111.back_ref
  50.9 2.6 stack.99.refs_4_.cols_ref
  53.5 1.5 fusion.6
  55.0 1.0 slice.431.x_ref
  56.0 1.3 fusion.8.refs_0_.h_ref.hidden_ref
  57.9 174.8 %delta_forward.1 = (bf16[1024,17152]{1,0:T(8,128)(2,1)}, bf16[528,4096]{1,0:T(8,128)(2,1)}, f32[528,128]{1,0:T(8,128)}, f32[512,2048]{1,0:T(8,128)}, bf16[512,10...) custom-call(bf16[528,1024]{1,0:T(8,128)(2,1)} %fusion.8.refs_0_.h_re, ...), custom_call_target="tpu_custom_call" | custom-call | flops 48000000000 | bytes 40000000 | tf_op jit(solution)/shard_map/delta_forward/pallas_call | solution.py:526
  232.7 6.4 %outgate.1.gpre_ref = f32[512,2048]{1,0:T(8,128)} custom-call(bf16[528,1024]{1,0:T(8,128)(2,1)} %fusion.8.refs_0_.h_ref.hidden_ref, bf16[1024,17152]{1,0:T(8,128)(2,1)} %get-tuple-element.55.w_ref.wg_ref.wu_ref.wd_ref.wl_ref), custom_call_target="tpu_custom_call" | custom-call | flops 2214592512 | bytes 8519680 | tf_op jit(solution)/shard_map/outgate/pallas_call | solution.py:93
  239.1 16.8 %mixer_out.1 = (f32[8,128,256]{2,1,0:T(8,128)}, f32[512,2048]{1,0:T(8,128)}, bf16[512,2048]{1,0:T(8,128)(2,1)}, f32[512,1024]{1,0:T(8,128)}, bf16[512,1024]{1,0:T(8,128)(2,1)}) custom-call(s32[1]{0:T(128)} %bitcast.place_ref, s32[4]{0:T(128)} %iota_xor_fusion.slot_ref, f32[512,2048]{1,0:T(8,128)} %get-tuple-element.52.part_ref, ...), custom_call_target="tpu_custom_call" | custom-call | flops 2147483648 | bytes 20000000 | tf_op jit(solution)/shard_map/mixer_out/pallas_call | solution.py:804
  256.0 28.2 %feed_forward.1 = (bf16[512,1024]{1,0:T(8,128)(2,1)}, bf16[512,2816]{1,0:T(8,128)(2,1)}, bf16[2,512,2816]{2,1,0:T(8,128)(2,1)}, f32[512,1024]{1,0:T(8,128)}, bf1...) custom-call(bf16[512,1024]{1,0:T(8,128)(2,1)} %get-tuple-element.56.h_ref.hmid_ref, bf16[512,1024]{1,0:T(8,128)(2,1)} %fusion.14.dout_ref, ...), custom_call_target="tpu_custom_call" | custom-call | flops 17716740096 | bytes 30000000 | tf_op jit(solution)/shard_map/feed_forward/pallas_call | solution.py:947
  284.2 11.7 %mixer_back.1 = (bf16[512,2048]{1,0:T(8,128)(2,1)}, bf16[512,2048]{1,0:T(8,128)(2,1)}, bf16[8,128,256]{2,1,0:T(8,128)(2,1)}, f32[8,256]{1,0:T(8,128)}) custom-call(bf16[512,1024]{1,0:T(8,128)(2,1)} %get-tuple-element.59.dmix_ref.dres_ref, bf16[1024,17152]{1,0:T(8,128)(2,1)} %get-tuple-element.55.w_ref.wg_ref.wu_ref.wd_ref.wl_ref, ...), custom_call_target="tpu_custom_call" | custom-call | flops 2147483648 | bytes 20000000 | tf_op jit(solution)/shard_map/mixer_back/pallas_call | solution.py:868
  295.9 239.2 %reduce_gradients.1 = (bf16[128,16896]{1,0:T(8,128)(2,1)}, bf16[512,4096]{1,0:T(8,128)(2,1)}, f32[512,128]{1,0:T(8,128)}, f32[8,4096]{1,0:T(8,128)}, f32[8,128]{1,0:T(8,128)}) custom-call(bf16[512,1024]{1,0:T(8,128)(2,1)} %fusion.14.dout_ref, bf16[512,1024]{1,0:T(8,128)(2,1)} %get-tuple-element.56.h_ref.hmid_ref, ...), custom_call_target="tpu_custom_call" | custom-call | flops 99999997952 | bytes 100000000 | tf_op jit(solution)/shard_map/reduce_gradients/pallas_call | solution.py:1296
  535.1 1.6 fusion.65
  536.7 1.6 slice.499
  539.0 0.9 convert_element_type.94
  539.9 0.8 slice_dynamic-update-slice_fusion.10
  540.6 2.7 copy-done.4
  543.3 1.2 slice_bitcast_fusion
  546.7 21.2 %input_grad.1 = (f32[512,1024]{1,0:T(8,128)}, f32[8,1024]{1,0:T(8,128)}) custom-call(bf16[512,4096]{1,0:T(8,128)(2,1)} %get-tuple-element.76.dp_ref, bf16[512,2048]{1,0:T(8,128)(2,1)} %get-tuple-element.64.dgpre_ref.dg_ref, bf16[512,128]{1,0:T(8,128)(2,1)} %convert_element_type.92.dl_ref, ...), custom_call_target="tpu_custom_call" | custom-call | flops 6442450944 | bytes 30000000 | tf_op jit(solution)/shard_map/input_grad/pallas_call | solution.py:1446
  567.9 2.7 fusion.1
  570.6 0.8 slice_bitcast_fusion.40
  572.1 1.9 fusion
  574.2 3.7 fusion.15
  577.9 1.0 slice_dynamic-update-slice_fusion.9
  578.9 1.0 slice_dynamic-update-slice_fusion.8
  579.9 1.0 slice_dynamic-update-slice_fusion.7
  580.9 1.0 slice_dynamic-update-slice_fusion.6
  581.9 1.0 slice_dynamic-update-slice_fusion.5
  582.9 1.0 slice_dynamic-update-slice_fusion.4
  583.9 1.1 slice_dynamic-update-slice_fusion.3
  585.0 1.0 slice_dynamic-update-slice_fusion.2
  586.1 1.0 slice_dynamic-update-slice_fusion.1
  587.1 1.0 slice_dynamic-update-slice_fusion
  588.6 1.1 copy-done.37
  590.7 1.6 collective-permute-start.2
  592.3 3.2 collective-permute-done.2
  595.5 1.2 collective-permute-start.3
  596.8 3.2 collective-permute-done.3
  600.7 1.2 collective-permute-start.4
  601.9 2.6 collective-permute-start.5
  604.5 0.8 copy-done.38
  605.3 2.3 slice.468
  607.6 1.4 slice.469
  609.0 1.5 copy.94
  610.5 1.3 copy.93
  612.5 1.0 add_add_fusion
  (195 shorter events, 22.2 us)
Async XLA Ops:
  0.7 27.4 %copy-start = (bf16[1,512,1024]{2,1,0:T(8,128)(2,1)S(1)}, bf16[1,512,1024]{2,1,0:T(8,128)(2,1)}, u32[]{:S(2)}) copy-start(bf16[1,512,1024]{2,1,0:T(8,128)(2,1)} %param.22) | copy-start | bytes 3145732
  0.7 7.7 %copy-start.22 = (f32[128,1024]{1,0:T(8,128)S(1)}, f32[128,1024]{1,0:T(8,128)}, u32[]{:S(2)}) copy-start(f32[128,1024]{1,0:T(8,128)} %param.24) | copy-start | bytes 1572868
  1.6 51.9 %collective-permute-start = (bf16[16,1024]{1,0:T(8,128)(2,1)S(1)}, bf16[16,1024]{1,0:T(8,128)(2,1)S(1)}, u32[]{:S(2)}, u32[]{:S(2)}) collective-permute-start(bf16[16,1024]{1,0:T(8,128)(2,1)S(1)} %slice_bitcast_fusion.33), channel_id=1, source_target_pairs={{0,1},{1,2},{2,3},{4,5},{5,6},{6,7},{8,9},{9,10},{10,11},{12,13},{... | collective-permute-start | bytes 98312 | tf_op jit(solution)/shard_map/ppermute | solution.py:1465
  5.0 3.5 copy-start.23
  6.1 47.4 %copy-start.28 = (s32[1024]{0:T(1024)}, s32[1024]{0:T(1024)S(1)}, u32[]{:S(2)}) copy-start(s32[1024]{0:T(1024)S(1)} %fusion.36) | copy-start | bytes 12292
  8.7 5.8 copy-start.36
  8.7 6.0 copy-start.18
  13.9 2.8 copy-start.2
  16.7 4.6 copy-start.3
  21.3 4.6 slice-start
  28.1 3.0 copy-start.19
  30.4 2.4 copy-start.6
  31.0 2.7 copy-start.7
  40.2 3.5 copy-start.42
  40.2 3.5 copy-start.43
  43.7 12.3 %copy-start.26 = (f32[1024]{0:T(1024)}, f32[1024]{0:T(1024)S(1)}, u32[]{:S(2)}) copy-start(f32[1024]{0:T(1024)S(1)} %get-tuple-element.225) | copy-start | bytes 12292
  50.8 2.7 copy-start.41
  535.1 3.2 copy-start.5
  539.9 3.5 copy-start.4
  543.3 2.5 copy-start.27
  543.3 2.7 copy-start.24
  544.5 44.0 %copy-start.10 = (f32[128,1,512]{2,0,1:T(8,128)}, f32[128,1,512]{2,0,1:T(8,128)S(1)}, u32[]{:S(2)}) copy-start(f32[128,1,512]{2,0,1:T(8,128)S(1)} %get-tuple-element.176) | copy-start | bytes 786436
  546.7 21.2 %copy-start.29 = (s32[1024]{0:T(1024)S(1)}, s32[1024]{0:T(1024)}, u32[]{:S(2)}) copy-start(s32[1024]{0:T(1024)} %copy-done.28) | copy-start | bytes 12292
  546.7 25.4 %copy-start.44 = (f32[8,1024]{1,0:T(8,128)S(1)}, f32[8,1024]{1,0:T(8,128)}, u32[]{:S(2)}) copy-start(f32[8,1024]{1,0:T(8,128)} %get-tuple-element.84) | copy-start | bytes 98308
  574.1 3.8 copy-start.8
  574.1 16.6 %collective-permute-start.1 = (f32[152,128]{1,0:T(8,128)S(1)}, f32[152,128]{1,0:T(8,128)S(1)}, u32[]{:S(2)}, u32[]{:S(2)}) collective-permute-start(f32[152,128]{1,0:T(8,128)S(1)} %pad_bitcast_fusion), channel_id=1, source_target_pairs={{0,4},{1,5},{2,6},{3,7},{4,0},{5,1},{6,2},{7,3},{8,12},{9,13},{10,... | collective-permute-start | bytes 233480 | tf_op jit(solution)/shard_map/ppermute | solution.py:1475
  574.2 3.7 copy-start.32
  574.2 3.7 copy-start.34
  583.9 4.5 copy-start.17
  583.9 4.5 copy-start.30
  585.0 3.4 copy-start.16
  585.0 3.4 copy-start.15
  586.0 2.4 copy-start.14
  586.1 2.4 copy-start.13
  587.1 1.4 copy-start.12
  588.2 2.0 copy-start.33
  588.2 2.0 copy-start.35
  588.2 1.5 copy-start.37
  588.2 2.0 copy-start.39
  588.2 2.2 copy-start.20
  588.2 2.4 copy-start.21
  588.5 2.2 copy-start.9
  588.5 1.7 copy-start.31
  590.6 13.9 %copy-start.11 = (f32[128,1,512]{2,0,1:T(8,128)S(1)}, f32[128,1,512]{2,0,1:T(8,128)}, u32[]{:S(2)}) copy-start(f32[128,1,512]{2,0,1:T(8,128)} %copy-done.10) | copy-start | bytes 786436
  590.7 4.8 collective-permute-start.2
  595.5 4.5 collective-permute-start.3
  600.7 11.8 %collective-permute-start.4 = (f32[152,128]{1,0:T(8,128)}, f32[152,128]{1,0:T(8,128)}, u32[]{:S(2)}, u32[]{:S(2)}) collective-permute-start(f32[152,128]{1,0:T(8,128)} %add.143), channel_id=1, source_target_pairs={{0,8},{1,9},{2,10},{3,11},{4,12},{5,13},{6,14},{7,15},{8,16},{9,17... | collective-permute-start | bytes 233480 | tf_op jit(solution)/shard_map/ppermute | solution.py:1475
  601.9 10.6 %collective-permute-start.5 = (f32[152,128]{1,0:T(8,128)}, f32[152,128]{1,0:T(8,128)}, u32[]{:S(2)}, u32[]{:S(2)}) collective-permute-start(f32[152,128]{1,0:T(8,128)} %add.143), channel_id=1, source_target_pairs={{0,16},{1,17},{2,18},{3,19},{4,20},{5,21},{6,22},{7,23},{8,24},{9,... | collective-permute-start | bytes 233480 | tf_op jit(solution)/shard_map/ppermute | solution.py:1475
  604.4 8.1 %collective-permute-start.6 = (f32[152,128]{1,0:T(8,128)}, f32[152,128]{1,0:T(8,128)}, u32[]{:S(2)}, u32[]{:S(2)}) collective-permute-start(f32[152,128]{1,0:T(8,128)} %add.143), channel_id=1, source_target_pairs={{0,24},{1,25},{2,26},{3,27},{4,28},{5,29},{6,30},{7,31},{8,0},{9,1... | collective-permute-start | bytes 233480 | tf_op jit(solution)/shard_map/ppermute | solution.py:1475
  604.5 0.8 copy-start.38
  605.3 2.3 copy-start.40
  609.0 7.7 %copy-start.1 = (bf16[1,512,1024]{2,1,0:T(8,128)(2,1)S(1)}, bf16[1,512,1024]{2,1,0:T(8,128)(2,1)}, u32[]{:S(2)}) copy-start(bf16[1,512,1024]{2,1,0:T(8,128)(2,1)} %param.22) | copy-start | bytes 3145732
  610.5 1.3 copy-start.25
